TPU v7x, 32 devices: a whole 2x2x4 slice. The times are simulated.
32 devices in a mesh: grp: 4 (over y, core), ctx: 8 (over z, x).
Axes of the slice: x: 2, y: 2, z: 4, core: 2. Of those that a mesh axis runs over, the one named last changes fastest.
Arguments:
- tokens: bfloat16 [18432, 1024], P(('grp', 'ctx')), may hold values from -6 to 6
- block_table: int32 [288], replicated, may hold values from 0 to 287, as said below
- norm1_gain: float32 [1024], replicated, may hold values from 0.25 to 1.75
- w_query: bfloat16 [1024, 2048], P('ctx'), may hold values from -0.1875 to 0.1875
- key_weight: bfloat16 [1024, 1024], P('ctx'), may hold values from -0.1875 to 0.1875
- value_weight: bfloat16 [1024, 1024], P('ctx'), may hold values from -0.1875 to 0.1875
- query_gain: float32 [128], replicated, may hold values from 0.25 to 1.75
- key_norm_gain: float32 [128], replicated, may hold values from 0.25 to 1.75
- w_out: bfloat16 [2048, 1024], P('ctx'), may hold values from -4 to 4
- norm2_gain: float32 [1024], replicated, may hold values from 0.25 to 1.75
- w_gate: bfloat16 [1024, 3072], P('ctx'), may hold values from -0.1875 to 0.1875
- w_up: bfloat16 [1024, 3072], P('ctx'), may hold values from -0.1875 to 0.1875
- w_down: bfloat16 [3072, 1024], P('ctx'), may hold values from -0.109375 to 0.109375
- out_grad: bfloat16 [18432, 1024], P(('grp', 'ctx')), may hold values from -6 to 6
Outputs:
- layer_out: bfloat16 [18432, 1024], P(('grp', 'ctx'))
- token_grad: float32 [18432, 1024], P(('grp', 'ctx'))
- norm1_gain_grad: float32 [1024], replicated
- w_query_grad: float32 [1024, 2048], P('ctx')
- w_key_grad: float32 [1024, 1024], P('ctx')
- w_value_grad: float32 [1024, 1024], P('ctx')
- query_gain_grad: float32 [128], replicated
- key_gain_grad: float32 [128], replicated
- w_out_grad: float32 [2048, 1024], P('ctx')
- norm2_gain_grad: float32 [1024], replicated
- w_gate_grad: float32 [1024, 3072], P('ctx')
- w_up_grad: float32 [1024, 3072], P('ctx')
- w_down_grad: float32 [3072, 1024], P('ctx')
Inputs may be any that keep to these rules, and one draw needn't show every extreme that they name: `block_table`: entry s is the natural block of 16 tokens that storage slot s of every group holds; a group's storage rows run slot after slot, and each device of ctx holds 36 consecutive slots. Every block appears once, and the k-th slots of all devices together hold the k-th run of consecutive natural blocks, one block each.
All inputs are finite; a program needn't handle non-finite values.
Results may differ from a plain program's by a relative error of at most 0.023.
Values may be sent and summed in bfloat16 or wider, within the bound.
No kernel may reach another device: no remote copies, remote signals or barrier semaphores. Data moves between devices by JAX's collectives and lax.ppermute only.
A program may use at most 320 MiB of HBM per device.

v0:
```python
import math

import jax
import jax.numpy as jnp
from jax import lax
from jax.sharding import PartitionSpec as P

QUERY_HEADS = 16
KEY_VALUE_HEADS = 8
HEAD_SIZE = 128
PROMPT = 1024
CONT_LEN = 448
BLK = 16


eps = 1e-06
theta = 1000000.0
key_span = 512
masked_score = -1e30


def normed_parts(value_rows):
    inverse = lax.rsqrt(jnp.mean(value_rows * value_rows, axis=-1, keepdims=True) + eps)
    return (value_rows * inverse, inverse)


def norm_back(grad_normed, normed, inverse):
    return inverse * (grad_normed - normed * jnp.mean(grad_normed * normed, axis=-1, keepdims=True))


def layout(block_table, slot_ids):
    natural = block_table[slot_ids // BLK] * BLK + slot_ids % BLK
    beyond = natural - PROMPT
    segment = jnp.where(natural < PROMPT, 0, 1 + beyond // CONT_LEN)
    places = jnp.where(natural < PROMPT, natural, PROMPT + beyond % CONT_LEN)
    return (natural, segment, places)


def rotation(places):
    half_dim = HEAD_SIZE // 2
    frequency = jnp.exp(
        jnp.arange(half_dim, dtype=jnp.float32) * (-2.0 * math.log(theta) / HEAD_SIZE)
    )
    angles = places.astype(jnp.float32)[:, None] * frequency[None, :]
    return (jnp.cos(angles)[:, None, :], jnp.sin(angles)[:, None, :])


def apply_rotation(value_rows, cosine_table, sine_table):
    half_dim = value_rows.shape[-1] // 2
    first_half = value_rows[..., :half_dim]
    second_half = value_rows[..., half_dim:]
    return jnp.concatenate(
        [
            first_half * cosine_table - second_half * sine_table,
            second_half * cosine_table + first_half * sine_table,
        ],
        axis=-1,
    )


def rotate_back(value_rows, cosine_table, sine_table):
    half_dim = value_rows.shape[-1] // 2
    first_half = value_rows[..., :half_dim]
    second_half = value_rows[..., half_dim:]
    return jnp.concatenate(
        [
            first_half * cosine_table + second_half * sine_table,
            second_half * cosine_table - first_half * sine_table,
        ],
        axis=-1,
    )


def allowed_mask(own_nat, own_seg, key_nat, key_seg):
    return (key_nat[None, :] <= own_nat[:, None]) & (
        (key_seg[None, :] == 0) | (key_seg[None, :] == own_seg[:, None])
    )


def span_of():
    return key_span


def over_blocks(advance, running, length):
    block_span_width = span_of()

    def scan_step(inner_state, key_first):
        return (advance(inner_state, key_first, block_span_width), None)

    running, ignored = lax.scan(
        scan_step,
        running,
        jnp.arange(length // block_span_width, dtype=jnp.int32) * block_span_width,
    )
    return running


def attend_block(running, query_head_rows, keys_part, values_part, allowed, softmax_scale):
    row_max, row_sum, accum = running
    raw_scores = (
        jnp.einsum("grtd,ngd->grtn", query_head_rows, keys_part, preferred_element_type=jnp.float32)
        * softmax_scale
    )
    scores = jnp.where(allowed, raw_scores, masked_score)
    new_max = jnp.maximum(row_max, jnp.max(scores, axis=-1))
    rescale = jnp.exp(row_max - new_max)
    weights = jnp.exp(scores - new_max[..., None])
    row_sum = row_sum * rescale + jnp.sum(weights, axis=-1)
    accum = accum * rescale[..., None] + jnp.einsum(
        "grtn,ngd->grtd",
        weights.astype(jnp.bfloat16),
        values_part,
        preferred_element_type=jnp.float32,
    )
    return (new_max, row_sum, accum)


def key_terms(
    grad_scores, weights, query_head_rows, scaled_high, scaled_rest, softmax_scale, block_span_width
):
    grad_keys = (
        jnp.einsum(
            "grtn,grtd->ngd", grad_scores, query_head_rows, preferred_element_type=jnp.float32
        )
        * softmax_scale
    )
    weights_low = weights.astype(jnp.bfloat16)
    grad_values = jnp.einsum(
        "grtn,grtd->ngd", weights_low, scaled_high, preferred_element_type=jnp.float32
    )
    grad_values = grad_values + jnp.einsum(
        "grtn,grtd->ngd", weights_low, scaled_rest, preferred_element_type=jnp.float32
    )
    return jnp.stack(
        [grad_keys.reshape(block_span_width, -1), grad_values.reshape(block_span_width, -1)], axis=1
    )


def shards(
    tokens,
    block_table,
    norm1_gain,
    w_query,
    key_weight,
    value_weight,
    query_gain,
    key_norm_gain,
    w_out,
    norm2_gain,
    w_gate,
    w_up,
    w_down,
    out_grad,
):
    row_total = tokens.shape[0]
    group_length = block_table.shape[0] * BLK
    sharing_count = QUERY_HEADS // KEY_VALUE_HEADS
    softmax_scale = 1.0 / math.sqrt(HEAD_SIZE)
    position = lax.axis_index("ctx")
    all_nat, all_seg, all_places = layout(block_table, jnp.arange(group_length, dtype=jnp.int32))
    own_slots = position * row_total + jnp.arange(row_total, dtype=jnp.int32)
    own_nat, own_seg, own_places = layout(block_table, own_slots)
    cosine_table, sine_table = rotation(own_places)
    query_full, key_full, value_full, out_full = (
        lax.all_gather(w_query, "ctx", axis=0, tiled=True),
        lax.all_gather(key_weight, "ctx", axis=0, tiled=True),
        lax.all_gather(value_weight, "ctx", axis=0, tiled=True),
        lax.all_gather(w_out, "ctx", axis=0, tiled=True),
    )
    inputs = tokens.astype(jnp.float32)
    normed_one, inverse_one = normed_parts(inputs)
    first_hidden = (normed_one * norm1_gain).astype(jnp.bfloat16)
    query_raw = jnp.dot(first_hidden, query_full, preferred_element_type=jnp.float32).reshape(
        row_total, QUERY_HEADS, HEAD_SIZE
    )
    unnormalized_keys = jnp.dot(first_hidden, key_full, preferred_element_type=jnp.float32).reshape(
        row_total, KEY_VALUE_HEADS, HEAD_SIZE
    )
    reduced_value = jnp.dot(first_hidden, value_full, preferred_element_type=jnp.float32).astype(
        jnp.bfloat16
    )
    query_normed, query_inverse = normed_parts(query_raw)
    normalized_keys, key_inverse = normed_parts(unnormalized_keys)
    reduced_query = apply_rotation(query_normed * query_gain, cosine_table, sine_table).astype(
        jnp.bfloat16
    )
    key_low = (
        apply_rotation(normalized_keys * key_norm_gain, cosine_table, sine_table)
        .astype(jnp.bfloat16)
        .reshape(row_total, KEY_VALUE_HEADS * HEAD_SIZE)
    )
    query_head_rows = jnp.transpose(
        reduced_query.reshape(row_total, KEY_VALUE_HEADS, sharing_count, HEAD_SIZE), (1, 2, 0, 3)
    )

    def attend(running, pieces):
        piece_keys, piece_values = pieces

        def advance(inner_state, key_first, block_span_width):
            keys_part = lax.dynamic_slice_in_dim(
                piece_keys, key_first, block_span_width, 0
            ).reshape(block_span_width, KEY_VALUE_HEADS, HEAD_SIZE)
            values_part = lax.dynamic_slice_in_dim(
                piece_values, key_first, block_span_width, 0
            ).reshape(block_span_width, KEY_VALUE_HEADS, HEAD_SIZE)
            key_nat = lax.dynamic_slice_in_dim(all_nat, key_first, block_span_width)
            key_seg = lax.dynamic_slice_in_dim(all_seg, key_first, block_span_width)
            allowed = allowed_mask(own_nat, own_seg, key_nat, key_seg)
            return attend_block(
                inner_state, query_head_rows, keys_part, values_part, allowed, softmax_scale
            )

        return over_blocks(advance, running, piece_keys.shape[0])

    statistic_shape = (KEY_VALUE_HEADS, sharing_count, row_total)
    initial = (
        jnp.full(statistic_shape, masked_score, jnp.float32),
        jnp.zeros(statistic_shape, jnp.float32),
        jnp.zeros(statistic_shape + (HEAD_SIZE,), jnp.float32),
    )
    row_max, row_sum, accum = attend(
        initial,
        (
            lax.all_gather(key_low, "ctx", axis=0, tiled=True),
            lax.all_gather(reduced_value, "ctx", axis=0, tiled=True),
        ),
    )
    mixed_heads = accum / row_sum[..., None]
    flat_low = (
        jnp.transpose(mixed_heads, (2, 0, 1, 3))
        .reshape(row_total, QUERY_HEADS * HEAD_SIZE)
        .astype(jnp.bfloat16)
    )
    resid_one = inputs + jnp.dot(flat_low, out_full, preferred_element_type=jnp.float32)
    gate_full, up_full, down_full = (
        lax.all_gather(w_gate, "ctx", axis=0, tiled=True),
        lax.all_gather(w_up, "ctx", axis=0, tiled=True),
        lax.all_gather(w_down, "ctx", axis=0, tiled=True),
    )
    normed_two, inverse_two = normed_parts(resid_one)
    hidden_two = (normed_two * norm2_gain).astype(jnp.bfloat16)
    gate_proj = jnp.dot(hidden_two, gate_full, preferred_element_type=jnp.float32)
    up_proj = jnp.dot(hidden_two, up_full, preferred_element_type=jnp.float32)
    gate_sigmoid = jax.nn.sigmoid(gate_proj)
    gate_silu = gate_proj * gate_sigmoid
    hidden_low = (gate_silu * up_proj).astype(jnp.bfloat16)
    outcome = resid_one + jnp.dot(hidden_low, down_full, preferred_element_type=jnp.float32)
    gate_full, up_full, down_full = (
        lax.all_gather(w_gate, "ctx", axis=0, tiled=True),
        lax.all_gather(w_up, "ctx", axis=0, tiled=True),
        lax.all_gather(w_down, "ctx", axis=0, tiled=True),
    )
    grad_out = out_grad.astype(jnp.float32)
    grad_down = jnp.einsum("tf,td->fd", hidden_low, out_grad, preferred_element_type=jnp.float32)
    grad_hidden = jnp.einsum("td,fd->tf", out_grad, down_full, preferred_element_type=jnp.float32)
    grad_gate = (
        grad_hidden * up_proj * gate_sigmoid * (1.0 + gate_proj * (1.0 - gate_sigmoid))
    ).astype(jnp.bfloat16)
    grad_up = (grad_hidden * gate_silu).astype(jnp.bfloat16)
    grad_wgate = jnp.einsum("tk,tf->kf", hidden_two, grad_gate, preferred_element_type=jnp.float32)
    grad_wup = jnp.einsum("tk,tf->kf", hidden_two, grad_up, preferred_element_type=jnp.float32)
    grad_two = jnp.einsum(
        "tf,kf->tk", grad_gate, gate_full, preferred_element_type=jnp.float32
    ) + jnp.einsum("tf,kf->tk", grad_up, up_full, preferred_element_type=jnp.float32)
    gain_two_part = jnp.sum(grad_two * normed_two, axis=0)
    grad_resid = grad_out + norm_back(grad_two * norm2_gain, normed_two, inverse_two)
    grad_attn = grad_resid.astype(jnp.bfloat16)
    query_full, key_full, value_full, out_full = (
        lax.all_gather(w_query, "ctx", axis=0, tiled=True),
        lax.all_gather(key_weight, "ctx", axis=0, tiled=True),
        lax.all_gather(value_weight, "ctx", axis=0, tiled=True),
        lax.all_gather(w_out, "ctx", axis=0, tiled=True),
    )
    keys_all, values_all = (
        lax.all_gather(key_low, "ctx", axis=0, tiled=True),
        lax.all_gather(reduced_value, "ctx", axis=0, tiled=True),
    )
    grad_wout = jnp.einsum("tk,td->kd", flat_low, grad_attn, preferred_element_type=jnp.float32)
    flattened_grad = jnp.einsum(
        "td,kd->tk", grad_attn, out_full, preferred_element_type=jnp.float32
    ).astype(jnp.bfloat16)
    head_grads = jnp.transpose(
        flattened_grad.reshape(row_total, KEY_VALUE_HEADS, sharing_count, HEAD_SIZE), (1, 2, 0, 3)
    )
    grad_heads_wide = head_grads.astype(jnp.float32)
    row_delta = jnp.sum(grad_heads_wide * mixed_heads, axis=-1)
    scaled_grad = grad_heads_wide / row_sum[..., None]
    scaled_high = scaled_grad.astype(jnp.bfloat16)
    scaled_rest = (scaled_grad - scaled_high.astype(jnp.float32)).astype(jnp.bfloat16)

    def block_back(key_first, block_span_width):
        keys_part = lax.dynamic_slice_in_dim(keys_all, key_first, block_span_width, 0).reshape(
            block_span_width, KEY_VALUE_HEADS, HEAD_SIZE
        )
        values_part = lax.dynamic_slice_in_dim(values_all, key_first, block_span_width, 0).reshape(
            block_span_width, KEY_VALUE_HEADS, HEAD_SIZE
        )
        key_nat = lax.dynamic_slice_in_dim(all_nat, key_first, block_span_width)
        key_seg = lax.dynamic_slice_in_dim(all_seg, key_first, block_span_width)
        allowed = allowed_mask(own_nat, own_seg, key_nat, key_seg)
        raw_scores = (
            jnp.einsum(
                "grtd,ngd->grtn", query_head_rows, keys_part, preferred_element_type=jnp.float32
            )
            * softmax_scale
        )
        scores = jnp.where(allowed, raw_scores, masked_score)
        weights = jnp.exp(scores - row_max[..., None])
        grad_prob = jnp.einsum(
            "grtd,ngd->grtn", head_grads, values_part, preferred_element_type=jnp.float32
        )
        grad_scores = (weights * (grad_prob - row_delta[..., None]) / row_sum[..., None]).astype(
            jnp.bfloat16
        )
        return (keys_part, grad_scores, weights)

    empty_query = jnp.zeros((KEY_VALUE_HEADS, sharing_count, row_total, HEAD_SIZE), jnp.float32)
    span_back = span_of()

    def pass_step(grad_query, key_first):
        keys_part, grad_scores, weights = block_back(key_first, span_back)
        grad_query = grad_query + jnp.einsum(
            "grtn,ngd->grtd", grad_scores, keys_part, preferred_element_type=jnp.float32
        )
        return (
            grad_query,
            key_terms(
                grad_scores,
                weights,
                query_head_rows,
                scaled_high,
                scaled_rest,
                softmax_scale,
                span_back,
            ),
        )

    grad_query, key_gradient_parts = lax.scan(
        pass_step, empty_query, jnp.arange(group_length // span_back, dtype=jnp.int32) * span_back
    )
    self_terms = lax.psum_scatter(
        key_gradient_parts.reshape(group_length, 2, KEY_VALUE_HEADS * HEAD_SIZE).astype(
            jnp.bfloat16
        ),
        "ctx",
        scatter_dimension=0,
        tiled=True,
    ).astype(jnp.float32)
    grad_query_rows = jnp.transpose(grad_query * softmax_scale, (2, 0, 1, 3)).reshape(
        row_total, QUERY_HEADS, HEAD_SIZE
    )
    grad_query_normed = rotate_back(grad_query_rows, cosine_table, sine_table)
    gain_query_part = jnp.sum(grad_query_normed * query_normed, axis=(0, 1))
    grad_query_raw = (
        norm_back(grad_query_normed * query_gain, query_normed, query_inverse)
        .reshape(row_total, QUERY_HEADS * HEAD_SIZE)
        .astype(jnp.bfloat16)
    )
    key_row_grads = self_terms[:, 0, :].reshape(row_total, KEY_VALUE_HEADS, HEAD_SIZE)
    grad_key_normed = rotate_back(key_row_grads, cosine_table, sine_table)
    gain_key_part = jnp.sum(grad_key_normed * normalized_keys, axis=(0, 1))
    grad_key_raw = (
        norm_back(grad_key_normed * key_norm_gain, normalized_keys, key_inverse)
        .reshape(row_total, KEY_VALUE_HEADS * HEAD_SIZE)
        .astype(jnp.bfloat16)
    )
    grad_value_low = self_terms[:, 1, :].astype(jnp.bfloat16)
    grad_wquery = jnp.einsum(
        "tk,tq->kq", first_hidden, grad_query_raw, preferred_element_type=jnp.float32
    )
    grad_wkey = jnp.einsum(
        "tk,tq->kq", first_hidden, grad_key_raw, preferred_element_type=jnp.float32
    )
    grad_wvalue = jnp.einsum(
        "tk,tq->kq", first_hidden, grad_value_low, preferred_element_type=jnp.float32
    )
    grad_one = jnp.einsum(
        "tq,kq->tk", grad_query_raw, query_full, preferred_element_type=jnp.float32
    )
    grad_one = grad_one + jnp.einsum(
        "tq,kq->tk", grad_key_raw, key_full, preferred_element_type=jnp.float32
    )
    grad_one = grad_one + jnp.einsum(
        "tq,kq->tk", grad_value_low, value_full, preferred_element_type=jnp.float32
    )
    gain_one_part = jnp.sum(grad_one * normed_one, axis=0)
    grad_tokens = grad_resid + norm_back(grad_one * norm1_gain, normed_one, inverse_one)
    shard_grads = (
        lax.psum_scatter(
            grad_wquery.astype(jnp.bfloat16), "ctx", scatter_dimension=0, tiled=True
        ).astype(jnp.float32),
        lax.psum_scatter(
            grad_wkey.astype(jnp.bfloat16), "ctx", scatter_dimension=0, tiled=True
        ).astype(jnp.float32),
        lax.psum_scatter(
            grad_wvalue.astype(jnp.bfloat16), "ctx", scatter_dimension=0, tiled=True
        ).astype(jnp.float32),
        lax.psum_scatter(
            grad_wout.astype(jnp.bfloat16), "ctx", scatter_dimension=0, tiled=True
        ).astype(jnp.float32),
        lax.psum_scatter(
            grad_wgate.astype(jnp.bfloat16), "ctx", scatter_dimension=0, tiled=True
        ).astype(jnp.float32),
        lax.psum_scatter(
            grad_wup.astype(jnp.bfloat16), "ctx", scatter_dimension=0, tiled=True
        ).astype(jnp.float32),
        lax.psum_scatter(
            grad_down.astype(jnp.bfloat16), "ctx", scatter_dimension=0, tiled=True
        ).astype(jnp.float32),
    )
    shard_grads = (
        lax.psum(shard_grads[0].astype(jnp.bfloat16), "grp").astype(jnp.float32),
        lax.psum(shard_grads[1].astype(jnp.bfloat16), "grp").astype(jnp.float32),
        lax.psum(shard_grads[2].astype(jnp.bfloat16), "grp").astype(jnp.float32),
        lax.psum(shard_grads[3].astype(jnp.bfloat16), "grp").astype(jnp.float32),
        lax.psum(shard_grads[4].astype(jnp.bfloat16), "grp").astype(jnp.float32),
        lax.psum(shard_grads[5].astype(jnp.bfloat16), "grp").astype(jnp.float32),
        lax.psum(shard_grads[6].astype(jnp.bfloat16), "grp").astype(jnp.float32),
    )
    gain_grads = lax.psum(
        (gain_one_part, gain_query_part, gain_key_part, gain_two_part), ("grp", "ctx")
    )
    return (
        outcome.astype(jnp.bfloat16),
        grad_tokens,
        gain_grads[0],
        shard_grads[0],
        shard_grads[1],
        shard_grads[2],
        gain_grads[1],
        gain_grads[2],
        shard_grads[3],
        gain_grads[3],
        shard_grads[4],
        shard_grads[5],
        shard_grads[6],
    )


def solution(mesh):
    return jax.shard_map(
        shards,
        mesh=mesh,
        in_specs=(
            P(("grp", "ctx"), None),
            P(),
            P(),
            P("ctx", None),
            P("ctx", None),
            P("ctx", None),
            P(),
            P(),
            P("ctx", None),
            P(),
            P("ctx", None),
            P("ctx", None),
            P("ctx", None),
            P(("grp", "ctx"), None),
        ),
        out_specs=(
            P(("grp", "ctx"), None),
            P(("grp", "ctx"), None),
            P(),
            P("ctx", None),
            P("ctx", None),
            P("ctx", None),
            P(),
            P(),
            P("ctx", None),
            P(),
            P("ctx", None),
            P("ctx", None),
            P("ctx", None),
        ),
        check_vma=False,
    )
```

profile of v0, /device:TPU:0, one launch (start us, length us, event | category | flops | bytes accessed | tf_op | source)
XLA Modules:
  0.0 2652.9 jit_solution(930703691607897160)
XLA Ops:
  11.1 51.1 %all-gather.16.cloned.1.call-done = bf16[1024,1024]{1,0:T(8,128)(2,1)} async-done(((bf16[128,1024]{1,0:T(8,128)(2,1)}), bf16[1024,1024]{1,0:T(8,128)(2,1)}) %all-gather.16.cloned.1.call-update) | async-done | bytes 2097168 | tf_op jit(solution)/shard_map/all_gather | solution.py:167
  71.9 40.2 %all-gather.10.cloned.1.call-done = bf16[1024,1024]{1,0:T(8,128)(2,1)} async-done(((bf16[128,1024]{1,0:T(8,128)(2,1)}), bf16[1024,1024]{1,0:T(8,128)(2,1)}) %all-gather.10.cloned.1.call-update) | async-done | bytes 2097168 | tf_op jit(solution)/shard_map/all_gather | solution.py:166
  124.4 27.3 %gather_fusion = s32[4608]{0:T(1024)S(1)} fusion(s32[288]{0:T(512)S(1)} %copy-done, s32[5120]{0:T(1024)S(1)} %pad_clamp_fusion), kind=kCustom, calls=%fused_computation | custom fusion | bytes 55296 | tf_op jit(solution)/shard_map/gather | solution.py:32
  151.8 34.4 %all-gather.14.cloned.1.call-done = bf16[1024,2048]{1,0:T(8,128)(2,1)} async-done(((bf16[128,2048]{1,0:T(8,128)(2,1)}), bf16[1024,2048]{1,0:T(8,128)(2,1)}) %all-gather.14.cloned.1.call-update) | async-done | bytes 4194320 | tf_op jit(solution)/shard_map/all_gather | solution.py:165
  203.4 121.8 %all-gather.18.cloned.1.call-done = bf16[4608,1024]{1,0:T(8,128)(2,1)} async-done(((bf16[576,1024]{1,0:T(8,128)(2,1)}), bf16[4608,1024]{1,0:T(8,128)(2,1)}) %all-gather.18.cloned.1.call-update) | async-done | bytes 9437200 | tf_op jit(solution)/shard_map/all_gather | solution.py:225
  325.1 12.7 copy.71
  337.9 126.2 %all-gather.12.cloned.1.call-done = bf16[4608,1024]{1,0:T(8,128)(2,1)} async-done(((bf16[576,1024]{1,0:T(8,128)(2,1)}), bf16[4608,1024]{1,0:T(8,128)(2,1)}) %all-gather.12.cloned.1.call-update) | async-done | bytes 9437200 | tf_op jit(solution)/shard_map/all_gather | solution.py:224
  464.0 12.4 copy.70
  476.5 243.6 %while.28 = (s32[]{:T(128)}, f32[8,2,576]{2,1,0:T(2,128)S(1)}, f32[8,2,576]{2,1,0:T(2,128)S(1)}, f32[8,2,576,128]{3,2,1,0:T(8,128)}, s32[9]{0:T(128)S(1)}, /*ind...) while((s32[]{:T(128)}, f32[8,2,576]{2,1,0:T(2,128)S(1)}, ...), condition=%wide.region_6.7_spmd.clone, body=%wide.region_3.6_spmd.clone.sunk | while | flops 2472588800 | bytes 118441768 | solution.py:90
  755.9 80.1 %all-gather.26.cloned.1.call-done = bf16[3072,1024]{1,0:T(8,128)(2,1)} async-done(((bf16[384,1024]{1,0:T(8,128)(2,1)}), bf16[3072,1024]{1,0:T(8,128)(2,1)}) %all-gather.26.cloned.1.call-update) | async-done | bytes 6291472 | tf_op jit(solution)/shard_map/all_gather | solution.py:238
  836.0 13.7 multiply_convert_fusion
  887.8 666.1 %while.29 = (s32[]{:T(128)}, f32[8,2,576,128]{3,2,1,0:T(8,128)}, bf16[9,512,2,1024]{3,1,0,2:T(8,128)(2,1)}, s32[9]{0:T(128)S(1)}, s32[4608]{0:T(1024)}, /*index=...) while((s32[]{:T(128)}, f32[8,2,576,128]{3,2,1,0:T(8,128)}, ...), condition=%wide.region_11.12_spmd.clone, body=%wide.region_10.11_spmd.clone.sunk | while | flops 7325221376 | bytes 180950864 | solution.py:338
  923.3 15.0 fusion.180
  996.1 15.0 fusion.180
  1070.2 15.0 fusion.180
  1144.4 15.0 fusion.180
  1218.5 15.0 fusion.180
  1292.6 15.0 fusion.180
  1366.7 15.0 fusion.180
  1440.8 15.0 fusion.180
  1514.7 15.0 fusion.180
  1569.9 13.1 multiply_add_fusion
  1635.1 230.6 %reduce-scatter.9.cloned.1.call-done = bf16[576,2,1024]{2,0,1:T(8,128)(2,1)} async-done(((bf16[4608,2,1024]{2,0,1:T(8,128)(2,1)}), bf16[576,2,1024]{2,0,1:T(8,128)(2,1)}) %reduce-scatter.9.cloned.1.call-update) | async-done | bytes 2359312 | tf_op jit(solution)/shard_map/reduce_scatter | solution.py:341
  1894.3 62.1 %reduce-scatter.17.cloned.1.call-done = bf16[256,1024]{1,0:T(8,128)(2,1)} async-done(((bf16[2048,1024]{1,0:T(8,128)(2,1)}), bf16[256,1024]{1,0:T(8,128)(2,1)}) %reduce-scatter.17.cloned.1.call-update) | async-done | bytes 524304 | tf_op jit(solution)/shard_map/reduce_scatter | solution.py:398
  1956.4 91.6 %reduce-scatter.11.cloned.1.call-done = bf16[128,2048]{1,0:T(8,128)(2,1)} async-done(((bf16[1024,2048]{1,0:T(8,128)(2,1)}), bf16[128,2048]{1,0:T(8,128)(2,1)}) %reduce-scatter.11.cloned.1.call-update) | async-done | bytes 524304 | tf_op jit(solution)/shard_map/reduce_scatter | solution.py:389
  2047.9 121.4 %reduce-scatter.23.cloned.1.call-done = bf16[384,1024]{1,0:T(8,128)(2,1)} async-done(((bf16[3072,1024]{1,0:T(8,128)(2,1)}), bf16[384,1024]{1,0:T(8,128)(2,1)}) %reduce-scatter.23.cloned.1.call-update) | async-done | bytes 786448 | tf_op jit(solution)/shard_map/reduce_scatter | solution.py:407
  2169.3 120.6 %reduce-scatter.21.cloned.1.call-done = bf16[128,3072]{1,0:T(8,128)(2,1)} async-done(((bf16[1024,3072]{1,0:T(8,128)(2,1)}), bf16[128,3072]{1,0:T(8,128)(2,1)}) %reduce-scatter.21.cloned.1.call-update) | async-done | bytes 786448 | tf_op jit(solution)/shard_map/reduce_scatter | solution.py:404
  2289.9 120.6 %reduce-scatter.19.cloned.1.call-done = bf16[128,3072]{1,0:T(8,128)(2,1)} async-done(((bf16[1024,3072]{1,0:T(8,128)(2,1)}), bf16[128,3072]{1,0:T(8,128)(2,1)}) %reduce-scatter.19.cloned.1.call-update) | async-done | bytes 786448 | tf_op jit(solution)/shard_map/reduce_scatter | solution.py:401
  2410.5 70.2 %reduce-scatter.15.cloned.1.call-done = bf16[128,1024]{1,0:T(8,128)(2,1)} async-done(((bf16[1024,1024]{1,0:T(8,128)(2,1)}), bf16[128,1024]{1,0:T(8,128)(2,1)}) %reduce-scatter.15.cloned.1.call-update) | async-done | bytes 262160 | tf_op jit(solution)/shard_map/reduce_scatter | solution.py:395
  2480.6 70.2 %reduce-scatter.13.cloned.1.call-done = bf16[128,1024]{1,0:T(8,128)(2,1)} async-done(((bf16[1024,1024]{1,0:T(8,128)(2,1)}), bf16[128,1024]{1,0:T(8,128)(2,1)}) %reduce-scatter.13.cloned.1.call-update) | async-done | bytes 262160 | tf_op jit(solution)/shard_map/reduce_scatter | solution.py:392
  2563.2 40.1 %all-reduce = (f32[1024]{0:T(1024)}, f32[128]{0:T(128)}, f32[128]{0:T(128)}, f32[1024]{0:T(1024)}) all-reduce(f32[1024]{0:T(1024)S(1)} %get-tuple-element.352, f32[128]{0:T(128)} %bitcast_reduce_fusion, f32[128]{0:T(128)} %bitcast_reduce_fusion.1, f32[1024]{0:T(1024)} %get-tuple-element.350), channel_id=1, replica_groups=mesh['grp'=4,'ctx'=8] {'grp','ctx'}, use_global_device_ids=true, to_apply=%region_17.18 | all-reduce | flops 2304 | bytes 18432 | tf_op jit(solution)/shard_map/psum | solution.py:420
  2607.1 28.5 %all-reduce.4.cloned.1.call-done = (bf16[128,2048]{1,0:T(8,128)(2,1)}, bf16[128,1024]{1,0:T(8,128)(2,1)}, bf16[128,1024]{1,0:T(8,128)(2,1)}, bf16[256,1024]{1,0:...) async-done(((bf16[128,2048]{1,0:T(8,128)(2,1)}, bf16[128,1024]{1,0:T(8,128)(2,1)}, bf16[128,1024]{1,0:T(8,128)(2,1)}, ...) | async-done | bytes 3932176 | tf_op jit(solution)/shard_map/psum | solution.py:412
  (592 shorter events, 976.0 us)
Async XLA Ops:
  7.2 59.6 %copy-start = (s32[288]{0:T(512)S(1)}, s32[288]{0:T(512)}, u32[]{:S(2)}) copy-start(s32[288]{0:T(512)} %param.19) | copy-start | bytes 3460
  7.2 55.0 %all-gather.16.cloned.1.call-start = ((), (), s32[]{:S(2)}) async-start(), calls=%async_computation.11 | async-start | bytes 2359296 | tf_op jit(solution)/shard_map/all_gather | solution.py:167
  7.9 104.2 %all-gather.10.cloned.1.call-start = ((), (), s32[]{:S(2)}) async-start(), calls=%async_computation.8 | async-start | bytes 2359296 | tf_op jit(solution)/shard_map/all_gather | solution.py:166
  8.7 177.5 %all-gather.14.cloned.1.call-start = ((), (), s32[]{:S(2)}) async-start(), calls=%async_computation.10 | async-start | bytes 4718592 | tf_op jit(solution)/shard_map/all_gather | solution.py:165
  9.4 315.7 %all-gather.18.cloned.1.call-start = ((), (), s32[]{:S(2)}) async-start(), calls=%async_computation.12 | async-start | bytes 10616832 | tf_op jit(solution)/shard_map/all_gather | solution.py:225
  11.1 175.1 %copy-start.54 = (f32[576]{0:T(1024)}, f32[576]{0:T(1024)S(1)}, u32[]{:S(2)}) copy-start(f32[576]{0:T(1024)S(1)} %add_rsqrt_fusion.3) | copy-start | bytes 6916
  66.6 397.4 %all-gather.12.cloned.1.call-start = ((), (), s32[]{:S(2)}) async-start(), calls=%async_computation.9 | async-start | bytes 10616832 | tf_op jit(solution)/shard_map/all_gather | solution.py:224
  66.7 45.4 %copy-start.11 = (bf16[576,1024]{1,0:T(8,128)(2,1)S(1)}, bf16[576,1024]{1,0:T(8,128)(2,1)}, u32[]{:S(2)}) copy-start(bf16[576,1024]{1,0:T(8,128)(2,1)} %param.18) | copy-start | bytes 3538948
  66.8 45.4 %copy-start.57 = (f32[1024]{0:T(1024)S(1)}, f32[1024]{0:T(1024)}, u32[]{:S(2)}) copy-start(f32[1024]{0:T(1024)} %param.20) | copy-start | bytes 12292
  71.9 125.5 %copy-start.21 = (f32[576,64]{1,0:T(8,128)}, f32[576,64]{1,0:T(8,128)S(1)}, u32[]{:S(2)}) copy-start(f32[576,64]{1,0:T(8,128)S(1)} %get-tuple-element.463) | copy-start | bytes 442372
  71.9 125.5 %copy-start.23 = (f32[576,64]{1,0:T(8,128)}, f32[576,64]{1,0:T(8,128)S(1)}, u32[]{:S(2)}) copy-start(f32[576,64]{1,0:T(8,128)S(1)} %get-tuple-element.464) | copy-start | bytes 442372
  121.2 609.0 %all-gather.20.cloned.1.call-start = ((), (), s32[]{:S(2)}) async-start(), calls=%async_computation.13 | async-start | bytes 4718592 | tf_op jit(solution)/shard_map/all_gather | solution.py:168
  121.7 614.0 %all-gather.24.cloned.1.call-start = ((), (), s32[]{:S(2)}) async-start(), calls=%async_computation.15 | async-start | bytes 7077888 | tf_op jit(solution)/shard_map/all_gather | solution.py:237
  122.5 623.2 %all-gather.22.cloned.1.call-start = ((), (), s32[]{:S(2)}) async-start(), calls=%async_computation.14 | async-start | bytes 7077888 | tf_op jit(solution)/shard_map/all_gather | solution.py:236
  123.2 712.8 %all-gather.26.cloned.1.call-start = ((), (), s32[]{:S(2)}) async-start(), calls=%async_computation.16 | async-start | bytes 7077888 | tf_op jit(solution)/shard_map/all_gather | solution.py:238
  124.0 1741.7 %reduce-scatter.9.cloned.1.call-start = ((), (), s32[]{:S(2)}) async-start(), calls=%async_computation.17 | async-start | bytes 21233664 | tf_op jit(solution)/shard_map/reduce_scatter | solution.py:341
  735.4 128.5 %copy-start.16 = (f32[576,1024]{1,0:T(8,128)}, f32[576,1024]{1,0:T(8,128)S(1)}, u32[]{:S(2)}) copy-start(f32[576,1024]{1,0:T(8,128)S(1)} %get-tuple-element.466) | copy-start | bytes 7077892
  745.7 90.3 %copy-start.41 = (bf16[576,1024]{1,0:T(8,128)(2,1)S(1)}, bf16[576,1024]{1,0:T(8,128)(2,1)}, u32[]{:S(2)}) copy-start(bf16[576,1024]{1,0:T(8,128)(2,1)} %param.31) | copy-start | bytes 3538948
  836.0 13.7 copy-start.64
  1554.0 402.4 %reduce-scatter.17.cloned.1.call-start = ((), (), s32[]{:S(2)}) async-start(), calls=%async_computation.21 | async-start | bytes 4718592 | tf_op jit(solution)/shard_map/reduce_scatter | solution.py:398
  1562.4 485.5 %reduce-scatter.11.cloned.1.call-start = ((), (), s32[]{:S(2)}) async-start(), calls=%async_computation.18 | async-start | bytes 4718592 | tf_op jit(solution)/shard_map/reduce_scatter | solution.py:389
  1569.8 13.2 copy-start.28
  1569.9 19.9 slice-start.2
  1605.0 564.3 %reduce-scatter.23.cloned.1.call-start = ((), (), s32[]{:S(2)}) async-start(), calls=%async_computation.24 | async-start | bytes 7077888 | tf_op jit(solution)/shard_map/reduce_scatter | solution.py:407
  1615.3 674.6 %reduce-scatter.21.cloned.1.call-start = ((), (), s32[]{:S(2)}) async-start(), calls=%async_computation.23 | async-start | bytes 7077888 | tf_op jit(solution)/shard_map/reduce_scatter | solution.py:404
  1625.6 784.8 %reduce-scatter.19.cloned.1.call-start = ((), (), s32[]{:S(2)}) async-start(), calls=%async_computation.22 | async-start | bytes 7077888 | tf_op jit(solution)/shard_map/reduce_scatter | solution.py:401
  1635.0 235.3 %copy-start.63 = (f32[128]{0:T(128)S(1)}, f32[128]{0:T(128)}, u32[]{:S(2)}) copy-start(f32[128]{0:T(128)} %param.25) | copy-start | bytes 1540
  1635.0 845.6 %reduce-scatter.15.cloned.1.call-start = ((), (), s32[]{:S(2)}) async-start(), calls=%async_computation.20 | async-start | bytes 2359296 | tf_op jit(solution)/shard_map/reduce_scatter | solution.py:395
  1870.2 680.6 %reduce-scatter.13.cloned.1.call-start = ((), (), s32[]{:S(2)}) async-start(), calls=%async_computation.19 | async-start | bytes 2359296 | tf_op jit(solution)/shard_map/reduce_scatter | solution.py:392
  1885.4 750.2 %all-reduce.4.cloned.1.call-start = ((), (), s32[]{:S(2)}) async-start(), calls=%async_computation.25 | async-start | bytes 7864320 | tf_op jit(solution)/shard_map/psum | solution.py:412
  1894.3 656.5 %copy-start.32 = (bf16[576,2048]{1,0:T(8,128)(2,1)S(1)}, bf16[576,2048]{1,0:T(8,128)(2,1)}, u32[]{:S(2)}) copy-start(bf16[576,2048]{1,0:T(8,128)(2,1)} %copy-done.31) | copy-start | bytes 7077892
  2559.9 43.4 %copy-start.20 = (f32[576,1024]{1,0:T(8,128)S(1)}, f32[576,1024]{1,0:T(8,128)}, u32[]{:S(2)}) copy-start(f32[576,1024]{1,0:T(8,128)} %copy-done.18) | copy-start | bytes 7077892
  (108 other events, 578.6 us)
Sparse Core Ops, SparseCore 0:
  10.2 51.9 all-gather.15
  64.3 47.7 all-gather.9
  114.2 71.8 all-gather.13
  188.8 136.3 all-gather.17
  327.7 136.2 all-gather.11
  466.0 71.5 all-gather.19
  539.8 97.2 all-gather.23
  639.3 97.2 all-gather.21
  738.7 97.2 all-gather.25
  1554.1 311.5 reduce-scatter.8
  1869.3 87.0 reduce-scatter.16
  1960.3 87.6 reduce-scatter.10
  2051.5 117.7 reduce-scatter.22
  2172.7 117.1 reduce-scatter.20
  2293.3 117.0 reduce-scatter.18
  2413.9 66.7 reduce-scatter.14
  2484.0 66.7 reduce-scatter.12
  2553.5 82.0 all-reduce.3
where the time goes:
time: 2660 us; the launch traced here: 2650 us
  waiting for transfers between devices  1370 us (52%)
  matrix products  761 us (29%)
  local copies, waits for them, and re-layouts  263 us (10%)
  other arithmetic  161 us (6%)
  blocking collectives  40.1 us (2%)
  loops' own time  37.1 us (1%)
    reduce_scatter x1, waiting for transfers between devices, shards(): lax.psum_scatter(key_gradient_parts.reshape(group_length, 2, KEY_VALUE_HE...  231 us
    dot_general x9, matrix products, block_back(): jnp.einsum('grtd,ngd->grtn', head_grads, values_part, preferred_element_t...  135 us
    all_gather x1, waiting for transfers between devices, shards(): lax.all_gather(key_low, 'ctx', axis=0, tiled=True)  126 us
    all_gather x1, waiting for transfers between devices, shards(): lax.all_gather(reduced_value, 'ctx', axis=0, tiled=True)  122 us
    reduce_scatter x1, waiting for transfers between devices, shards(): lax.psum_scatter(grad_down.astype(jnp.bfloat16), 'ctx', scatter_dimension...  121 us
    reduce_scatter x1, waiting for transfers between devices, shards(): lax.psum_scatter(grad_wup.astype(jnp.bfloat16), 'ctx', scatter_dimension=...  121 us
    reduce_scatter x1, waiting for transfers between devices, shards(): lax.psum_scatter(grad_wgate.astype(jnp.bfloat16), 'ctx', scatter_dimensio...  121 us
    dot_general x9, matrix products, key_terms(): jnp.einsum('grtn,grtd->ngd', weights_low, scaled_high, preferred_element_...  92.2 us
  transfers between devices with their start and end apart: 18, of which 15 were waited for; matrix products, arithmetic and copies ran while one was open for 17% of the time, Pallas kernels for 0%

commit v1 on v0

--- a/solution.py
+++ b/solution.py
@@ -1,8 +1,11 @@
+import functools
 import math
 
 import jax
 import jax.numpy as jnp
 from jax import lax
+from jax.experimental import pallas as pl
+from jax.experimental.pallas import tpu as pltpu
 from jax.sharding import PartitionSpec as P
 
 QUERY_HEADS = 16
@@ -437,9 +440,549 @@
     )
 
 
+f32 = jnp.float32
+bf16 = jnp.bfloat16
+AXES = ("grp", "ctx")
+N_GRP = 4
+N_CTX = 8
+SCALE = 1.0 / math.sqrt(HEAD_SIZE)
+EXP2_SCALE = math.log2(math.e) / math.sqrt(HEAD_SIZE)
+VMEM_LIMIT = 60 * 1024 * 1024
+
+
+def nt(a, b):
+    return lax.dot_general(a, b, (((1,), (1,)), ((), ())), preferred_element_type=f32)
+
+
+def nn(a, b):
+    return jnp.dot(a, b, preferred_element_type=f32)
+
+
+def tn(a, b):
+    return lax.dot_general(a, b, (((0,), (0,)), ((), ())), preferred_element_type=f32)
+
+
+def rows16(start):
+    return pl.ds(pl.multiple_of(start, BLK), BLK)
+
+
+def rope_kernel_form(u, cos, sin):
+    return u * cos + pltpu.roll(u, HEAD_SIZE // 2, 1) * sin
+
+
+def rope_back_kernel_form(d, cos, sin):
+    return d * cos - pltpu.roll(d, HEAD_SIZE // 2, 1) * sin
+
+
+def qkv_kernel(dst, *refs):
+    pieces = refs[:8]
+    w_ref, qg_ref, kg_ref, cos_ref, sin_ref, h_ref, q_ref, k_ref, v_ref, raw_ref = refs[8:]
+    step = pl.program_id(0)
+    for r in range(8):
+        for kk in range(4):
+            place = dst[r, step * 4 + kk]
+            h_ref[rows16(kk * 128 + place * BLK), :] = pieces[r][kk * BLK : (kk + 1) * BLK, :]
+    acc = nn(h_ref[...], w_ref[...])
+    cos, sin = cos_ref[...], sin_ref[...]
+    for i in range(3):
+        u = acc[:, i * 128 : (i + 1) * 128]
+        raw_ref[:, i * 128 : (i + 1) * 128] = u
+        n, _ = normed_parts(u)
+        gain = qg_ref[...] if i < 2 else kg_ref[...]
+        out = rope_kernel_form(n * gain, cos, sin).astype(bf16)
+        if i < 2:
+            q_ref[:, i * 128 : (i + 1) * 128] = out
+        else:
+            k_ref[...] = out
+    v_ref[...] = acc[:, 384:].astype(bf16)
+
+
+def qkv_call(dst, pieces, w, qg, kg, cos, sin, group_length):
+    rows = 512
+    return pl.pallas_call(
+        qkv_kernel,
+        grid_spec=pltpu.PrefetchScalarGridSpec(
+            num_scalar_prefetch=1,
+            grid=(group_length // rows,),
+            in_specs=[pl.BlockSpec((rows // 8, w.shape[0]), lambda g, d: (g, 0))] * 8
+            + [
+                pl.BlockSpec(w.shape, lambda g, d: (0, 0)),
+                pl.BlockSpec((1, 128), lambda g, d: (0, 0)),
+                pl.BlockSpec((1, 128), lambda g, d: (0, 0)),
+                pl.BlockSpec((rows, 128), lambda g, d: (g, 0)),
+                pl.BlockSpec((rows, 128), lambda g, d: (g, 0)),
+            ],
+            out_specs=[
+                pl.BlockSpec((rows, w.shape[0]), lambda g, d: (g, 0)),
+                pl.BlockSpec((rows, 256), lambda g, d: (g, 0)),
+                pl.BlockSpec((rows, 128), lambda g, d: (g, 0)),
+                pl.BlockSpec((rows, 128), lambda g, d: (g, 0)),
+                pl.BlockSpec((rows, 384), lambda g, d: (g, 0)),
+            ],
+        ),
+        out_shape=[
+            jax.ShapeDtypeStruct((group_length, w.shape[0]), bf16),
+            jax.ShapeDtypeStruct((group_length, 256), bf16),
+            jax.ShapeDtypeStruct((group_length, 128), bf16),
+            jax.ShapeDtypeStruct((group_length, 128), bf16),
+            jax.ShapeDtypeStruct((group_length, 384), f32),
+        ],
+        compiler_params=pltpu.CompilerParams(vmem_limit_bytes=VMEM_LIMIT),
+        name="qkv_rope",
+    )(dst, *pieces, w, qg, kg, cos, sin)
+
+
+def causal(p, first_key, first_row):
+    key = lax.broadcasted_iota(jnp.int32, p.shape, 0) + first_key
+    row = lax.broadcasted_iota(jnp.int32, p.shape, 1) + first_row
+    return jnp.where(key <= row, p, 0.0)
+
+
+SPAN = 512
+PROMPT_UNITS = tuple(
+    (row0, tuple((key0, key0 == row0) for key0 in range(0, row0 + 1, SPAN)))
+    for row0 in range(0, PROMPT, SPAN)
+)
+
+
+def attn_fwd_kernel(n_cont, dst, q_ref, k_ref, v_ref, *refs):
+    outs = refs[:8]
+    o_ref, lse_ref, vt_ref = refs[8:]
+    vt_ref[...] = jnp.transpose(v_ref[:PROMPT, :])
+
+    def unit(index, row0, n, tiles):
+        for h in range(2):
+            cols = slice(h * 128, (h + 1) * 128)
+            qh = q_ref[pl.ds(row0, n), cols]
+            total = jnp.zeros((1, n), f32)
+            mixed = jnp.zeros((HEAD_SIZE, n), f32)
+            for keys, values_t, diagonal in tiles:
+                p = jnp.exp2(nt(keys, qh) * EXP2_SCALE)
+                if diagonal:
+                    p = causal(p, 0, 0)
+                total = total + jnp.sum(p, axis=0, keepdims=True)
+                mixed = mixed + nn(values_t, p.astype(bf16))
+            o_ref[pl.ds(row0, n), cols] = jnp.transpose(mixed / total)
+            lse_ref[index, h : h + 1, :n] = jnp.log2(total)
+
+    def prompt_tile(key0, diagonal):
+        return (k_ref[key0 : key0 + SPAN, :], vt_ref[:, key0 : key0 + SPAN], diagonal)
+
+    for index, (row0, tiles) in enumerate(PROMPT_UNITS):
+        unit(index, row0, SPAN, [prompt_tile(*t) for t in tiles])
+
+    def continuation(c, carry):
+        row0 = pl.multiple_of(PROMPT + c * CONT_LEN, 64)
+        own = pl.ds(row0, CONT_LEN)
+        tiles = [prompt_tile(key0, False) for key0 in range(0, PROMPT, SPAN)]
+        tiles.append((k_ref[own, :], jnp.transpose(v_ref[own, :]), True))
+        unit(c + len(PROMPT_UNITS), row0, CONT_LEN, tiles)
+        return carry
+
+    lax.fori_loop(0, n_cont, continuation, 0)
+
+    def send_slot(slot, carry):
+        for r in range(8):
+            natural = slot * 128 + dst[r, slot] * BLK
+            rows = o_ref[rows16(natural), :].astype(bf16)
+            head, other = r // 4, 1 - r // 4
+            outs[r][rows16(slot * BLK), :] = rows[:, head * 128 : (head + 1) * 128]
+            outs[r ^ 4][rows16(slot * BLK + outs[0].shape[0] // 2), :] = rows[
+                :, other * 128 : (other + 1) * 128
+            ]
+        return carry
+
+    lax.fori_loop(0, outs[0].shape[0] // 2 // BLK, send_slot, 0)
+
+
+def whole_call(kernel, name, args, outs, scratch, cost):
+    smem = pl.BlockSpec(memory_space=pltpu.SMEM)
+    vmem = pl.BlockSpec(memory_space=pltpu.VMEM)
+    return pl.pallas_call(
+        kernel,
+        in_specs=[smem if a.dtype == jnp.int32 else vmem for a in args],
+        out_specs=[vmem] * len(outs),
+        out_shape=[jax.ShapeDtypeStruct(s, t) for s, t in outs],
+        scratch_shapes=scratch,
+        compiler_params=pltpu.CompilerParams(vmem_limit_bytes=VMEM_LIMIT),
+        cost_estimate=pl.CostEstimate(flops=cost, bytes_accessed=20000000, transcendentals=0),
+        name=name,
+    )(*args)
+
+
+def attn_fwd_call(dst, q, k, v):
+    length = q.shape[0]
+    n_cont = (length - PROMPT) // CONT_LEN
+    row_total = length // 8
+    outs = [((2 * row_total, 128), bf16)] * 8 + [
+        ((length, 256), f32),
+        ((n_cont + len(PROMPT_UNITS), 8, SPAN), f32),
+    ]
+    return whole_call(
+        functools.partial(attn_fwd_kernel, n_cont),
+        "attn_fwd",
+        (dst, q, k, v),
+        outs,
+        [pltpu.VMEM((128, PROMPT), bf16)],
+        7000000000,
+    )
+
+
+def attn_bwd_kernel(n_cont, dst, flag, q_ref, k_ref, v_ref, o_ref, lse_ref, raw_ref, *refs):
+    pieces = refs[:8]
+    qg_ref, kg_ref, cos_ref, sin_ref = refs[8:12]
+    outs = refs[12:20]
+    grads_ref, gains_ref, do_ref, kt_ref, dk_ref, dv_ref = refs[20:]
+    row_total = pieces[0].shape[0] // 2
+
+    def take_slot(slot, carry):
+        for r in range(8):
+            natural = slot * 128 + dst[r, slot] * BLK
+            head, other = r // 4, 1 - r // 4
+            do_ref[rows16(natural), head * 128 : (head + 1) * 128] = pieces[r][
+                rows16(slot * BLK), :
+            ]
+            do_ref[rows16(natural), other * 128 : (other + 1) * 128] = pieces[r ^ 4][
+                rows16(slot * BLK + row_total), :
+            ]
+        return carry
+
+    lax.fori_loop(0, row_total // BLK, take_slot, 0)
+    kt_ref[...] = jnp.transpose(k_ref[:PROMPT, :])
+    dk_ref[...] = jnp.zeros_like(dk_ref)
+    dv_ref[...] = jnp.zeros_like(dv_ref)
+    gains_ref[...] = jnp.zeros_like(gains_ref)
+
+    def head_back(grad, row0, n, head, table0, gain, gain_row):
+        cols = slice(head * 128, (head + 1) * 128)
+        table = slice(table0, table0 + n)
+        normed, inverse = normed_parts(raw_ref[pl.ds(row0, n), cols])
+        back = rope_back_kernel_form(grad * SCALE, cos_ref[table, :], sin_ref[table, :])
+        gains_ref[gain_row : gain_row + 1, :] += jnp.sum(back * normed, axis=0, keepdims=True)
+        grads_ref[pl.ds(row0, n), cols] = norm_back(back * gain, normed, inverse).astype(bf16)
+
+    def unit(index, row0, n, table0, tiles):
+        for h in range(2):
+            cols = slice(h * 128, (h + 1) * 128)
+            qh = q_ref[pl.ds(row0, n), cols]
+            doh = do_ref[pl.ds(row0, n), cols]
+            lse = lse_ref[index, h : h + 1, :n]
+            delta = jnp.sum(
+                jnp.transpose(doh.astype(f32) * o_ref[pl.ds(row0, n), cols]), axis=0, keepdims=True
+            )
+            dq = jnp.zeros((HEAD_SIZE, n), f32)
+            for keys, keys_t, values, diagonal, accumulate in tiles:
+                p = jnp.exp2(nt(keys, qh) * EXP2_SCALE - lse)
+                if diagonal:
+                    p = causal(p, 0, 0)
+                ds = (p * (nt(values, doh) - delta)).astype(bf16)
+                accumulate(h, nn(ds, qh), nn(p.astype(bf16), doh))
+                dq = dq + nn(keys_t, ds)
+            head_back(jnp.transpose(dq), row0, n, h, table0, qg_ref[...], 0)
+
+    def prompt_tile(key0, diagonal):
+        keys = slice(key0, key0 + SPAN)
+
+        def accumulate(h, dk, dv):
+            dk_ref[keys, :] += dk
+            dv_ref[keys, :] += dv
+
+        return (k_ref[keys, :], kt_ref[:, keys], v_ref[keys, :], diagonal, accumulate)
+
+    for index, (row0, tiles) in enumerate(PROMPT_UNITS):
+        unit(index, row0, SPAN, row0, [prompt_tile(*t) for t in tiles])
+
+    def continuation(c, carry):
+        row0 = pl.multiple_of(PROMPT + c * CONT_LEN, 64)
+        own = pl.ds(row0, CONT_LEN)
+        kept = []
+
+        def accumulate(h, dk, dv):
+            kept.append((dk, dv))
+
+        tiles = [prompt_tile(key0, False) for key0 in range(0, PROMPT, SPAN)]
+        keys = k_ref[own, :]
+        tiles.append((keys, jnp.transpose(keys), v_ref[own, :], True, accumulate))
+        unit(c + len(PROMPT_UNITS), row0, CONT_LEN, PROMPT, tiles)
+        head_back(kept[0][0] + kept[1][0], row0, CONT_LEN, 2, PROMPT, kg_ref[...], 1)
+        grads_ref[own, 384:] = (kept[0][1] + kept[1][1]).astype(bf16)
+        return carry
+
+    lax.fori_loop(0, n_cont, continuation, 0)
+    head_back(dk_ref[...], 0, PROMPT, 2, 0, kg_ref[...], 1)
+    grads_ref[:PROMPT, 384:] = dv_ref[...].astype(bf16)
+
+    def send_slot(slot, carry):
+        for r in range(8):
+            natural = slot * 128 + dst[r, slot] * BLK
+            rows = grads_ref[rows16(natural), :]
+            first = flag[0] == 0
+            parts = (
+                jnp.where(first, rows[:, 256:384], rows[:, 384:]),
+                jnp.where(first, rows[:, 384:], rows[:, 256:384]),
+            )
+            head, other = r // 4, 1 - r // 4
+            own = rows16(slot * BLK)
+            outs[r][own, :128] = rows[:, head * 128 : (head + 1) * 128]
+            outs[r][own, 128:] = parts[head]
+            sibling = rows16(slot * BLK + row_total)
+            outs[r ^ 4][sibling, :128] = rows[:, other * 128 : (other + 1) * 128]
+            outs[r ^ 4][sibling, 128:] = parts[other]
+        return carry
+
+    lax.fori_loop(0, row_total // BLK, send_slot, 0)
+
+
+def attn_bwd_call(dst, flag, q, k, v, o, lse, raw, pieces, qg, kg, cos, sin):
+    length = q.shape[0]
+    n_cont = (length - PROMPT) // CONT_LEN
+    row_total = length // 8
+    outs = [((2 * row_total, 256), bf16)] * 8 + [((length, 512), bf16), ((8, 128), f32)]
+    scratch = [
+        pltpu.VMEM((length, 256), bf16),
+        pltpu.VMEM((128, PROMPT), bf16),
+        pltpu.VMEM((PROMPT, 128), f32),
+        pltpu.VMEM((PROMPT, 128), f32),
+    ]
+    return whole_call(
+        functools.partial(attn_bwd_kernel, n_cont),
+        "attn_bwd",
+        (dst, flag, q, k, v, o, lse, raw, *pieces, qg, kg, cos, sin),
+        outs,
+        scratch,
+        17000000000,
+    )
+
+
+def device_of(y, core, z_hi, z_lo, x):
+    return (y * 2 + core) * N_CTX + z_hi * 4 + z_lo * 2 + x
+
+
+def permutation(target):
+    pairs = []
+    for i in range(N_GRP * N_CTX):
+        bits = ((i >> 4) & 1, (i >> 3) & 1, (i >> 2) & 1, (i >> 1) & 1, i & 1)
+        pairs.append((i, device_of(*target(*bits))))
+    return pairs
+
+
+HALVES = permutation(lambda y, core, z_hi, z_lo, x: (y, z_hi, core, z_lo, x))
+OVER_Y = permutation(lambda y, core, z_hi, z_lo, x: (1 - y, core, z_hi, z_lo, x))
+SIBLING = permutation(lambda y, core, z_hi, z_lo, x: (y, 1 - core, z_hi, z_lo, x))
+CUBE = [
+    permutation(
+        lambda y, core, z_hi, z_lo, x, r=r: (
+            y,
+            core ^ (r >> 2),
+            z_hi,
+            z_lo ^ ((r >> 1) & 1),
+            x ^ (r & 1),
+        )
+    )
+    for r in range(8)
+]
+CUBES = [
+    [device_of(y, m >> 2, z_hi, (m >> 1) & 1, m & 1) for m in range(8)]
+    for y in range(2)
+    for z_hi in range(2)
+]
+
+
+def permute(a, pairs):
+    return lax.ppermute(a, AXES, pairs)
+
+
+def exchange(chunks):
+    return [chunks[0]] + [permute(chunks[r], CUBE[r]) for r in range(1, 8)]
+
+
+def gather_cube(a):
+    near = [a] + [permute(a, CUBE[r]) for r in range(1, 4)]
+    return near + [permute(t, SIBLING) for t in near]
+
+
+def relative(a, member):
+    return jnp.concatenate(
+        [lax.dynamic_slice_in_dim(a, member ^ r, 1, 0) for r in range(a.shape[0])], axis=0
+    )
+
+
+def reduce_owned(grad, core):
+    part = lax.psum_scatter(grad, "ctx", scatter_dimension=0, tiled=True)
+    part = (part.astype(f32) + permute(part, OVER_Y).astype(f32)).astype(bf16)
+    other = permute(part, SIBLING)
+    first = core == 0
+    return jnp.where(first, part, other), jnp.where(first, other, part)
+
+
+def shards_split(
+    tokens,
+    block_table,
+    norm1_gain,
+    w_query,
+    key_weight,
+    value_weight,
+    query_gain,
+    key_norm_gain,
+    w_out,
+    norm2_gain,
+    w_gate,
+    w_up,
+    w_down,
+    out_grad,
+):
+    row_total, width = tokens.shape
+    group_length = block_table.shape[0] * BLK
+    n_slots = row_total // BLK
+    ff = w_gate.shape[1]
+    position = lax.axis_index("ctx")
+    core = lax.axis_index("grp") % 2
+    member = core * 4 + position % 4
+    qg, kg = query_gain.reshape(1, 128), key_norm_gain.reshape(1, 128)
+
+    inputs_low = permute(tokens, HALVES)
+    inputs = inputs_low.astype(f32)
+    normed_one, inverse_one = normed_parts(inputs)
+    first_hidden = (normed_one * norm1_gain).astype(bf16)
+    hidden_pieces = gather_cube(first_hidden)
+
+    def half(w, parts):
+        return lax.dynamic_index_in_dim(w, core, parts, keepdims=False)
+
+    query_parts = w_query.reshape(-1, 8, 2, 128)
+    key_parts = key_weight.reshape(-1, 8, 128)
+    value_parts = value_weight.reshape(-1, 8, 128)
+    swapped = jnp.concatenate([query_parts[:, :4], query_parts[:, 4:, ::-1]], axis=1)
+    own_columns = jnp.concatenate(
+        [swapped.reshape(-1, 8, 256), key_parts, value_parts], axis=2
+    ).transpose(1, 0, 2)
+    w_attn = lax.all_to_all(
+        permute(own_columns, HALVES), AXES, 0, 0, tiled=True, axis_index_groups=CUBES
+    ).reshape(width, 512)
+
+    gate_half = half(w_gate.reshape(-1, N_CTX, 2, ff // 16), 2).reshape(-1, ff // 2)
+    up_half = half(w_up.reshape(-1, N_CTX, 2, ff // 16), 2).reshape(-1, ff // 2)
+    down_half = half(w_down.reshape(2, -1, width), 0)
+    out_half = half(w_out.reshape(2, -1, width), 0)
+    back_half = jnp.concatenate(
+        [half(query_parts, 2), jnp.where(core == 0, key_parts, value_parts)], axis=2
+    ).reshape(-1, 2048)
+
+    def gather(w):
+        return lax.all_gather(w, "ctx", axis=0, tiled=True)
+
+    out_rel = relative(gather(out_half).reshape(8, 128, width), member).reshape(8 * 128, width)
+    gate_full, up_full, down_full = gather(gate_half), gather(up_half), gather(down_half)
+    back_full = gather(back_half).reshape(width, 8, 256).transpose(1, 0, 2)
+    back_rel = relative(back_full, member).transpose(1, 0, 2).reshape(width, 2048)
+    grad_low = permute(out_grad, HALVES)
+    grad_both = jnp.concatenate([grad_low, permute(grad_low, SIBLING)], axis=0)
+
+    cosine, sine = rotation(jnp.arange(PROMPT + CONT_LEN, dtype=jnp.int32))
+    cos = jnp.concatenate([cosine[:, 0], cosine[:, 0]], axis=1)
+    sin = jnp.concatenate([-sine[:, 0], sine[:, 0]], axis=1)
+    n_cont = (group_length - PROMPT) // CONT_LEN
+    cos_all = jnp.concatenate([cos[:PROMPT]] + [cos[PROMPT:]] * n_cont, axis=0)
+    sin_all = jnp.concatenate([sin[:PROMPT]] + [sin[PROMPT:]] * n_cont, axis=0)
+
+    dst = relative(block_table.reshape(8, n_slots), member) - 8 * jnp.arange(n_slots)[None, :]
+
+    h_nat, q, k, v, raw = qkv_call(
+        dst, hidden_pieces, w_attn, qg, kg, cos_all, sin_all, group_length
+    )
+    *mixed_out, mixed, lse = attn_fwd_call(dst, q, k, v)
+    mixed_both = jnp.concatenate(exchange(mixed_out), axis=1)
+
+    def with_sibling(part):
+        return part[:row_total] + permute(part[row_total:].astype(bf16), SIBLING).astype(f32)
+
+    def both(a):
+        return jnp.concatenate([a, permute(a, SIBLING)], axis=0)
+
+    resid_one = inputs + with_sibling(nn(mixed_both, out_rel))
+    normed_two, inverse_two = normed_parts(resid_one)
+    hidden_two = both((normed_two * norm2_gain).astype(bf16))
+    gate_proj = nn(hidden_two, gate_full)
+    up_proj = nn(hidden_two, up_full)
+    gate_sigmoid = jax.nn.sigmoid(gate_proj)
+    gate_silu = gate_proj * gate_sigmoid
+    hidden_low = (gate_silu * up_proj).astype(bf16)
+    outcome = (resid_one + with_sibling(nn(hidden_low, down_full))).astype(bf16)
+    outcome = permute(outcome, HALVES)
+
+    grad_hidden = nt(grad_both, down_full)
+    grad_gate = (
+        grad_hidden * up_proj * gate_sigmoid * (1.0 + gate_proj * (1.0 - gate_sigmoid))
+    ).astype(bf16)
+    grad_up = (grad_hidden * gate_silu).astype(bf16)
+    grad_two = with_sibling(nt(grad_gate, gate_full) + nt(grad_up, up_full))
+    gain_two_part = jnp.sum(grad_two * normed_two, axis=0)
+    grad_resid = grad_low.astype(f32) + norm_back(grad_two * norm2_gain, normed_two, inverse_two)
+    grad_attn = both(grad_resid.astype(bf16))
+    mixed_grads = nt(grad_attn, out_rel).astype(bf16)
+    grad_pieces = exchange([mixed_grads[:, r * 128 : (r + 1) * 128] for r in range(8)])
+
+    grad_wdown = tn(hidden_low, grad_both).astype(bf16)
+    grad_wgate = tn(hidden_two, grad_gate).astype(bf16)
+    grad_wup = tn(hidden_two, grad_up).astype(bf16)
+    grad_wout = tn(mixed_both, grad_attn).astype(bf16)
+    grad_wout = relative(grad_wout.reshape(8, 128, width), member).reshape(8 * 128, width)
+
+    flag = core.astype(jnp.int32).reshape(1)
+    *qkv_out, qkv_grads, gains = attn_bwd_call(
+        dst, flag, q, k, v, mixed, lse, raw, grad_pieces, qg, kg, cos, sin
+    )
+    qkv_both = jnp.concatenate(exchange(qkv_out), axis=1)
+    grad_one = with_sibling(nt(qkv_both, back_rel))
+    gain_one_part = jnp.sum(grad_one * normed_one, axis=0)
+    grad_tokens = grad_resid + norm_back(grad_one * norm1_gain, normed_one, inverse_one)
+    grad_tokens = permute(grad_tokens.astype(bf16), HALVES).astype(f32)
+
+    def interleave(grad):
+        pair = reduce_owned(grad, core)
+        return (
+            jnp.stack([p.reshape(-1, N_CTX, ff // 16) for p in pair], axis=2)
+            .reshape(-1, ff)
+            .astype(f32)
+        )
+
+    grad_wgate, grad_wup = interleave(grad_wgate), interleave(grad_wup)
+    grad_wdown = jnp.concatenate(reduce_owned(grad_wdown, core), axis=0).astype(f32)
+    grad_wout = jnp.concatenate(reduce_owned(grad_wout, core), axis=0).astype(f32)
+
+    grad_attn_w = tn(h_nat, qkv_grads).astype(bf16)
+    owned = lax.all_to_all(
+        grad_attn_w.reshape(8, -1, 512), AXES, 0, 0, tiled=True, axis_index_groups=CUBES
+    )
+    owned = permute(owned, HALVES)
+    owned = (owned.astype(f32) + permute(owned, OVER_Y).astype(f32)).astype(bf16)
+    owned = owned.astype(f32) + permute(owned, SIBLING).astype(f32)
+    owned = owned.transpose(1, 0, 2)
+    query_grads = owned[:, :, :256].reshape(-1, 8, 2, 128)
+    query_grads = jnp.concatenate([query_grads[:, :4], query_grads[:, 4:, ::-1]], axis=1)
+
+    gain_grads = lax.psum((gain_one_part, gains[0], gains[1], gain_two_part), AXES)
+    return (
+        outcome,
+        grad_tokens,
+        gain_grads[0],
+        query_grads.reshape(-1, 2048),
+        owned[:, :, 256:384].reshape(-1, 1024),
+        owned[:, :, 384:].reshape(-1, 1024),
+        gain_grads[1],
+        gain_grads[2],
+        grad_wout,
+        gain_grads[3],
+        grad_wgate,
+        grad_wup,
+        grad_wdown,
+    )
+
+
 def solution(mesh):
+    split = mesh.shape["grp"] == N_GRP and mesh.shape["ctx"] == N_CTX
     return jax.shard_map(
-        shards,
+        shards_split if split else shards,
         mesh=mesh,
         in_specs=(
             P(("grp", "ctx"), None),

time: 2660 us -> 877 us (0.33)
  waiting for transfers between devices: 1370 us -> 160 us
  matrix products: 761 us -> 105 us
  starting transfers between devices: 0.72 us -> 212 us
  local copies, waits for them, and re-layouts: 263 us -> 113 us
  other arithmetic: 161 us -> 49.1 us
  Pallas kernels: 0 us -> 98.6 us
  blocking collectives: 40.1 us -> 113 us
  loops' own time: 37.1 us -> 0 us
    reduce_scatter x8 -> x4, waiting for transfers between devices: 887 us -> 0.01 us  [reduce_owned(): part = lax.psum_scatter(grad, 'ctx', scatter_dimension=0, tiled=True)]
    dot_general x93 -> x14, matrix products: 761 us -> 105 us  [the longest x5 38.5 us: tn(): lax.dot_general(a, b, (((0,), (0,)), ((), ())), preferred_element_type=f32)]
    all_gather x9 -> x5, waiting for transfers between devices: 454 us -> 2.52 us  [gather(): return lax.all_gather(w, 'ctx', axis=0, tiled=True)]
    ppermute x0 -> x51, starting transfers between devices: none -> 156 us  [permute(): return lax.ppermute(a, AXES, pairs)]
    ppermute x0 -> x51, waiting for transfers between devices: none -> 150 us  [permute(): return lax.ppermute(a, AXES, pairs)]
    pallas_call x0 -> x3, Pallas kernels: none -> 98.6 us  [the longest x2 77.7 us: whole_call(): pl.pallas_call(kernel, in_specs=[smem if a.dtype == jnp.int32 else vmem f...]
    psum x1, blocking collectives: 40.1 us -> 113 us  [shards_split(): lax.psum((gain_one_part, gains[0], gains[1], gain_two_part), AXES)]
    dynamic_slice x54 -> x7, local copies, waits for them, and re-layouts: 77.1 us -> 6.67 us  [the longest x6 6.65 us: half(): return lax.dynamic_index_in_dim(w, core, parts, keepdims=False)]
  transfers between devices with their start and end apart: 18 -> 62, of which waited for: 15 -> 18; matrix products, arithmetic and copies ran while one was open for 17% -> 28% of each run, Pallas kernels for 0% -> 11%
where the time goes in v1:
time: 877 us; the launch traced here: 867 us
  starting transfers between devices  212 us (24%)
  waiting for transfers between devices  160 us (18%)
  local copies, waits for them, and re-layouts  113 us (13%)
  blocking collectives  113 us (13%)
  matrix products  105 us (12%)
  Pallas kernels  98.6 us (11%)
  other arithmetic  49.1 us (6%)
  between operations  15.2 us (2%)
    ppermute x51, starting transfers between devices, permute(): return lax.ppermute(a, AXES, pairs)  156 us
    ppermute x51, waiting for transfers between devices, permute(): return lax.ppermute(a, AXES, pairs)  150 us
    psum x1, blocking collectives, shards_split(): lax.psum((gain_one_part, gains[0], gains[1], gain_two_part), AXES)  113 us
    pallas_call x2, Pallas kernels, whole_call(): pl.pallas_call(kernel, in_specs=[smem if a.dtype == jnp.int32 else vmem f...  77.7 us
    all_to_all x1, starting transfers between devices, shards_split(): lax.all_to_all(permute(own_columns, HALVES), AXES, 0, 0, tiled=True, axis...  50.9 us
    unnamed x144, local copies, waits for them, and re-layouts  50.6 us
    dot_general x5, matrix products, tn(): lax.dot_general(a, b, (((0,), (0,)), ((), ())), preferred_element_type=f32)  38.5 us
    dot_general x5, matrix products, nt(): lax.dot_general(a, b, (((1,), (1,)), ((), ())), preferred_element_type=f32)  38.3 us
  transfers between devices with their start and end apart: 62, of which 18 were waited for; matrix products, arithmetic and copies ran while one was open for 28% of the time, Pallas kernels for 11%

profile of v1, /device:TPU:0, one launch (start us, length us, event | category | flops | bytes accessed | tf_op | source)
XLA Modules:
  0.0 866.6 jit_solution(1759396229801831813)
XLA Ops:
  23.3 9.5 %collective-permute-start.8 = (bf16[8,128,512]{2,0,1:T(8,128)(2,1)}, bf16[8,128,512]{2,0,1:T(8,128)(2,1)}, u32[]{:S(2)}, u32[]{:S(2)}) collective-permute-start(bf16[8,128,512]{2,0,1:T(8,128)(2,1)} %maximum_bitcast_fusion), channel_id=1, source_target_pairs={{0,0},{1,1},{2,2},{3,3},{4,8},{5,9},{6,10},{7,11},{8,4},{9,5},{10,... | collective-permute-start | bytes 3145736 | tf_op jit(solution)/shard_map/ppermute | solution.py:792
  32.8 10.4 %collective-permute-start.20 = (bf16[576,1024]{1,0:T(8,128)(2,1)}, bf16[576,1024]{1,0:T(8,128)(2,1)}, u32[]{:S(2)}, u32[]{:S(2)}) collective-permute-start(bf16[576,1024]{1,0:T(8,128)(2,1)} %param.27), channel_id=1, source_target_pairs={{0,0},{1,1},{2,2},{3,3},{4,8},{5,9},{6,10},{7,11},{8,4},{9,5},{10,... | collective-permute-start | bytes 3538952 | tf_op jit(solution)/shard_map/ppermute | solution.py:792
  61.3 50.9 %all-to-all-start = ((bf16[8,128,512]{2,1,0:T(8,128)(2,1)}), bf16[8,128,512]{2,1,0:T(8,128)(2,1)S(1)}, u32[]{:S(2)}, u32[]{:S(2)}) async-start(bf16[8,128,512]{2,1,0:T(8,128)(2,1)} %copy.83), calls=%async_computation | async-start | bytes 2097152 | tf_op jit(solution)/shard_map/all_to_all | solution.py:859
  116.8 50.6 %collective-permute-start.6 = (bf16[576,1024]{1,0:T(8,128)(2,1)}, bf16[576,1024]{1,0:T(8,128)(2,1)}, u32[]{:S(2)}, u32[]{:S(2)}) collective-permute-start(bf16[576,1024]{1,0:T(8,128)(2,1)} %collective-permute-done.2.refs_2_), channel_id=1, source_target_pairs={{0,8},{1,9},{2,10},{3,11},{4,12},{5,13},{6,14},{7,15},{8,0},{9,1},... | collective-permute-start | bytes 3538952 | tf_op jit(solution)/shard_map/ppermute | solution.py:792
  167.3 32.0 %collective-permute-start.7 = (bf16[576,1024]{1,0:T(8,128)(2,1)}, bf16[576,1024]{1,0:T(8,128)(2,1)}, u32[]{:S(2)}, u32[]{:S(2)}) collective-permute-start(bf16[576,1024]{1,0:T(8,128)(2,1)} %collective-permute-done.3.refs_3_), channel_id=1, source_target_pairs={{0,8},{1,9},{2,10},{3,11},{4,12},{5,13},{6,14},{7,15},{8,0},{9,1},... | collective-permute-start | bytes 3538952 | tf_op jit(solution)/shard_map/ppermute | solution.py:792
  205.0 7.2 all-to-all-done
  213.2 21.0 %qkv_rope.1 = (bf16[4608,1024]{1,0:T(8,128)(2,1)}, bf16[4608,256]{1,0:T(8,128)(2,1)}, bf16[4608,128]{1,0:T(8,128)(2,1)}, bf16[4608,128]{1,0:T(8,128)(2,1)}, f32[4608,384]{1,0:T(8,128)}) custom-call(s32[8,36]{1,0:T(8,128)} %broadcast_subtract_fusion.dst, bf16[576,1024]{1,0:T(8,128)(2,1)} %fusion.9.refs_0_, bf16[576,1024]{1,0:T(8,128)(2,1)} %collective-permute-done.1.refs_1_, ...), custom_call_target="tpu_custom_call" | custom-call | tf_op jit(solution)/shard_map/qkv_rope/pallas_call | solution.py:502
  234.1 23.5 %attn_fwd.1 = (bf16[1152,128]{1,0:T(8,128)(2,1)}, bf16[1152,128]{1,0:T(8,128)(2,1)}, bf16[1152,128]{1,0:T(8,128)(2,1)}, bf16[1152,128]{1,0:T(8,128)(2,1)}, bf16[...) custom-call(s32[8,36]{1,0:T(8,128)} %broadcast_subtract_fusion.dst, ...), custom_call_target="tpu_custom_call" | custom-call | flops 7000000000 | bytes 20000000 | tf_op jit(solution)/shard_map/attn_fwd/pallas_call | solution.py:601
  271.5 14.3 %collective-permute-done.11 = bf16[1152,128]{1,0:T(8,128)(2,1)S(1)} collective-permute-done((bf16[1152,128]{1,0:T(8,128)(2,1)}, bf16[1152,128]{1,0:T(8,128)(2,1)S(1)}, u32[]{:S(2)}, u32[]{:S(2)}) %collective-permute-start.11) | collective-permute-done | bytes 294944 | tf_op jit(solution)/shard_map/ppermute | solution.py:792
  315.6 9.5 %fusion.24 = f32[1152,1536]{1,0:T(8,128)} fusion(bf16[1024,1536]{0,1:T(8,128)(2,1)} %all-gather.10.cloned.1.call-done, bf16[576,1024]{1,0:T(8,128)(2,1)} %collective-permute-done.17, bf16[576,1024]{1,0:T(8,128)(2,1)} %multiply_convert_fusion.3), kind=kOutput, calls=%fused_computation.177 | convolution fusion | flops 3628597248 | bytes 12582912 | tf_op jit(solution)/shard_map/dot_general | solution.py:458
  325.1 9.3 %fusion.25 = f32[1152,1536]{1,0:T(8,128)} fusion(bf16[1024,1536]{0,1:T(8,128)(2,1)} %all-gather.8.cloned.1.call-done, bf16[576,1024]{1,0:T(8,128)(2,1)} %collective-permute-done.17, bf16[576,1024]{1,0:T(8,128)(2,1)} %multiply_convert_fusion.3), kind=kOutput, calls=%fused_computation.178 | convolution fusion | flops 3628597248 | bytes 12582912 | tf_op jit(solution)/shard_map/dot_general | solution.py:458
  334.4 14.2 %multiply_convert_fusion = (bf16[1152,1536]{1,0:T(8,128)(2,1)}, bf16[1152,1536]{1,0:T(8,128)(2,1)}, bf16[1152,1536]{1,0:T(8,128)(2,1)S(1)}) fusion(f32[1152,1536]{1,0:T(8,128)} %fusion.25, f32[1152,1536]{1,0:T(8,128)} %fusion.24, bf16[1152,1024]{1,0:T(8,128)(2,1)} %constant_dynamic-update-slice_fusion.24, bf16[1,1536,1024]{2,1,0:T(8,128)(2,1)} %all-gather.16.cloned.1.call-done), kind=kOutput, calls=%fused_computation | convolution fusion | flops 3650420736 | bytes 30277632 | tf_op jit(solution)/shard_map/dot_general | solution.py:454
  350.5 7.4 convolution_convert_fusion.1
  358.0 8.6 convolution_convert_fusion.2
  366.7 7.0 fusion.33
  382.9 7.5 convolution_convert_fusion.3
  390.5 7.0 fusion.7
  442.8 6.6 copy.96
  472.8 7.6 collective-permute-done.26.refs_3_
  481.6 9.0 %collective-permute-done.29.refs_6_ = bf16[1152,128]{1,0:T(8,128)(2,1)} collective-permute-done((bf16[1152,128]{1,0:T(8,128)(2,1)}, bf16[1152,128]{1,0:T(8,128)(2,1)}, u32[]{:S(2)}, u32[]{:S(2)}) %collective-permute-start.29) | collective-permute-done | bytes 294944 | tf_op jit(solution)/shard_map/ppermute | solution.py:792
  490.6 6.9 collective-permute-done.30.refs_7_
  497.5 54.2 %attn_bwd.1 = (bf16[1152,256]{1,0:T(8,128)(2,1)}, bf16[1152,256]{1,0:T(8,128)(2,1)}, bf16[1152,256]{1,0:T(8,128)(2,1)}, bf16[1152,256]{1,0:T(8,128)(2,1)}, bf16[...) custom-call(s32[8,36]{1,0:T(8,128)} %broadcast_subtract_fusion.dst, ...), custom_call_target="tpu_custom_call" | custom-call | flops 16999999488 | bytes 20000000 | tf_op jit(solution)/shard_map/attn_bwd/pallas_call | solution.py:601
  553.1 10.1 %convolution_convert_fusion.5 = bf16[1024,512]{1,0:T(8,128)(2,1)} fusion(bf16[4608,1024]{1,0:T(8,128)(2,1)} %get-tuple-element.60, bf16[4608,512]{1,0:T(8,128)(2,1)} %get-tuple-element.61), kind=kOutput, calls=%fused_computation.49 | convolution fusion | flops 4832362496 | bytes 15204352 | tf_op jit(solution)/shard_map/dot_general | solution.py:462
  574.2 7.2 collective-permute-done.32
  581.5 31.9 %collective-permute-done.33 = bf16[1152,256]{1,0:T(8,128)(2,1)S(1)} collective-permute-done((bf16[1152,256]{1,0:T(8,128)(2,1)}, bf16[1152,256]{1,0:T(8,128)(2,1)S(1)}, u32[]{:S(2)}, u32[]{:S(2)}) %collective-permute-start.33) | collective-permute-done | bytes 589856 | tf_op jit(solution)/shard_map/ppermute | solution.py:792
  613.6 24.1 %collective-permute-done.36 = bf16[1152,256]{1,0:T(8,128)(2,1)S(1)} collective-permute-done((bf16[1152,256]{1,0:T(8,128)(2,1)}, bf16[1152,256]{1,0:T(8,128)(2,1)S(1)}, u32[]{:S(2)}, u32[]{:S(2)}) %collective-permute-start.36) | collective-permute-done | bytes 589856 | tf_op jit(solution)/shard_map/ppermute | solution.py:792
  637.8 16.6 %collective-permute-done.37 = bf16[1152,256]{1,0:T(8,128)(2,1)S(1)} collective-permute-done((bf16[1152,256]{1,0:T(8,128)(2,1)}, bf16[1152,256]{1,0:T(8,128)(2,1)S(1)}, u32[]{:S(2)}, u32[]{:S(2)}) %collective-permute-start.37) | collective-permute-done | bytes 589856 | tf_op jit(solution)/shard_map/ppermute | solution.py:792
  654.5 6.7 fusion.34
  665.2 10.5 %collective-permute-start.19 = (bf16[576,1024]{1,0:T(8,128)(2,1)}, bf16[576,1024]{1,0:T(8,128)(2,1)}, u32[]{:S(2)}, u32[]{:S(2)}) collective-permute-start(bf16[576,1024]{1,0:T(8,128)(2,1)} %get-tuple-element.139), channel_id=1, source_target_pairs={{0,0},{1,1},{2,2},{3,3},{4,8},{5,9},{6,10},{7,11},{8,4},{9,5},{10,... | collective-permute-start | bytes 3538952 | tf_op jit(solution)/shard_map/ppermute | solution.py:792
  675.6 9.5 %collective-permute-start.40 = (bf16[8,128,512]{2,1,0:T(8,128)(2,1)}, bf16[8,128,512]{2,1,0:T(8,128)(2,1)}, u32[]{:S(2)}, u32[]{:S(2)}) collective-permute-start(bf16[8,128,512]{2,1,0:T(8,128)(2,1)} %all-to-all-done.1), channel_id=1, source_target_pairs={{0,0},{1,1},{2,2},{3,3},{4,8},{5,9},{6,10},{7,11},{8,4},{9,5},{10,... | collective-permute-start | bytes 3145736 | tf_op jit(solution)/shard_map/ppermute | solution.py:792
  696.6 113.3 %all-reduce = (f32[1024]{0:T(1024)}, f32[128]{0:T(128)}, f32[128]{0:T(128)}, f32[1024]{0:T(1024)}) all-reduce(f32[1024]{0:T(1024)S(1)} %get-tuple-element.104, f32[128]{0:T(128)S(1)} %get-tuple-element.160, f32[128]{0:T(128)S(1)} %get-tuple-element.159, f32[1024]{0:T(1024)S(1)} %get-tuple-element.102), channel_id=1, replica_groups=mesh['grp'=4,'ctx'=8] {'grp','ctx'}, use_global_device_ids=true, to_apply=%region_5.6 | all-reduce | flops 2304 | bytes 18432 | tf_op jit(solution)/shard_map/psum | solution.py:964
  824.7 8.2 collective-permute-done.45
  (354 shorter events, 239.3 us)
Async XLA Ops:
  7.2 255.6 %all-gather.14.cloned.1.call-start = ((), (), s32[]{:S(2)}) async-start(), calls=%async_computation.13 | async-start | bytes 2359296 | tf_op jit(solution)/shard_map/all_gather | solution.py:872
  9.1 306.5 %all-gather.10.cloned.1.call-start = ((), (), s32[]{:S(2)}) async-start(), calls=%async_computation.7 | async-start | bytes 3538944 | tf_op jit(solution)/shard_map/all_gather | solution.py:872
  11.4 313.7 %all-gather.8.cloned.1.call-start = ((), (), s32[]{:S(2)}) async-start(), calls=%async_computation.6 | async-start | bytes 3538944 | tf_op jit(solution)/shard_map/all_gather | solution.py:872
  12.7 321.8 %all-gather.16.cloned.1.call-start = ((), (), s32[]{:S(2)}) async-start(), calls=%async_computation.14 | async-start | bytes 3538944 | tf_op jit(solution)/shard_map/all_gather | solution.py:872
  12.7 31.2 %collective-permute-start = (bf16[576,1024]{1,0:T(8,128)(2,1)}, bf16[576,1024]{1,0:T(8,128)(2,1)S(1)}, u32[]{:S(2)}, u32[]{:S(2)}) collective-permute-start(bf16[576,1024]{1,0:T(8,128)(2,1)} %param.14), channel_id=1, source_target_pairs={{0,0},{1,1},{2,2},{3,3},{4,8},{5,9},{6,10},{7,11},{8,4},{9,5},{10,... | collective-permute-start | bytes 3538952 | tf_op jit(solution)/shard_map/ppermute | solution.py:792
  23.3 35.5 %collective-permute-start.8 = (bf16[8,128,512]{2,0,1:T(8,128)(2,1)}, bf16[8,128,512]{2,0,1:T(8,128)(2,1)}, u32[]{:S(2)}, u32[]{:S(2)}) collective-permute-start(bf16[8,128,512]{2,0,1:T(8,128)(2,1)} %maximum_bitcast_fusion), channel_id=1, source_target_pairs={{0,0},{1,1},{2,2},{3,3},{4,8},{5,9},{6,10},{7,11},{8,4},{9,5},{10,... | collective-permute-start | bytes 3145736 | tf_op jit(solution)/shard_map/ppermute | solution.py:792
  32.8 274.5 %collective-permute-start.20 = (bf16[576,1024]{1,0:T(8,128)(2,1)}, bf16[576,1024]{1,0:T(8,128)(2,1)}, u32[]{:S(2)}, u32[]{:S(2)}) collective-permute-start(bf16[576,1024]{1,0:T(8,128)(2,1)} %param.27), channel_id=1, source_target_pairs={{0,0},{1,1},{2,2},{3,3},{4,8},{5,9},{6,10},{7,11},{8,4},{9,5},{10,... | collective-permute-start | bytes 3538952 | tf_op jit(solution)/shard_map/ppermute | solution.py:792
  45.7 71.0 %collective-permute-start.1 = (bf16[576,1024]{1,0:T(8,128)(2,1)}, bf16[576,1024]{1,0:T(8,128)(2,1)}, u32[]{:S(2)}, u32[]{:S(2)}) collective-permute-start(bf16[576,1024]{1,0:T(8,128)(2,1)} %fusion.9.refs_0_), channel_id=1, source_target_pairs={{0,1},{1,0},{2,3},{3,2},{4,5},{5,4},{6,7},{7,6},{8,9},{9,8},{10,11... | collective-permute-start | bytes 3538952 | tf_op jit(solution)/shard_map/ppermute | solution.py:792
  48.6 68.2 %collective-permute-start.2 = (bf16[576,1024]{1,0:T(8,128)(2,1)}, bf16[576,1024]{1,0:T(8,128)(2,1)}, u32[]{:S(2)}, u32[]{:S(2)}) collective-permute-start(bf16[576,1024]{1,0:T(8,128)(2,1)} %fusion.9.refs_0_), channel_id=1, source_target_pairs={{0,2},{1,3},{2,0},{3,1},{4,6},{5,7},{6,4},{7,5},{8,10},{9,11},{10,... | collective-permute-start | bytes 3538952 | tf_op jit(solution)/shard_map/ppermute | solution.py:792
  50.2 117.2 %collective-permute-start.3 = (bf16[576,1024]{1,0:T(8,128)(2,1)}, bf16[576,1024]{1,0:T(8,128)(2,1)}, u32[]{:S(2)}, u32[]{:S(2)}) collective-permute-start(bf16[576,1024]{1,0:T(8,128)(2,1)} %fusion.9.refs_0_), channel_id=1, source_target_pairs={{0,3},{1,2},{2,1},{3,0},{4,7},{5,6},{6,5},{7,4},{8,11},{9,10},{10,... | collective-permute-start | bytes 3538952 | tf_op jit(solution)/shard_map/ppermute | solution.py:792
  61.3 150.9 %all-to-all-start = ((bf16[8,128,512]{2,1,0:T(8,128)(2,1)}), bf16[8,128,512]{2,1,0:T(8,128)(2,1)S(1)}, u32[]{:S(2)}, u32[]{:S(2)}) async-start(bf16[8,128,512]{2,1,0:T(8,128)(2,1)} %copy.83), calls=%async_computation | async-start | bytes 2097152 | tf_op jit(solution)/shard_map/all_to_all | solution.py:859
  112.2 291.3 %all-gather.12.cloned.1.call-start = ((), (), s32[]{:S(2)}) async-start(), calls=%async_computation.8 | async-start | bytes 4718592 | tf_op jit(solution)/shard_map/all_gather | solution.py:872
  116.3 88.7 %collective-permute-start.4 = (bf16[576,1024]{1,0:T(8,128)(2,1)}, bf16[576,1024]{1,0:T(8,128)(2,1)}, u32[]{:S(2)}, u32[]{:S(2)}) collective-permute-start(bf16[576,1024]{1,0:T(8,128)(2,1)} %fusion.9.refs_0_), channel_id=1, source_target_pairs={{0,8},{1,9},{2,10},{3,11},{4,12},{5,13},{6,14},{7,15},{8,0},{9,1},... | collective-permute-start | bytes 3538952 | tf_op jit(solution)/shard_map/ppermute | solution.py:792
  116.7 95.4 %collective-permute-start.5 = (bf16[576,1024]{1,0:T(8,128)(2,1)}, bf16[576,1024]{1,0:T(8,128)(2,1)}, u32[]{:S(2)}, u32[]{:S(2)}) collective-permute-start(bf16[576,1024]{1,0:T(8,128)(2,1)} %collective-permute-done.1.refs_1_), channel_id=1, source_target_pairs={{0,8},{1,9},{2,10},{3,11},{4,12},{5,13},{6,14},{7,15},{8,0},{9,1},... | collective-permute-start | bytes 3538952 | tf_op jit(solution)/shard_map/ppermute | solution.py:792
  116.8 95.4 %collective-permute-start.6 = (bf16[576,1024]{1,0:T(8,128)(2,1)}, bf16[576,1024]{1,0:T(8,128)(2,1)}, u32[]{:S(2)}, u32[]{:S(2)}) collective-permute-start(bf16[576,1024]{1,0:T(8,128)(2,1)} %collective-permute-done.2.refs_2_), channel_id=1, source_target_pairs={{0,8},{1,9},{2,10},{3,11},{4,12},{5,13},{6,14},{7,15},{8,0},{9,1},... | collective-permute-start | bytes 3538952 | tf_op jit(solution)/shard_map/ppermute | solution.py:792
  167.3 44.9 %collective-permute-start.7 = (bf16[576,1024]{1,0:T(8,128)(2,1)}, bf16[576,1024]{1,0:T(8,128)(2,1)}, u32[]{:S(2)}, u32[]{:S(2)}) collective-permute-start(bf16[576,1024]{1,0:T(8,128)(2,1)} %collective-permute-done.3.refs_3_), channel_id=1, source_target_pairs={{0,8},{1,9},{2,10},{3,11},{4,12},{5,13},{6,14},{7,15},{8,0},{9,1},... | collective-permute-start | bytes 3538952 | tf_op jit(solution)/shard_map/ppermute | solution.py:792
  307.1 388.2 %reduce-scatter.11.cloned.1.call-start = ((), (), s32[]{:S(2)}) async-start(), calls=%async_computation.12 | async-start | bytes 3538944 | tf_op jit(solution)/shard_map/reduce_scatter | solution.py:811
  357.9 453.7 %reduce-scatter.9.cloned.1.call-start = ((), (), s32[]{:S(2)}) async-start(), calls=%async_computation.11 | async-start | bytes 3538944 | tf_op jit(solution)/shard_map/reduce_scatter | solution.py:811
  366.6 447.6 %reduce-scatter.7.cloned.1.call-start = ((), (), s32[]{:S(2)}) async-start(), calls=%async_computation.10 | async-start | bytes 3538944 | tf_op jit(solution)/shard_map/reduce_scatter | solution.py:811
  382.5 47.4 %collective-permute-start.22 = (bf16[576,1024]{1,0:T(8,128)(2,1)}, bf16[576,1024]{1,0:T(8,128)(2,1)}, u32[]{:S(2)}, u32[]{:S(2)}) collective-permute-start(bf16[576,1024]{1,0:T(8,128)(2,1)} %slice.186), channel_id=1, source_target_pairs={{0,8},{1,9},{2,10},{3,11},{4,12},{5,13},{6,14},{7,15},{8,0},{9,1},... | collective-permute-start | bytes 3538952 | tf_op jit(solution)/shard_map/ppermute | solution.py:792
  390.4 424.0 %reduce-scatter.5.cloned.1.call-start = ((), (), s32[]{:S(2)}) async-start(), calls=%async_computation.9 | async-start | bytes 2359296 | tf_op jit(solution)/shard_map/reduce_scatter | solution.py:811
  400.8 31.9 %collective-permute-start.18 = (bf16[576,1024]{1,0:T(8,128)(2,1)}, bf16[576,1024]{1,0:T(8,128)(2,1)}, u32[]{:S(2)}, u32[]{:S(2)}) collective-permute-start(bf16[576,1024]{1,0:T(8,128)(2,1)} %slice.187), channel_id=1, source_target_pairs={{0,8},{1,9},{2,10},{3,11},{4,12},{5,13},{6,14},{7,15},{8,0},{9,1},... | collective-permute-start | bytes 3538952 | tf_op jit(solution)/shard_map/ppermute | solution.py:792
  563.2 112.5 %all-to-all-start.1 = ((bf16[8,128,512]{2,1,0:T(8,128)(2,1)}), bf16[8,128,512]{2,1,0:T(8,128)(2,1)}, u32[]{:S(2)}, u32[]{:S(2)}) async-start(bf16[8,128,512]{2,1,0:T(8,128)(2,1)} %bitcast.29), calls=%async_computation.1 | async-start | bytes 2097152 | tf_op jit(solution)/shard_map/all_to_all | solution.py:954
  567.6 45.8 %collective-permute-start.33 = (bf16[1152,256]{1,0:T(8,128)(2,1)}, bf16[1152,256]{1,0:T(8,128)(2,1)S(1)}, u32[]{:S(2)}, u32[]{:S(2)}) collective-permute-start(bf16[1152,256]{1,0:T(8,128)(2,1)} %get-tuple-element.55), channel_id=1, source_target_pairs={{0,3},{1,2},{2,1},{3,0},{4,7},{5,6},{6,5},{7,4},{8,11},{9,10},{10,... | collective-permute-start | bytes 1769480 | tf_op jit(solution)/shard_map/ppermute | solution.py:792
  570.4 43.0 %collective-permute-start.34 = (bf16[1152,256]{1,0:T(8,128)(2,1)}, bf16[1152,256]{1,0:T(8,128)(2,1)S(1)}, u32[]{:S(2)}, u32[]{:S(2)}) collective-permute-start(bf16[1152,256]{1,0:T(8,128)(2,1)} %get-tuple-element.56), channel_id=1, source_target_pairs={{0,8},{1,9},{2,10},{3,11},{4,12},{5,13},{6,14},{7,15},{8,0},{9,1},... | collective-permute-start | bytes 1769480 | tf_op jit(solution)/shard_map/ppermute | solution.py:792
  570.5 43.0 %collective-permute-start.35 = (bf16[1152,256]{1,0:T(8,128)(2,1)}, bf16[1152,256]{1,0:T(8,128)(2,1)S(1)}, u32[]{:S(2)}, u32[]{:S(2)}) collective-permute-start(bf16[1152,256]{1,0:T(8,128)(2,1)} %get-tuple-element.57), channel_id=1, source_target_pairs={{0,9},{1,8},{2,11},{3,10},{4,13},{5,12},{6,15},{7,14},{8,1},{9,0},... | collective-permute-start | bytes 1769480 | tf_op jit(solution)/shard_map/ppermute | solution.py:792
  573.0 64.7 %collective-permute-start.36 = (bf16[1152,256]{1,0:T(8,128)(2,1)}, bf16[1152,256]{1,0:T(8,128)(2,1)S(1)}, u32[]{:S(2)}, u32[]{:S(2)}) collective-permute-start(bf16[1152,256]{1,0:T(8,128)(2,1)} %get-tuple-element.58), channel_id=1, source_target_pairs={{0,10},{1,11},{2,8},{3,9},{4,14},{5,15},{6,12},{7,13},{8,2},{9,3},... | collective-permute-start | bytes 1769480 | tf_op jit(solution)/shard_map/ppermute | solution.py:792
  581.4 73.0 %collective-permute-start.37 = (bf16[1152,256]{1,0:T(8,128)(2,1)}, bf16[1152,256]{1,0:T(8,128)(2,1)S(1)}, u32[]{:S(2)}, u32[]{:S(2)}) collective-permute-start(bf16[1152,256]{1,0:T(8,128)(2,1)} %get-tuple-element.59), channel_id=1, source_target_pairs={{0,11},{1,10},{2,9},{3,8},{4,15},{5,14},{6,13},{7,12},{8,3},{9,2},... | collective-permute-start | bytes 1769480 | tf_op jit(solution)/shard_map/ppermute | solution.py:792
  665.2 30.2 %collective-permute-start.19 = (bf16[576,1024]{1,0:T(8,128)(2,1)}, bf16[576,1024]{1,0:T(8,128)(2,1)}, u32[]{:S(2)}, u32[]{:S(2)}) collective-permute-start(bf16[576,1024]{1,0:T(8,128)(2,1)} %get-tuple-element.139), channel_id=1, source_target_pairs={{0,0},{1,1},{2,2},{3,3},{4,8},{5,9},{6,10},{7,11},{8,4},{9,5},{10,... | collective-permute-start | bytes 3538952 | tf_op jit(solution)/shard_map/ppermute | solution.py:792
  691.9 118.0 %collective-permute-start.39 = (bf16[576,1024]{1,0:T(8,128)(2,1)}, bf16[576,1024]{1,0:T(8,128)(2,1)S(1)}, u32[]{:S(2)}, u32[]{:S(2)}) collective-permute-start(bf16[576,1024]{1,0:T(8,128)(2,1)} %fusion.14), channel_id=1, source_target_pairs={{0,0},{1,1},{2,2},{3,3},{4,8},{5,9},{6,10},{7,11},{8,4},{9,5},{10,... | collective-permute-start | bytes 3538952 | tf_op jit(solution)/shard_map/ppermute | solution.py:792
  693.8 122.5 %collective-permute-start.41 = (bf16[8,128,512]{2,1,0:T(8,128)(2,1)}, bf16[8,128,512]{2,1,0:T(8,128)(2,1)S(1)}, u32[]{:S(2)}, u32[]{:S(2)}) collective-permute-start(bf16[8,128,512]{2,1,0:T(8,128)(2,1)} %collective-permute-done.40), channel_id=1, source_target_pairs={{0,16},{1,17},{2,18},{3,19},{4,20},{5,21},{6,22},{7,23},{8,24},{9,... | collective-permute-start | bytes 3145736 | tf_op jit(solution)/shard_map/ppermute | solution.py:792
  695.3 123.5 %collective-permute-start.49 = (bf16[192,1024]{1,0:T(8,128)(2,1)}, bf16[192,1024]{1,0:T(8,128)(2,1)}, u32[]{:S(2)}, u32[]{:S(2)}) collective-permute-start(bf16[192,1024]{1,0:T(8,128)(2,1)} %reduce-scatter.11.cloned.1.call-done), channel_id=1, source_target_pairs={{0,16},{1,17},{2,18},{3,19},{4,20},{5,21},{6,22},{7,23},{8,24},{9,... | collective-permute-start | bytes 1179656 | tf_op jit(solution)/shard_map/ppermute | solution.py:792
  (74 other events, 940.1 us)
Sparse Core Ops, SparseCore 0:
  10.2 85.3 all-gather.13
  97.6 91.1 all-gather.9
  191.4 64.7 all-gather.7
  258.3 69.0 all-gather.15
  329.8 73.6 all-gather.11
  406.9 83.3 reduce-scatter.10
  493.9 87.0 reduce-scatter.8
  584.5 139.8 reduce-scatter.6
  728.0 78.9 reduce-scatter.4

commit v2 on v0

--- a/solution.py
+++ b/solution.py
@@ -3,6 +3,8 @@
 import jax
 import jax.numpy as jnp
 from jax import lax
+from jax.experimental import pallas as pl
+from jax.experimental.pallas import tpu as pltpu
 from jax.sharding import PartitionSpec as P
 
 QUERY_HEADS = 16
@@ -437,9 +439,891 @@
     )
 
 
+f32 = jnp.float32
+bf16 = jnp.bfloat16
+AXES = ("grp", "ctx")
+N_GRP = 4
+N_CTX = 8
+SCALE = 1.0 / math.sqrt(HEAD_SIZE)
+EXP2_SCALE = math.log2(math.e) / math.sqrt(HEAD_SIZE)
+VMEM_LIMIT = 60 * 1024 * 1024
+RUN = 8 * BLK
+PROMPT_BLOCKS = PROMPT // BLK
+CONT_BLOCKS = CONT_LEN // BLK
+CHUNK = 5
+HELD = RUN + CONT_LEN
+
+
+def nt(a, b):
+    return lax.dot_general(a, b, (((1,), (1,)), ((), ())), preferred_element_type=f32)
+
+
+def nn(a, b):
+    return jnp.dot(a, b, preferred_element_type=f32)
+
+
+def tn(a, b):
+    return lax.dot_general(a, b, (((0,), (0,)), ((), ())), preferred_element_type=f32)
+
+
+def rows_at(start, size):
+    return pl.ds(pl.multiple_of(start, size), size)
+
+
+def turned(u):
+    return pltpu.roll(u, HEAD_SIZE // 2, 1)
+
+
+def head(i):
+    return slice(i * HEAD_SIZE, (i + 1) * HEAD_SIZE)
+
+
+def params():
+    return pltpu.CompilerParams(vmem_limit_bytes=VMEM_LIMIT)
+
+
+def whole_call(kernel, name, args, outs, scratch=()):
+    smem = pl.BlockSpec(memory_space=pltpu.SMEM)
+    vmem = pl.BlockSpec(memory_space=pltpu.VMEM)
+    return pl.pallas_call(
+        kernel,
+        in_specs=[smem if a.dtype == jnp.int32 else vmem for a in args],
+        out_specs=[vmem] * len(outs),
+        out_shape=[jax.ShapeDtypeStruct(s, t) for s, t in outs],
+        scratch_shapes=list(scratch),
+        compiler_params=params(),
+        name=name,
+    )(*args)
+
+
+def deal_kernel(table, rows_ref, *outs):
+    for e in range(8):
+        for i in range(CHUNK):
+            outs[e][i * BLK : (i + 1) * BLK, :] = rows_ref[rows_at(table[e, i] * BLK, BLK), :]
+
+
+def deal(table, rows):
+    shape = (CHUNK * BLK, rows.shape[1])
+    return whole_call(deal_kernel, "deal_rows", (table, rows), [(shape, rows.dtype)] * 8)
+
+
+def deal_all_kernel(table, rows_ref, out_ref):
+    for e in range(8):
+        for i in range(CHUNK):
+            out_ref[e, i * BLK : (i + 1) * BLK, :] = rows_ref[rows_at(table[e, i] * BLK, BLK), :]
+
+
+def deal_all(table, rows):
+    shape = (8, CHUNK * BLK, rows.shape[1])
+    return whole_call(deal_all_kernel, "deal_all", (table, rows), [(shape, rows.dtype)])[0]
+
+
+def place_all_kernel(table, pieces, out_ref, held):
+    for e in range(8):
+        for i in range(CHUNK):
+            held[rows_at(table[e, i] * BLK, BLK), :] = pieces[e, i * BLK : (i + 1) * BLK, :]
+    out_ref[...] = held[: out_ref.shape[0], :].astype(out_ref.dtype)
+
+
+def place_all(table, pieces, n_rows, kind):
+    shape = (n_rows, pieces.shape[2])
+    return whole_call(
+        place_all_kernel,
+        "place_all",
+        (table, pieces),
+        [(shape, kind)],
+        [pltpu.VMEM((n_rows + BLK, shape[1]), pieces.dtype)],
+    )[0]
+
+
+def place_kernel(table, *refs):
+    pieces, out_ref, held = refs[:8], refs[8], refs[-1]
+    for e in range(8):
+        for i in range(CHUNK):
+            held[rows_at(table[e, i] * BLK, BLK), :] = pieces[e][i * BLK : (i + 1) * BLK, :]
+    out_ref[...] = held[: out_ref.shape[0], :].astype(out_ref.dtype)
+
+
+def place(table, pieces, n_rows, kind):
+    shape = (n_rows, pieces[0].shape[1])
+    return whole_call(
+        place_kernel,
+        "place_rows",
+        (table, *pieces),
+        [(shape, kind)],
+        [pltpu.VMEM((n_rows + BLK, shape[1]), pieces[0].dtype)],
+    )[0]
+
+
+def place_norm_kernel(table, *refs):
+    gain_ref, out_ref, low_ref, held = refs[8:]
+    place_kernel(table, *refs[:8], out_ref, held)
+    normed, _ = normed_parts(out_ref[...].astype(f32))
+    low_ref[...] = (normed * gain_ref[...]).astype(bf16)
+
+
+def place_norm(table, pieces, gain, n_rows):
+    shape = (n_rows, pieces[0].shape[1])
+    return whole_call(
+        place_norm_kernel,
+        "place_rows_norm",
+        (table, *pieces, gain),
+        [(shape, bf16), (shape, bf16)],
+        [pltpu.VMEM((n_rows + BLK, shape[1]), bf16)],
+    )
+
+
+def gathered_rows(info, pieces, w_ref):
+    for e in range(8):
+        w_ref[rows_at((info[0] ^ e) * 128, 128), :] = pieces[e][...]
+
+
+def lane_mean(u):
+    ones = jnp.full((HEAD_SIZE, HEAD_SIZE), 1.0 / HEAD_SIZE, bf16)
+    high = u.astype(bf16)
+    return nn(high, ones) + nn((u - high.astype(f32)).astype(bf16), ones)
+
+
+def head_normed(u):
+    inverse = lax.rsqrt(lane_mean(u * u) + eps)
+    return u * inverse, inverse
+
+
+def query_kernel(info, h_ref, *refs):
+    gain_ref, cos_ref, sin_ref, q_ref, raw_ref, w_ref = refs[8:]
+    gathered_rows(info, refs[:8], w_ref)
+    acc = nn(h_ref[...], w_ref[...])
+    raw_ref[...] = acc
+    for i in range(2):
+        normed, _ = head_normed(acc[:, head(i)])
+        u = normed * gain_ref[...]
+        q_ref[:, head(i)] = (u * cos_ref[...] + turned(u) * sin_ref[...]).astype(bf16)
+
+
+def key_value_kernel(info, h_ref, *refs):
+    gain_ref, cos_ref, sin_ref, kv_ref, raw_ref, w_ref, send_ref = refs[8:]
+    gathered_rows(info, refs[:8], w_ref)
+    acc = nn(h_ref[...], w_ref[...])
+    raw_ref[...] = acc[:, head(0)]
+    normed, _ = head_normed(acc[:, head(0)])
+    u = normed * gain_ref[...]
+    kv_ref[:, head(0)] = (u * cos_ref[...] + turned(u) * sin_ref[...]).astype(bf16)
+    kv_ref[:, head(1)] = acc[:, head(1)].astype(bf16)
+    for b in range(2):
+        send_ref[b * RUN : (b + 1) * RUN, :] = kv_ref[b * HELD : b * HELD + RUN, :]
+
+
+def project(kernel, name, info, hidden, pieces, first, gain, cos, sin, raw_width, extra):
+    rows, width = hidden.shape
+
+    def still(g, s):
+        return (0, 0)
+
+    def moving(g, s):
+        return (0, g)
+
+    return pl.pallas_call(
+        kernel,
+        grid_spec=pltpu.PrefetchScalarGridSpec(
+            num_scalar_prefetch=1,
+            grid=(4,),
+            in_specs=[pl.BlockSpec((rows, width), still)]
+            + [pl.BlockSpec((128, 256), lambda g, s: (0, g + first))] * 8
+            + [
+                pl.BlockSpec((1, HEAD_SIZE), still),
+                pl.BlockSpec((rows, HEAD_SIZE), still),
+                pl.BlockSpec((rows, HEAD_SIZE), still),
+            ],
+            out_specs=[
+                pl.BlockSpec((rows, 256), moving),
+                pl.BlockSpec((rows, raw_width), moving),
+                pl.BlockSpec((width, 256), moving),
+            ]
+            + [pl.BlockSpec((2 * RUN, 256), moving)] * extra,
+        ),
+        out_shape=[
+            jax.ShapeDtypeStruct((rows, 1024), bf16),
+            jax.ShapeDtypeStruct((rows, 4 * raw_width), f32),
+            jax.ShapeDtypeStruct((width, 1024), bf16),
+        ]
+        + [jax.ShapeDtypeStruct((2 * RUN, 1024), bf16)] * extra,
+        compiler_params=params(),
+        name=name,
+    )(info, hidden, *pieces, gain, cos, sin)
+
+
+def seen_in_prompt(info, half):
+    key = lax.broadcasted_iota(jnp.int32, (PROMPT, RUN), 0)
+    tile = key // RUN
+    run = info[3] ^ (tile // 2 + 4 * (tile % 2))
+    row = lax.broadcasted_iota(jnp.int32, (PROMPT, RUN), 1) + (info[3] ^ (4 * half)) * RUN
+    return run * RUN + key % RUN <= row
+
+
+def seen_in_own():
+    key = lax.broadcasted_iota(jnp.int32, (CONT_LEN, CONT_LEN), 0)
+    row = lax.broadcasted_iota(jnp.int32, (CONT_LEN, CONT_LEN), 1)
+    return key <= row
+
+
+LSE_SPAN = 640
+
+
+def units():
+    for b in range(2):
+        yield b, b * HELD + RUN, CONT_LEN, b * LSE_SPAN, False
+    for b in range(2):
+        yield b, b * HELD, RUN, b * LSE_SPAN + 512, True
+
+
+def attn_fwd_kernel(info, q_ref, kv_ref, p0, p1, p2, p3, o_ref, lse_ref, p_ref):
+    for t, p in enumerate((p0, p1, p2, p3)):
+        p_ref[t * 2 * RUN : (t + 1) * 2 * RUN, :] = p[...]
+    prompt = (p_ref[:, head(0)], jnp.transpose(p_ref[:, head(1)]))
+    for b, row0, n, lane, in_prompt in units():
+        own = slice(row0, row0 + n)
+        tiles = [(*prompt, seen_in_prompt(info, b) if in_prompt else None)]
+        if not in_prompt:
+            tiles.append((kv_ref[own, head(0)], jnp.transpose(kv_ref[own, head(1)]), seen_in_own()))
+        for i in range(2):
+            q = q_ref[own, head(i)]
+            total = jnp.zeros((1, n), f32)
+            mixed = jnp.zeros((HEAD_SIZE, n), f32)
+            for keys, values_t, seen in tiles:
+                p = jnp.exp2(nt(keys, q) * EXP2_SCALE)
+                if seen is not None:
+                    p = jnp.where(seen, p, 0.0)
+                total = total + jnp.sum(p, axis=0, keepdims=True)
+                mixed = mixed + nn(values_t, p.astype(bf16))
+            o_ref[own, head(i)] = jnp.transpose(mixed / total).astype(bf16)
+            lse_ref[0, i : i + 1, lane : lane + n] = jnp.log2(total)
+
+
+def attn_specs(rows, *names):
+    specs = {
+        "wide": pl.BlockSpec((rows, 256), lambda g, s: (0, g)),
+        "head": pl.BlockSpec((rows, HEAD_SIZE), lambda g, s: (0, g)),
+        "prompt": pl.BlockSpec((2 * RUN, 256), lambda g, s: (0, g)),
+        "lse": pl.BlockSpec((1, 8, 2 * LSE_SPAN), lambda g, s: (g, 0, 0)),
+        "table": pl.BlockSpec((rows, HEAD_SIZE), lambda g, s: (0, 0)),
+        "gain": pl.BlockSpec((1, HEAD_SIZE), lambda g, s: (0, 0)),
+        "gains": pl.BlockSpec((8, HEAD_SIZE), lambda g, s: (0, 0)),
+    }
+    return [specs[n] for n in names]
+
+
+def attn_fwd(info, q, kv, prompt):
+    rows = q.shape[0]
+    return pl.pallas_call(
+        attn_fwd_kernel,
+        grid_spec=pltpu.PrefetchScalarGridSpec(
+            num_scalar_prefetch=1,
+            grid=(4,),
+            in_specs=attn_specs(rows, "wide", "wide", *["prompt"] * 4),
+            out_specs=attn_specs(rows, "wide", "lse"),
+            scratch_shapes=[pltpu.VMEM((PROMPT, 256), bf16)],
+        ),
+        out_shape=[
+            jax.ShapeDtypeStruct((rows, 1024), bf16),
+            jax.ShapeDtypeStruct((4, 8, 2 * LSE_SPAN), f32),
+        ],
+        compiler_params=params(),
+        cost_estimate=pl.CostEstimate(flops=20*10**9, bytes_accessed=10**7, transcendentals=0),
+        name="attn_fwd",
+    )(info, q, kv, *prompt)
+
+
+def key_back(grad, raw, cos, sin, gain):
+    normed, inverse = normed_parts(raw)
+    grad = grad * SCALE
+    back = grad * cos - turned(grad) * sin
+    part = jnp.sum(back * normed, axis=0, keepdims=True)
+    return norm_back(back * gain, normed, inverse).astype(bf16), part
+
+
+def attn_bwd_kernel(info, q_ref, kv_ref, p0, p1, p2, p3, *refs):
+    do_ref, o_ref, lse_ref, rawq_ref, rawk_ref, qg_ref, kg_ref, cos_ref, sin_ref = refs[:9]
+    dq_ref, dkv_ref, d0, d1, d2, d3, gains_ref, dk_ref, dv_ref, p_ref = refs[9:]
+    for t, p in enumerate((p0, p1, p2, p3)):
+        p_ref[t * 2 * RUN : (t + 1) * 2 * RUN, :] = p[...]
+    prompt = (p_ref[:, head(0)], jnp.transpose(p_ref[:, head(0)]), p_ref[:, head(1)])
+
+    @pl.when(pl.program_id(0) == 0)
+    def first():
+        gains_ref[...] = jnp.zeros_like(gains_ref)
+
+    for number, (b, row0, n, lane, in_prompt) in enumerate(units()):
+        own = slice(row0, row0 + n)
+        cos, sin = cos_ref[own, :], sin_ref[own, :]
+        tiles = [(*prompt, seen_in_prompt(info, b) if in_prompt else None, True)]
+        if not in_prompt:
+            keys = kv_ref[own, head(0)]
+            tiles.append((keys, jnp.transpose(keys), kv_ref[own, head(1)], seen_in_own(), False))
+        own_dk = own_dv = 0.0
+        for i in range(2):
+            q, do = q_ref[own, head(i)], do_ref[own, head(i)]
+            lse = lse_ref[0, i : i + 1, lane : lane + n]
+            product = do.astype(f32) * o_ref[own, head(i)].astype(f32)
+            delta = jnp.sum(jnp.transpose(product), axis=0, keepdims=True)
+            dq = jnp.zeros((HEAD_SIZE, n), f32)
+            for keys, keys_t, values, seen, shared in tiles:
+                p = jnp.exp2(nt(keys, q) * EXP2_SCALE - lse)
+                if seen is not None:
+                    p = jnp.where(seen, p, 0.0)
+                ds = (p * (nt(values, do) - delta)).astype(bf16)
+                dk, dv = nn(ds, q), nn(p.astype(bf16), do)
+                dq = dq + nn(keys_t, ds)
+                if not shared:
+                    own_dk, own_dv = own_dk + dk, own_dv + dv
+                elif number == 0 and i == 0:
+                    dk_ref[...] = dk
+                    dv_ref[...] = dv
+                else:
+                    dk_ref[...] += dk
+                    dv_ref[...] += dv
+            back, part = key_back(jnp.transpose(dq), rawq_ref[own, head(i)], cos, sin, qg_ref[...])
+            dq_ref[own, head(i)] = back
+            gains_ref[0:1, :] += part
+        if not in_prompt:
+            back, part = key_back(own_dk, rawk_ref[own, :], cos, sin, kg_ref[...])
+            dkv_ref[own, head(0)] = back
+            dkv_ref[own, head(1)] = own_dv.astype(bf16)
+            gains_ref[1:2, :] += part
+        else:
+            dkv_ref[own, :] = jnp.zeros((n, 256), bf16)
+    for t, ref in enumerate((d0, d1, d2, d3)):
+        ref[:, head(0)] = dk_ref[t * 256 : (t + 1) * 256, :].astype(bf16)
+        ref[:, head(1)] = dv_ref[t * 256 : (t + 1) * 256, :].astype(bf16)
+
+
+def attn_bwd(info, q, kv, prompt, do, o, lse, rawq, rawk, qg, kg, cos, sin):
+    rows = q.shape[0]
+    return pl.pallas_call(
+        attn_bwd_kernel,
+        grid_spec=pltpu.PrefetchScalarGridSpec(
+            num_scalar_prefetch=1,
+            grid=(4,),
+            in_specs=attn_specs(rows, "wide", "wide", *["prompt"] * 4, "wide", "wide", "lse")
+            + attn_specs(rows, "wide", "head", "gain", "gain", "table", "table"),
+            out_specs=attn_specs(rows, "wide", "wide", *["prompt"] * 4, "gains"),
+            scratch_shapes=[pltpu.VMEM((PROMPT, HEAD_SIZE), f32)] * 2
+            + [pltpu.VMEM((PROMPT, 256), bf16)],
+        ),
+        out_shape=[jax.ShapeDtypeStruct((rows, 1024), bf16)] * 2
+        + [jax.ShapeDtypeStruct((2 * RUN, 1024), bf16)] * 4
+        + [jax.ShapeDtypeStruct((8, HEAD_SIZE), f32)],
+        compiler_params=params(),
+        cost_estimate=pl.CostEstimate(flops=45*10**9, bytes_accessed=10**7, transcendentals=0),
+        name="attn_bwd",
+    )(info, q, kv, *prompt, do, o, lse, rawq, rawk, qg, kg, cos, sin)
+
+
+def prompt_back_kernel(d0, d1, d2, d3, dkv_ref, raw_ref, kg_ref, cos_ref, sin_ref, out_ref, gains_ref):
+    out_ref[...] = dkv_ref[...]
+    gains_ref[...] = jnp.zeros_like(gains_ref)
+    for b in range(2):
+        rows = slice(b * RUN, (b + 1) * RUN)
+        own = slice(b * HELD, b * HELD + RUN)
+        for h in range(4):
+            cols = slice(h * 256, (h + 1) * 256)
+            total = sum(d[rows, cols].astype(f32) for d in (d0, d1, d2, d3))
+            back, part = key_back(
+                total[:, head(0)], raw_ref[own, head(h)], cos_ref[own, :], sin_ref[own, :], kg_ref[...]
+            )
+            out_ref[own, h * 256 : h * 256 + 128] = back
+            out_ref[own, h * 256 + 128 : (h + 1) * 256] = total[:, head(1)].astype(bf16)
+            gains_ref[0:1, :] += part
+
+
+def out_kernel(info, o_ref, *refs):
+    pieces, (own_ref, sib_ref, w_ref) = refs[:2], refs[2:]
+    for t in range(4):
+        w_ref[rows_at((info[4] ^ t) * 256, 256), :] = pieces[t % 2][t // 2]
+    half = own_ref.shape[0]
+    own_ref[...] = nn(o_ref[:half, :], w_ref[...])
+    sib_ref[...] = nn(o_ref[half:, :], w_ref[...]).astype(bf16)
+
+
+def mlp_kernel(info, h_ref, g_ref, *refs):
+    w2, w3 = refs[:10], refs[10:14]
+    hid_ref, dgu_ref, out_ref, outs_ref, dh_ref, dhs_ref = refs[14:20]
+    w_ref, wd_ref, out_acc, dh_acc = refs[20:]
+    step = pl.program_id(0)
+    width = h_ref.shape[1]
+    ff = hid_ref.shape[1]
+    half = out_ref.shape[0]
+    for e in range(8):
+        row = (info[0] ^ e) * 128
+        w_ref[rows_at(row + info[1] * 64, 64), :] = w2[e][...]
+        w_ref[rows_at(row + (1 - info[1]) * 64, 64), :] = w2[8 + e // 4][e % 4]
+    for t in range(4):
+
+        @pl.when(step == t)
+        def take(t=t):
+            wd_ref[...] = w3[t][...]
+
+    @pl.when(step == 0)
+    def zero():
+        for ref in (out_ref, dh_ref, out_acc, dh_acc):
+            ref[...] = jnp.zeros_like(ref)
+
+    for b, out, dh in ((0, out_ref, dh_ref), (1, out_acc, dh_acc)):
+        rows = slice(b * half, (b + 1) * half)
+        both = nn(h_ref[rows, :], w_ref[...])
+        gate, up = both[:, :ff], both[:, ff:]
+        sig = jax.nn.sigmoid(gate)
+        silu = gate * sig
+        hid = (silu * up).astype(bf16)
+        hid_ref[rows, :] = hid
+        dhid = nt(g_ref[rows, :], wd_ref[...])
+        dgu_ref[rows, :ff] = (dhid * up * sig * (1.0 + gate * (1.0 - sig))).astype(bf16)
+        dgu_ref[rows, ff:] = (dhid * silu).astype(bf16)
+        dh[...] += nt(dgu_ref[rows, :], w_ref[...])
+        out[...] += nn(hid, wd_ref[...])
+
+    @pl.when(step == 3)
+    def finish():
+        outs_ref[...] = out_acc[...].astype(bf16)
+        dhs_ref[...] = dh_acc[...].astype(bf16)
+
+
+def mlp(info, hidden, grad, w2, w3, ff):
+    rows, width = hidden.shape
+    half = rows // 2
+    once = pl.Buffered(1)
+
+    def still(shape):
+        return pl.BlockSpec(shape, lambda g, s: (0, 0), pipeline_mode=once)
+
+    return pl.pallas_call(
+        mlp_kernel,
+        grid_spec=pltpu.PrefetchScalarGridSpec(
+            num_scalar_prefetch=1,
+            grid=(4,),
+            in_specs=[still((rows, width))] * 2
+            + [pl.BlockSpec((64, 2 * ff), lambda g, s: (0, s[4] ^ g))] * 8
+            + [pl.BlockSpec((4, 64, 2 * ff), lambda g, s: (0, 0, s[4] ^ g))] * 2
+            + [still(w3[0].shape)] * 4,
+            out_specs=[
+                pl.BlockSpec((rows, ff), lambda g, s: (0, s[4] ^ g)),
+                pl.BlockSpec((rows, 2 * ff), lambda g, s: (0, s[4] ^ g)),
+            ]
+            + [pl.BlockSpec((half, width), lambda g, s: (0, 0))] * 4,
+            scratch_shapes=[
+                pltpu.VMEM((width, 2 * ff), bf16),
+                pltpu.VMEM((ff, width), bf16),
+                pltpu.VMEM((half, width), f32),
+                pltpu.VMEM((half, width), f32),
+            ],
+        ),
+        out_shape=[
+            jax.ShapeDtypeStruct((rows, 4 * ff), bf16),
+            jax.ShapeDtypeStruct((rows, 8 * ff), bf16),
+            jax.ShapeDtypeStruct((half, width), f32),
+            jax.ShapeDtypeStruct((half, width), bf16),
+            jax.ShapeDtypeStruct((half, width), f32),
+            jax.ShapeDtypeStruct((half, width), bf16),
+        ],
+        compiler_params=params(),
+        cost_estimate=pl.CostEstimate(flops=38*10**9, bytes_accessed=10**7, transcendentals=0),
+        name="feed_forward",
+    )(info, hidden, grad, *w2, *w3)
+
+
+def device_of(y, core, z_hi, z_lo, x):
+    return (y * 2 + core) * N_CTX + z_hi * 4 + z_lo * 2 + x
+
+
+def bits_of(i):
+    return ((i >> 4) & 1, (i >> 3) & 1, (i >> 2) & 1, (i >> 1) & 1, i & 1)
+
+
+def permutation(target, sends=lambda *bits: True):
+    devices = range(N_GRP * N_CTX)
+    return [(i, device_of(*target(*bits_of(i)))) for i in devices if sends(*bits_of(i))]
+
+
+def member_device(e):
+    def target(y, core, z_hi, z_lo, x):
+        m = (z_hi * 4 + z_lo * 2 + x) ^ e
+        return (y, m >> 2, core, (m >> 1) & 1, m & 1)
+
+    return target
+
+
+SPREAD = [permutation(member_device(e)) for e in range(8)]
+COLLECT = [[(b, a) for a, b in pairs] for pairs in SPREAD]
+HALVES = permutation(
+    lambda y, core, z_hi, z_lo, x: (y, z_hi, core, z_lo, x),
+    lambda y, core, z_hi, z_lo, x: z_hi != core,
+)
+CUBES = [
+    [device_of(y, m >> 2, z_hi, (m >> 1) & 1, m & 1) for m in range(8)]
+    for y in range(2)
+    for z_hi in range(2)
+]
+OVER_Y = permutation(lambda y, core, z_hi, z_lo, x: (1 - y, core, z_hi, z_lo, x))
+SIBLING = permutation(lambda y, core, z_hi, z_lo, x: (y, 1 - core, z_hi, z_lo, x))
+MIDDLE = permutation(lambda y, core, z_hi, z_lo, x: (y, core, 1 - z_hi, z_lo, x))
+MIDDLE_OUT = permutation(
+    lambda y, core, z_hi, z_lo, x: (y, core, 1 - z_hi, z_lo, x),
+    lambda y, core, z_hi, z_lo, x: z_hi == core,
+)
+MIDDLE_IN = permutation(
+    lambda y, core, z_hi, z_lo, x: (y, core, 1 - z_hi, z_lo, x),
+    lambda y, core, z_hi, z_lo, x: z_hi != core,
+)
+CHIP = [
+    permutation(
+        lambda y, core, z_hi, z_lo, x, t=t: (y, core, z_hi, z_lo ^ (t >> 1), x ^ (t & 1))
+    )
+    for t in range(4)
+]
+
+
+def permute(a, pairs):
+    return lax.ppermute(a, AXES, pairs)
+
+
+def pick(a, i, axis=0):
+    return lax.dynamic_index_in_dim(a, i, axis, keepdims=False)
+
+
+def added(*terms):
+    return sum(t.astype(f32) for t in terms).astype(bf16)
+
+
+def after(a, b):
+    return lax.optimization_barrier((a, b))[0]
+
+
+def together(*arrays):
+    return lax.optimization_barrier(arrays)
+
+
+def in_order(first, mine, other):
+    return [jnp.where(first, mine, other), jnp.where(first, other, mine)]
+
+
+def shards_split(
+    tokens,
+    block_table,
+    norm1_gain,
+    w_query,
+    key_weight,
+    value_weight,
+    query_gain,
+    key_norm_gain,
+    w_out,
+    norm2_gain,
+    w_gate,
+    w_up,
+    w_down,
+    out_grad,
+):
+    row_total, width = tokens.shape
+    n_slots = row_total // BLK
+    ff = w_gate.shape[1] // 8
+    position = lax.axis_index("ctx").astype(jnp.int32)
+    group_index = lax.axis_index("grp").astype(jnp.int32)
+    y, core = group_index // 2, group_index % 2
+    z_hi, chip = position // 4, position % 4
+    z_lo, x = chip // 2, chip % 2
+    member = core * 4 + chip
+    info = jnp.stack([position, y, core, member, chip])
+    at_home = z_hi == core
+    qg, kg = query_gain.reshape(1, HEAD_SIZE), key_norm_gain.reshape(1, HEAD_SIZE)
+
+    eight = jnp.arange(8, dtype=jnp.int32)
+    five = jnp.arange(CHUNK, dtype=jnp.int32)[None, :]
+
+    def slots_of(m):
+        m = m.reshape(-1, 1)
+        return jnp.where(five == 0, m, 7 + 7 * (m // 2) + 3 * (m % 2) + five)
+
+    def held_at(natural, m):
+        inside = natural - (PROMPT_BLOCKS + CONT_BLOCKS * m)
+        valid = (five == 0) | ((inside >= 0) & (inside < CONT_BLOCKS))
+        return jnp.where(valid, jnp.where(five == 0, natural - 8 * m, 8 + inside), n_slots), valid
+
+    def look_up(rows, slots):
+        match = slots[:, :, None] == jnp.arange(n_slots, dtype=jnp.int32)
+        return jnp.sum(jnp.where(match, rows[:, None, :], 0), axis=2)
+
+    tables = block_table.reshape(8, n_slots)
+    send_slots = slots_of(position ^ eight)
+    from_tables = jnp.concatenate(
+        [lax.dynamic_slice_in_dim(tables, member ^ e, 1, 0) for e in range(8)], axis=0
+    )
+    arrive, _ = held_at(look_up(from_tables, jnp.broadcast_to(slots_of(member), (8, CHUNK))), member)
+    leave = jnp.minimum(arrive, n_slots - 1)
+    own_table = lax.dynamic_slice_in_dim(tables, position, 1, 0)
+    _, valid = held_at(look_up(own_table, send_slots), (position ^ eight).reshape(-1, 1))
+    home_slots = jnp.where(valid, send_slots, n_slots)
+
+    def spread(a):
+        return [permute(c, pairs) for c, pairs in zip(deal(send_slots, a), SPREAD)]
+
+    def collect(a, kind):
+        pieces = [permute(c, pairs) for c, pairs in zip(deal(leave, a), COLLECT)]
+        return place(home_slots, pieces, row_total, kind)
+
+    def regrouped(a):
+        return jnp.where(at_home, a, permute(a, HALVES))
+
+    def both(a):
+        return jnp.concatenate([a, permute(a, SIBLING)], axis=0)
+
+    def columns(w, parts):
+        return pick(w.reshape(w.shape[0], 2, 4, -1), core, 1)
+
+    own_one = jnp.concatenate(
+        [
+            columns(w_query, 2).reshape(-1, 1024),
+            jnp.concatenate([columns(key_weight, 2), columns(value_weight, 2)], axis=2).reshape(
+                -1, 1024
+            ),
+        ],
+        axis=1,
+    )
+    own_two = jnp.concatenate([columns(w_gate, 2), columns(w_up, 2)], axis=2)
+    own_two = pick(own_two.reshape(2, 64, 8 * ff), y)
+    own_out, own_down = w_out, w_down
+
+    def around(a):
+        return [a] + [permute(a, CHIP[t]) for t in range(1, 4)]
+
+    one = around(own_one)
+    middle_one = permute(own_one, MIDDLE)
+    arrived = spread(tokens)
+    one = one + around(middle_one)
+
+    cosine, sine = rotation(jnp.arange(PROMPT + CONT_LEN, dtype=jnp.int32))
+    cos = jnp.concatenate([cosine[:, 0], cosine[:, 0]], axis=1)
+    sin = jnp.concatenate([-sine[:, 0], sine[:, 0]], axis=1)
+
+    def of_rows(table):
+        parts = []
+        for m in (member, member ^ 4):
+            parts += [lax.dynamic_slice_in_dim(table, m * RUN, RUN, 0), table[PROMPT:]]
+        return jnp.concatenate(parts, axis=0)
+
+    cos, sin = of_rows(cos), of_rows(sin)
+
+    inputs_low, first_low = place_norm(arrive, arrived, norm1_gain.reshape(1, width), row_total)
+    hidden_one = both(first_low)
+    own_two, own_three, out_grad = together(
+        own_two, jnp.concatenate([w_down, w_out], axis=0), out_grad, first_low
+    )[:3]
+    middle_three = permute(own_three, MIDDLE_OUT)
+    hidden_one, middle_three, own_two, out_grad, *one = together(
+        hidden_one, middle_three, own_two, out_grad, *one
+    )
+    home_three = jnp.where(at_home, own_three, middle_three)
+    home_down, home_out = home_three[: 3 * RUN], home_three[3 * RUN :]
+
+    two = around(own_two)
+    middle_two = permute(own_two, MIDDLE)
+    kv, rawk, w_kv, prompt_kv = project(
+        key_value_kernel, "key_value", info, hidden_one, one, 4, kg, cos, sin, HEAD_SIZE, 1
+    )
+    prompt_kv, home_out, out_grad, hidden_q, middle_two, *two = together(
+        prompt_kv, home_out, out_grad, hidden_one, middle_two, *two
+    )
+
+    prompt = around(prompt_kv)
+    outs = jnp.stack([home_out, permute(home_out, CHIP[2])])
+    grad_here = regrouped(out_grad)
+    q, rawq, w_q = project(query_kernel, "query", info, hidden_q, one, 0, qg, cos, sin, 256, 0)
+    q, outs, grad_here, middle_two, home_down, *prompt = together(
+        q, outs, grad_here, middle_two, home_down, *prompt
+    )
+
+    two += around(middle_two)
+    other_two = [permute(jnp.stack(two[:4]), OVER_Y)]
+    outs = [outs, permute(outs, CHIP[1])]
+    mixed, lse = attn_fwd(info, q, kv, prompt)
+    mixed, home_down, grad_here, *rest = together(mixed, home_down, grad_here, *two, *outs, *other_two)
+    two, outs, other_two = rest[:8], rest[8:10], rest[10:]
+
+    other_two.append(permute(jnp.stack(two[4:]), OVER_Y))
+    downs = around(home_down)
+    chunk_starts = [8 + 7 * (m // 2) + 3 * (m % 2) for m in range(8)]
+    grad_here = jnp.concatenate(
+        [
+            grad_here[: 8 * BLK].reshape(8, BLK, width),
+            jnp.stack([grad_here[start * BLK : (start + 4) * BLK] for start in chunk_starts]),
+        ],
+        axis=1,
+    )
+
+    def swap_cube(a):
+        return lax.all_to_all(a, AXES, 0, 0, tiled=True, axis_index_groups=CUBES)
+
+    grad_here = swap_cube(grad_here)
+    in_turn = jnp.concatenate(
+        [lax.dynamic_slice_in_dim(arrive, member ^ e, 1, 0) for e in range(8)], axis=0
+    )
+    leave_in_turn = jnp.minimum(in_turn, n_slots - 1)
+    home_in_turn = jnp.concatenate(
+        [lax.dynamic_slice_in_dim(home_slots, position ^ e, 1, 0) for e in range(8)], axis=0
+    )
+
+    rows_kind = ((row_total, width), f32), ((row_total, width), bf16)
+    out_own, out_sib, w_o = whole_call(
+        out_kernel,
+        "out_projection",
+        (info, mixed, *outs),
+        [*rows_kind, ((1024, width), bf16)],
+    )
+    inputs = inputs_low.astype(f32)
+    resid_one = inputs + out_own + permute(out_sib, SIBLING).astype(f32)
+    normed_two, inverse_two = normed_parts(resid_one)
+    hidden_two = (normed_two * norm2_gain).astype(bf16)
+    hidden_two, other_far, *downs = together(hidden_two, other_two[1], *downs)
+    other_two = [other_two[0], other_far]
+    hidden_two = both(hidden_two)
+    grad_low = place_all(in_turn, grad_here, row_total, bf16)
+    grad_both = both(grad_low)
+    hid, grad_gu, ff_own, ff_sib, back_own, back_sib = mlp(
+        info, hidden_two, grad_both, two + other_two, downs, ff
+    )
+    grad_two = back_own + permute(back_sib, SIBLING).astype(f32)
+    gain_two_part = jnp.sum(grad_two * normed_two, axis=0)
+    grad_resid = grad_low.astype(f32) + norm_back(grad_two * norm2_gain, normed_two, inverse_two)
+    grad_attn = both(grad_resid.astype(bf16))
+
+    def chip_parts(grad):
+        grad = grad.reshape(8, -1, grad.shape[-1])
+        return [
+            jnp.stack([pick(grad, position ^ t), pick(grad, position ^ (4 + t))]) for t in range(4)
+        ]
+
+    def sent_to_chips(parts):
+        return [permute(parts[t], CHIP[t]) for t in range(1, 4)]
+
+    def from_middle(part):
+        return added(pick(part, z_hi), permute(pick(part, 1 - z_hi), MIDDLE))
+
+    def halved(grad, axis, bit, pairs):
+        return added(pick(grad, bit, axis), permute(pick(grad, 1 - bit, axis), pairs))
+
+    grad_two_w = tn(hidden_two, grad_gu).astype(bf16).reshape(2, 2, 2, 2, 64, -1)
+    keep_two, send_two = pick(grad_two_w, y, 3), pick(grad_two_w, 1 - y, 3)
+    send_two = permute(send_two, OVER_Y)
+    grad_down = tn(hid, grad_both).astype(bf16).reshape(2, 2, -1, width)
+    grad_out = tn(mixed, grad_attn).astype(bf16).reshape(2, 2, -1, width)
+    outcome = resid_one + ff_own + permute(ff_sib, SIBLING).astype(f32)
+    leaving = deal_all(leave_in_turn, outcome.astype(bf16))
+    grad_attn, grad_down, grad_out, leaving, _ = together(
+        grad_attn, grad_down, grad_out, leaving, keep_two
+    )
+    keep_down, send_down = pick(grad_down, x, 1), permute(pick(grad_down, 1 - x, 1), CHIP[1])
+    keep_out, send_out = pick(grad_out, z_lo), permute(pick(grad_out, 1 - z_lo), CHIP[2])
+    leaving = swap_cube(leaving)
+    grad_mixed = nt(grad_attn, w_o).astype(bf16)
+    grad_q, grad_kv, *prompt_parts, gains = attn_bwd(
+        info, q, kv, prompt, grad_mixed, mixed, lse, rawq, rawk, qg, kg, cos, sin
+    )
+    grad_q, grad_kv, send_down, send_out, leaving, *prompt_parts = together(
+        grad_q, grad_kv, send_down, send_out, leaving, *prompt_parts
+    )
+
+    prompt_parts = [prompt_parts[0]] + [permute(prompt_parts[t], CHIP[t]) for t in range(1, 4)]
+    grad_wq = tn(hidden_one, grad_q).astype(bf16).reshape(8, 2, 64, -1)
+    keep_q, send_q = pick(grad_wq, y, 1), permute(pick(grad_wq, 1 - y, 1), OVER_Y)
+    left = regrouped(leaving.reshape(-1, width))
+    grad_q, keep_q, send_q, send_down, send_out, send_two, left, *prompt_parts = together(
+        grad_q, keep_q, send_q, send_down, send_out, send_two, left, *prompt_parts
+    )
+    sum_two = added(keep_two, send_two)
+    down, out = added(keep_down, send_down), added(keep_out, send_out)
+    down = halved(down, 0, z_lo, CHIP[2])
+    out = halved(out, 0, x, CHIP[1])
+    sum_two = halved(sum_two, 2, x, CHIP[1])
+    grad_kv, key_gains = whole_call(
+        prompt_back_kernel,
+        "prompt_back",
+        (*prompt_parts, grad_kv, rawk, kg, cos, sin),
+        [(grad_kv.shape, bf16), ((8, HEAD_SIZE), f32)],
+    )
+    grad_wkv = tn(hidden_one, grad_kv).astype(bf16).reshape(8, 2, 64, -1)
+    grad_one = nt(grad_q, w_q) + nt(after(grad_kv, grad_wkv), w_kv)
+    grad_one, sum_two = together(grad_one, sum_two)
+    grad_one = grad_one[:row_total] + permute(
+        grad_one[row_total:].astype(bf16), SIBLING
+    ).astype(f32)
+    normed_one, inverse_one = normed_parts(inputs)
+    gain_one_part = jnp.sum(grad_one * normed_one, axis=0)
+    grad_tokens = grad_resid + norm_back(grad_one * norm1_gain, normed_one, inverse_one)
+    going = deal_all(leave_in_turn, grad_tokens.astype(bf16))
+    gain_grads = jnp.concatenate(
+        [gain_one_part, gain_two_part, gains[0], gains[1] + key_gains[0]]
+    ).reshape(-1, HEAD_SIZE)
+    going, gain_grads, down, out, keep_q, send_q, grad_wkv, left, sum_two = together(
+        going, gain_grads, down, out, keep_q, send_q, grad_wkv, left, sum_two
+    )
+    going = swap_cube(going)
+    q_parts = chip_parts(added(keep_q, send_q))
+    q_sent = sent_to_chips(q_parts)
+    keep_kv, send_kv = pick(grad_wkv, y, 1), permute(pick(grad_wkv, 1 - y, 1), OVER_Y)
+    three = jnp.concatenate([down, out], axis=0)
+    three = added(three, permute(three, MIDDLE_IN))
+    gain_grads = gain_grads + permute(gain_grads, SIBLING)
+    outcome = place_all(home_in_turn, left.reshape(8, -1, width), row_total, bf16)
+    going, three, gain_grads, outcome, keep_kv, send_kv, sum_two, *q_sent = together(
+        going, three, gain_grads, outcome, keep_kv, send_kv, sum_two, *q_sent
+    )
+    going = regrouped(going.reshape(-1, width))
+    sum_two = halved(sum_two, 1, z_lo, CHIP[2])
+    gain_grads = gain_grads + permute(gain_grads, CHIP[1])
+    kv_parts = chip_parts(added(keep_kv, send_kv))
+    kv_sent = sent_to_chips(kv_parts)
+    part_q = added(q_parts[0], *q_sent)
+    going, gain_grads, sum_two, *kv_sent = together(going, gain_grads, sum_two, *kv_sent)
+    gain_grads = gain_grads + permute(gain_grads, CHIP[2])
+    grad_tokens = place_all(home_in_turn, going.reshape(8, -1, width), row_total, f32)
+    part_kv = added(kv_parts[0], *kv_sent)
+    sum_one = jnp.concatenate([part_q, part_kv], axis=2)
+    sum_one = added(sum_one[0], permute(sum_one[1], MIDDLE))
+    three = added(three, permute(three, OVER_Y))
+    sum_two = from_middle(sum_two)
+    sum_one, sum_two, three, gain_grads = together(sum_one, sum_two, three, gain_grads)
+    sum_two = jnp.concatenate(in_order(y == 0, sum_two, permute(sum_two, OVER_Y)), axis=0)
+    gain_grads = gain_grads + permute(gain_grads, OVER_Y)
+    sum_one = jnp.concatenate(in_order(y == 0, sum_one, permute(sum_one, OVER_Y)), axis=0)
+    total = jnp.where(at_home, three, permute(three, SIBLING)).astype(f32)
+    sum_one, sum_two, gain_grads = together(sum_one, sum_two, gain_grads)
+    gain_grads = gain_grads + permute(gain_grads, MIDDLE)
+    gate_up = jnp.stack(in_order(core == 0, sum_two, permute(sum_two, SIBLING)), axis=1)
+    gate_up = gate_up.reshape(-1, 2, 4, 2, ff).astype(f32)
+    one_halves = in_order(core == 0, sum_one, permute(sum_one, SIBLING))
+    query_halves = [part[:, :1024] for part in one_halves]
+    kv_halves = [part[:, 1024:] for part in one_halves]
+    kv_grad = jnp.concatenate(kv_halves, axis=1).reshape(-1, 8, 2, HEAD_SIZE).astype(f32)
+
+    gain_grads = gain_grads.reshape(-1)
+    return (
+        outcome,
+        grad_tokens,
+        gain_grads[:width],
+        jnp.concatenate(query_halves, axis=1).astype(f32),
+        kv_grad[:, :, 0].reshape(-1, 1024),
+        kv_grad[:, :, 1].reshape(-1, 1024),
+        gain_grads[2 * width : 2 * width + HEAD_SIZE],
+        gain_grads[2 * width + HEAD_SIZE :],
+        total[3 * RUN :],
+        gain_grads[width : 2 * width],
+        gate_up[:, :, :, 0].reshape(-1, 8 * ff),
+        gate_up[:, :, :, 1].reshape(-1, 8 * ff),
+        total[: 3 * RUN],
+    )
+
+
 def solution(mesh):
+    split = mesh.shape["grp"] == N_GRP and mesh.shape["ctx"] == N_CTX
     return jax.shard_map(
-        shards,
+        shards_split if split else shards,
         mesh=mesh,
         in_specs=(
             P(("grp", "ctx"), None),

time: 2660 us -> 741 us (0.28)
  waiting for transfers between devices: 1370 us -> 302 us
  matrix products: 761 us -> 45.3 us
  local copies, waits for them, and re-layouts: 263 us -> 49.5 us
  Pallas kernels: 0 us -> 157 us
  starting transfers between devices: 0.72 us -> 111 us
  other arithmetic: 161 us -> 67.4 us
  blocking collectives: 40.1 us -> 0 us
  loops' own time: 37.1 us -> 0 us
    reduce_scatter x8 -> x0, waiting for transfers between devices: 887 us -> none  [the longest x1 231 us: shards(): lax.psum_scatter(key_gradient_parts.reshape(group_length, 2, KEY_VALUE_HE...]
    dot_general x93 -> x8, matrix products: 761 us -> 45.3 us  [the longest x5 34.4 us: tn(): lax.dot_general(a, b, (((0,), (0,)), ((), ())), preferred_element_type=f32)]
    all_gather x9 -> x0, waiting for transfers between devices: 454 us -> none  [the longest x1 126 us: shards(): lax.all_gather(key_low, 'ctx', axis=0, tiled=True)]
    ppermute x0 -> x76, waiting for transfers between devices: none -> 302 us  [permute(): return lax.ppermute(a, AXES, pairs)]
    pallas_call x0 -> x14, Pallas kernels: none -> 157 us  [the longest x1 45.5 us: attn_bwd(): pl.pallas_call(attn_bwd_kernel, grid_spec=pltpu.PrefetchScalarGridSpec(nu...]
    ppermute x0 -> x76, starting transfers between devices: none -> 98.2 us  [permute(): return lax.ppermute(a, AXES, pairs)]
    dynamic_slice x54 -> x6, local copies, waits for them, and re-layouts: 77.1 us -> 3.67 us  [the longest x4 3.62 us: pick(): return lax.dynamic_index_in_dim(a, i, axis, keepdims=False)]
    reduce_sum x15 -> x4, other arithmetic: 74.8 us -> 3.59 us  [the longest x1 2.15 us: shards_split(): gain_two_part = jnp.sum(grad_two * normed_two, axis=0)]
  transfers between devices with their start and end apart: 18 -> 79, of which waited for: 15 -> 30; matrix products, arithmetic and copies ran while one was open for 17% -> 18% of each run, Pallas kernels for 0% -> 15%
where the time goes in v2:
time: 741 us; the launch traced here: 734 us
  waiting for transfers between devices  302 us (41%)
  Pallas kernels  157 us (21%)
  starting transfers between devices  111 us (15%)
  other arithmetic  67.4 us (9%)
  local copies, waits for them, and re-layouts  49.5 us (7%)
  matrix products  45.3 us (6%)
    ppermute x76, waiting for transfers between devices, permute(): return lax.ppermute(a, AXES, pairs)  302 us
    ppermute x76, starting transfers between devices, permute(): return lax.ppermute(a, AXES, pairs)  98.2 us
    pallas_call x1, Pallas kernels, attn_bwd(): pl.pallas_call(attn_bwd_kernel, grid_spec=pltpu.PrefetchScalarGridSpec(nu...  45.5 us
    pallas_call x1, Pallas kernels, mlp(): pl.pallas_call(mlp_kernel, grid_spec=pltpu.PrefetchScalarGridSpec(num_sca...  39.1 us
    dot_general x5, matrix products, tn(): lax.dot_general(a, b, (((0,), (0,)), ((), ())), preferred_element_type=f32)  34.4 us
    pallas_call x9, Pallas kernels, whole_call(): pl.pallas_call(kernel, in_specs=[smem if a.dtype == jnp.int32 else vmem f...  31 us
    pallas_call x2, Pallas kernels, project(): pl.pallas_call(kernel, grid_spec=pltpu.PrefetchScalarGridSpec(num_scalar_...  21.2 us
    pallas_call x1, Pallas kernels, attn_fwd(): pl.pallas_call(attn_fwd_kernel, grid_spec=pltpu.PrefetchScalarGridSpec(nu...  19.8 us
  transfers between devices with their start and end apart: 79, of which 30 were waited for; matrix products, arithmetic and copies ran while one was open for 18% of the time, Pallas kernels for 15%

profile of v2, /device:TPU:0, one launch (start us, length us, event | category | flops | bytes accessed | tf_op | source)
XLA Modules:
  0.0 734.4 jit_solution(3492805377074562525)
XLA Ops:
  35.9 14.1 %collective-permute-done.5.refs_5_ = bf16[80,1024]{1,0:T(8,128)(2,1)S(1)} collective-permute-done((bf16[80,1024]{1,0:T(8,128)(2,1)}, bf16[80,1024]{1,0:T(8,128)(2,1)S(1)}, u32[]{:S(2)}, u32[]{:S(2)}) %collective-permute-start.5) | collective-permute-done | bytes 163872 | tf_op jit(solution)/shard_map/ppermute | solution.py:985
  54.8 11.3 %collective-permute-start.9 = (bf16[640,1024]{1,0:T(8,128)(2,1)S(1)}, bf16[640,1024]{1,0:T(8,128)(2,1)S(1)}, u32[]{:S(2)}, u32[]{:S(2)}) collective-permute-start(bf16[640,1024]{1,0:T(8,128)(2,1)S(1)} %pad_maximum_fusion.5), channel_id=1, source_target_pairs={{0,4},{1,5},{2,6},{3,7},{12,8},{13,9},{14,10},{15,11},{16,20},{17,... | collective-permute-start | bytes 3932168 | tf_op jit(solution)/shard_map/ppermute | solution.py:985
  69.7 6.4 collective-permute-done.11.refs_2_
  80.4 22.9 %collective-permute-done.12.refs_3_ = bf16[128,2048]{1,0:T(8,128)(2,1)S(1)} collective-permute-done((bf16[128,2048]{1,0:T(8,128)(2,1)S(1)}, bf16[128,2048]{1,0:T(8,128)(2,1)S(1)}, u32[]{:S(2)}, u32[]{:S(2)}) %collective-permute-start.12) | collective-permute-done | bytes 524320 | tf_op jit(solution)/shard_map/ppermute | solution.py:985
  103.3 5.8 collective-permute-done.15.refs_6_
  109.1 10.5 %collective-permute-done.16.refs_7_ = bf16[128,2048]{1,0:T(8,128)(2,1)S(1)} collective-permute-done((bf16[128,2048]{1,0:T(8,128)(2,1)S(1)}, bf16[128,2048]{1,0:T(8,128)(2,1)S(1)}, u32[]{:S(2)}, u32[]{:S(2)}) %collective-permute-start.16) | collective-permute-done | bytes 524320 | tf_op jit(solution)/shard_map/ppermute | solution.py:985
  124.9 9.8 %key_value.1 = (bf16[1152,1024]{1,0:T(8,128)(2,1)}, f32[1152,512]{1,0:T(8,128)}, bf16[1024,1024]{1,0:T(8,128)(2,1)}, bf16[256,1024]{1,0:T(8,128)(2,1)}) custom-call(s32[5]{0:T(128)} %stack.138.info, bf16[1152,1024]{1,0:T(8,128)(2,1)} %pad_maximum_fusion.h_ref, bf16[128,2048]{1,0:T(8,128)(2,1)} %copy-done.14, bf16[128,2048]{1,0:T(8,128)(2,1)} %copy-done.20, ...), custom_call_target="tpu_custom_call" | custom-call | tf_op jit(solution)/shard_map/key_value/pallas_call | solution.py:625
  140.9 8.0 %collective-permute-done.20.refs_3_ = bf16[64,3072]{1,0:T(8,128)(2,1)} collective-permute-done((bf16[64,3072]{1,0:T(8,128)(2,1)S(1)}, bf16[64,3072]{1,0:T(8,128)(2,1)}, u32[]{:S(2)}, u32[]{:S(2)}) %collective-permute-start.20) | collective-permute-done | bytes 393248 | tf_op jit(solution)/shard_map/ppermute | solution.py:985
  157.0 11.4 %query.1 = (bf16[1152,1024]{1,0:T(8,128)(2,1)}, f32[1152,1024]{1,0:T(8,128)}, bf16[1024,1024]{1,0:T(8,128)(2,1)}) custom-call(s32[5]{0:T(128)} %stack.138.info, bf16[1152,1024]{1,0:T(8,128)(2,1)} %pad_maximum_fusion.h_ref, bf16[128,2048]{1,0:T(8,128)(2,1)} %copy-done.14, bf16[128,2048]{1,0:T(8,128)(2,1)} %copy-done.20, bf16[128,2048]{1,0:T(8,128)(2,1)} %copy-done.21, ...), custom_call_target="tpu_custom_call" | custom-call | tf_op jit(solution)/shard_map/query/pallas_call | solution.py:625
  168.4 8.6 %collective-permute-done.21 = bf16[256,1024]{1,0:T(8,128)(2,1)S(1)} collective-permute-done((bf16[256,1024]{1,0:T(8,128)(2,1)S(1)}, bf16[256,1024]{1,0:T(8,128)(2,1)S(1)}, u32[]{:S(2)}, u32[]{:S(2)}) %collective-permute-start.21) | collective-permute-done | bytes 524320 | tf_op jit(solution)/shard_map/ppermute | solution.py:985
  181.5 8.2 %collective-permute-done.24.p2 = bf16[256,1024]{1,0:T(8,128)(2,1)} collective-permute-done((bf16[256,1024]{1,0:T(8,128)(2,1)}, bf16[256,1024]{1,0:T(8,128)(2,1)}, u32[]{:S(2)}, u32[]{:S(2)}) %collective-permute-start.24) | collective-permute-done | bytes 524320 | tf_op jit(solution)/shard_map/ppermute | solution.py:985
  189.7 11.4 %collective-permute-done.25.p3 = bf16[256,1024]{1,0:T(8,128)(2,1)} collective-permute-done((bf16[256,1024]{1,0:T(8,128)(2,1)}, bf16[256,1024]{1,0:T(8,128)(2,1)}, u32[]{:S(2)}, u32[]{:S(2)}) %collective-permute-start.25) | collective-permute-done | bytes 524320 | tf_op jit(solution)/shard_map/ppermute | solution.py:985
  205.9 19.8 %attn_fwd.1 = (bf16[1152,1024]{1,0:T(8,128)(2,1)}, f32[4,8,1280]{2,1,0:T(8,128)}) custom-call(s32[5]{0:T(128)} %stack.138.info, bf16[1152,1024]{1,0:T(8,128)(2,1)} %get-tuple-element.193.q_ref, bf16[1152,1024]{1,0:T(8,128)(2,1)} %get-tuple-element.194.kv_ref, bf16[256,1024]{1,0:T(8,128)(2,1)} %get-tuple-element.195.p0, ...), custom_call_target="tpu_custom_call" | custom-call | flops 20000000000 | bytes 10000000 | tf_op jit(solution)/shard_map/attn_fwd/pallas_call | solution.py:717
  225.8 17.6 %collective-permute-done.29.refs_1_ = bf16[2,256,1024]{2,1,0:T(8,128)(2,1)} collective-permute-done((bf16[2,256,1024]{2,1,0:T(8,128)(2,1)S(1)}, bf16[2,256,1024]{2,1,0:T(8,128)(2,1)}, u32[]{:S(2)}, u32[]{:S(2)}) %collective-permute-start.29) | collective-permute-done | bytes 1048608 | tf_op jit(solution)/shard_map/ppermute | solution.py:985
  249.2 6.7 out_projection.1
  267.4 17.1 %collective-permute-done.33.refs_11_ = bf16[384,1024]{1,0:T(8,128)(2,1)S(1)} collective-permute-done((bf16[384,1024]{1,0:T(8,128)(2,1)S(1)}, bf16[384,1024]{1,0:T(8,128)(2,1)S(1)}, u32[]{:S(2)}, u32[]{:S(2)}) %collective-permute-start.33) | collective-permute-done | bytes 786464 | tf_op jit(solution)/shard_map/ppermute | solution.py:985
  284.6 16.5 %collective-permute-done.35.refs_13_ = bf16[384,1024]{1,0:T(8,128)(2,1)S(1)} collective-permute-done((bf16[384,1024]{1,0:T(8,128)(2,1)S(1)}, bf16[384,1024]{1,0:T(8,128)(2,1)S(1)}, u32[]{:S(2)}, u32[]{:S(2)}) %collective-permute-start.35) | collective-permute-done | bytes 786464 | tf_op jit(solution)/shard_map/ppermute | solution.py:985
  314.0 39.1 %feed_forward.1 = (bf16[1152,1536]{1,0:T(8,128)(2,1)}, bf16[1152,3072]{1,0:T(8,128)(2,1)}, f32[576,1024]{1,0:T(8,128)}, bf16[576,1024]{1,0:T(8,128)(2,1)}, f32[5...) custom-call(s32[5]{0:T(128)} %stack.138.info, bf16[1152,1024]{1,0:T(8,128)(2,1)} %constant_dynamic-update-slice_fusion.2.h_ref, ...), custom_call_target="tpu_custom_call" | custom-call | flops 38000001024 | bytes 10000000 | tf_op jit(solution)/shard_map/feed_forward/pallas_call | solution.py:898
  353.8 11.7 %convolution_convert_fusion = bf16[1024,3072]{1,0:T(8,128)(2,1)S(1)} fusion(bf16[1152,1024]{1,0:T(8,128)(2,1)} %constant_dynamic-update-slice_fusion.2.h_ref, bf16[1152,3072]{1,0:T(8,128)(2,1)} %get-tuple-element.236), kind=kOutput, calls=%fused_computation.1 | convolution fusion | flops 7250903040 | bytes 15728640 | tf_op jit(solution)/shard_map/dot_general | solution.py:466
  375.6 7.0 convolution_convert_fusion.2
  405.9 45.5 %attn_bwd.1 = (bf16[1152,1024]{1,0:T(8,128)(2,1)}, bf16[1152,1024]{1,0:T(8,128)(2,1)}, bf16[256,1024]{1,0:T(8,128)(2,1)}, bf16[256,1024]{1,0:T(8,128)(2,1)}, bf1...) custom-call(s32[5]{0:T(128)} %stack.138.info, bf16[1152,1024]{1,0:T(8,128)(2,1)} %get-tuple-element.193.q_ref, ...), custom_call_target="tpu_custom_call" | custom-call | flops 44999999488 | bytes 10000000 | tf_op jit(solution)/shard_map/attn_bwd/pallas_call | solution.py:801
  466.4 8.3 %collective-permute-done.46.d1 = bf16[256,1024]{1,0:T(8,128)(2,1)} collective-permute-done((bf16[256,1024]{1,0:T(8,128)(2,1)}, bf16[256,1024]{1,0:T(8,128)(2,1)}, u32[]{:S(2)}, u32[]{:S(2)}) %collective-permute-start.46) | collective-permute-done | bytes 524320 | tf_op jit(solution)/shard_map/ppermute | solution.py:985
  474.7 12.2 %collective-permute-done.47.d2 = bf16[256,1024]{1,0:T(8,128)(2,1)} collective-permute-done((bf16[256,1024]{1,0:T(8,128)(2,1)}, bf16[256,1024]{1,0:T(8,128)(2,1)}, u32[]{:S(2)}, u32[]{:S(2)}) %collective-permute-start.47) | collective-permute-done | bytes 524320 | tf_op jit(solution)/shard_map/ppermute | solution.py:985
  486.9 7.8 %collective-permute-done.48.d3 = bf16[256,1024]{1,0:T(8,128)(2,1)} collective-permute-done((bf16[256,1024]{1,0:T(8,128)(2,1)}, bf16[256,1024]{1,0:T(8,128)(2,1)}, u32[]{:S(2)}, u32[]{:S(2)}) %collective-permute-start.48) | collective-permute-done | bytes 524320 | tf_op jit(solution)/shard_map/ppermute | solution.py:985
  511.9 5.9 convolution_convert_fusion.3
  523.3 16.6 %collective-permute-done.49 = bf16[2,2,64,3072]{3,2,1,0:T(8,128)(2,1)} collective-permute-done((bf16[2,2,64,3072]{3,2,1,0:T(8,128)(2,1)}, bf16[2,2,64,3072]{3,2,1,0:T(8,128)(2,1)}, u32[]{:S(2)}, u32[]{:S(2)}) %collective-permute-start.49) | collective-permute-done | bytes 1572896 | tf_op jit(solution)/shard_map/ppermute | solution.py:985
  548.4 12.1 %collective-permute-done.52 = bf16[256,1024]{1,0:T(8,128)(2,1)S(1)} collective-permute-done((bf16[256,1024]{1,0:T(8,128)(2,1)S(1)}, bf16[256,1024]{1,0:T(8,128)(2,1)S(1)}, u32[]{:S(2)}, u32[]{:S(2)}) %collective-permute-start.52) | collective-permute-done | bytes 524320 | tf_op jit(solution)/shard_map/ppermute | solution.py:985
  593.7 17.0 %collective-permute-done.53 = bf16[640,1024]{1,0:T(8,128)(2,1)} collective-permute-done((bf16[640,1024]{1,0:T(8,128)(2,1)}, bf16[640,1024]{1,0:T(8,128)(2,1)}, u32[]{:S(2)}, u32[]{:S(2)}) %collective-permute-start.53) | collective-permute-done | bytes 1310752 | tf_op jit(solution)/shard_map/ppermute | solution.py:985
  627.6 24.0 %collective-permute-done.61 = bf16[2,64,3072]{2,1,0:T(8,128)(2,1)S(1)} collective-permute-done((bf16[2,64,3072]{2,1,0:T(8,128)(2,1)S(1)}, bf16[2,64,3072]{2,1,0:T(8,128)(2,1)S(1)}, u32[]{:S(2)}, u32[]{:S(2)}) %collective-permute-start.61) | collective-permute-done | bytes 786464 | tf_op jit(solution)/shard_map/ppermute | solution.py:985
  664.8 16.4 %collective-permute-done.67 = bf16[640,1024]{1,0:T(8,128)(2,1)S(1)} collective-permute-done((bf16[640,1024]{1,0:T(8,128)(2,1)S(1)}, bf16[640,1024]{1,0:T(8,128)(2,1)S(1)}, u32[]{:S(2)}, u32[]{:S(2)}) %collective-permute-start.67) | collective-permute-done | bytes 1310752 | tf_op jit(solution)/shard_map/ppermute | solution.py:985
  682.8 10.5 %collective-permute-done.65 = bf16[64,2048]{1,0:T(8,128)(2,1)S(1)} collective-permute-done((bf16[64,2048]{1,0:T(8,128)(2,1)S(1)}, bf16[64,2048]{1,0:T(8,128)(2,1)S(1)}, u32[]{:S(2)}, u32[]{:S(2)}) %collective-permute-start.65) | collective-permute-done | bytes 262176 | tf_op jit(solution)/shard_map/ppermute | solution.py:985
  704.2 7.8 %collective-permute-done.70 = bf16[64,3072]{1,0:T(8,128)(2,1)S(1)} collective-permute-done((bf16[64,3072]{1,0:T(8,128)(2,1)S(1)}, bf16[64,3072]{1,0:T(8,128)(2,1)S(1)}, u32[]{:S(2)}, u32[]{:S(2)}) %collective-permute-start.70) | collective-permute-done | bytes 393248 | tf_op jit(solution)/shard_map/ppermute | solution.py:985
  (421 shorter events, 284.0 us)
Async XLA Ops:
  32.5 36.7 %collective-permute-start.13 = (bf16[128,2048]{1,0:T(8,128)(2,1)S(1)}, bf16[128,2048]{1,0:T(8,128)(2,1)S(1)}, u32[]{:S(2)}, u32[]{:S(2)}) collective-permute-start(bf16[128,2048]{1,0:T(8,128)(2,1)S(1)} %constant_dynamic-update-slice_fusion.refs_0_), channel_id=1, source_target_pairs={{0,4},{1,5},{2,6},{3,7},{4,0},{5,1},{6,2},{7,3},{8,12},{9,13},{10,... | collective-permute-start | bytes 1572872 | tf_op jit(solution)/shard_map/ppermute | solution.py:985
  35.5 33.8 %collective-permute-start.10 = (bf16[128,2048]{1,0:T(8,128)(2,1)S(1)}, bf16[128,2048]{1,0:T(8,128)(2,1)S(1)}, u32[]{:S(2)}, u32[]{:S(2)}) collective-permute-start(bf16[128,2048]{1,0:T(8,128)(2,1)S(1)} %constant_dynamic-update-slice_fusion.refs_0_), channel_id=1, source_target_pairs={{0,1},{1,0},{2,3},{3,2},{4,5},{5,4},{6,7},{7,6},{8,9},{9,8},{10,11... | collective-permute-start | bytes 1572872 | tf_op jit(solution)/shard_map/ppermute | solution.py:985
  54.8 64.8 %collective-permute-start.9 = (bf16[640,1024]{1,0:T(8,128)(2,1)S(1)}, bf16[640,1024]{1,0:T(8,128)(2,1)S(1)}, u32[]{:S(2)}, u32[]{:S(2)}) collective-permute-start(bf16[640,1024]{1,0:T(8,128)(2,1)S(1)} %pad_maximum_fusion.5), channel_id=1, source_target_pairs={{0,4},{1,5},{2,6},{3,7},{12,8},{13,9},{14,10},{15,11},{16,20},{17,... | collective-permute-start | bytes 3932168 | tf_op jit(solution)/shard_map/ppermute | solution.py:985
  69.2 34.1 %collective-permute-start.12 = (bf16[128,2048]{1,0:T(8,128)(2,1)S(1)}, bf16[128,2048]{1,0:T(8,128)(2,1)S(1)}, u32[]{:S(2)}, u32[]{:S(2)}) collective-permute-start(bf16[128,2048]{1,0:T(8,128)(2,1)S(1)} %constant_dynamic-update-slice_fusion.refs_0_), channel_id=1, source_target_pairs={{0,3},{1,2},{2,1},{3,0},{4,7},{5,6},{6,5},{7,4},{8,11},{9,10},{10,... | collective-permute-start | bytes 1572872 | tf_op jit(solution)/shard_map/ppermute | solution.py:985
  69.3 34.0 %collective-permute-start.14 = (bf16[128,2048]{1,0:T(8,128)(2,1)S(1)}, bf16[128,2048]{1,0:T(8,128)(2,1)S(1)}, u32[]{:S(2)}, u32[]{:S(2)}) collective-permute-start(bf16[128,2048]{1,0:T(8,128)(2,1)S(1)} %collective-permute-done.13.refs_4_), channel_id=1, source_target_pairs={{0,1},{1,0},{2,3},{3,2},{4,5},{5,4},{6,7},{7,6},{8,9},{9,8},{10,11... | collective-permute-start | bytes 1572872 | tf_op jit(solution)/shard_map/ppermute | solution.py:985
  76.1 33.0 %collective-permute-start.15 = (bf16[128,2048]{1,0:T(8,128)(2,1)S(1)}, bf16[128,2048]{1,0:T(8,128)(2,1)S(1)}, u32[]{:S(2)}, u32[]{:S(2)}) collective-permute-start(bf16[128,2048]{1,0:T(8,128)(2,1)S(1)} %collective-permute-done.13.refs_4_), channel_id=1, source_target_pairs={{0,2},{1,3},{2,0},{3,1},{4,6},{5,7},{6,4},{7,5},{8,10},{9,11},{10,... | collective-permute-start | bytes 1572872 | tf_op jit(solution)/shard_map/ppermute | solution.py:985
  76.1 43.4 %collective-permute-start.16 = (bf16[128,2048]{1,0:T(8,128)(2,1)S(1)}, bf16[128,2048]{1,0:T(8,128)(2,1)S(1)}, u32[]{:S(2)}, u32[]{:S(2)}) collective-permute-start(bf16[128,2048]{1,0:T(8,128)(2,1)S(1)} %collective-permute-done.13.refs_4_), channel_id=1, source_target_pairs={{0,3},{1,2},{2,1},{3,0},{4,7},{5,6},{6,5},{7,4},{8,11},{9,10},{10,... | collective-permute-start | bytes 1572872 | tf_op jit(solution)/shard_map/ppermute | solution.py:985
  152.9 36.8 %collective-permute-start.24 = (bf16[256,1024]{1,0:T(8,128)(2,1)}, bf16[256,1024]{1,0:T(8,128)(2,1)}, u32[]{:S(2)}, u32[]{:S(2)}) collective-permute-start(bf16[256,1024]{1,0:T(8,128)(2,1)} %get-tuple-element.195.p0), channel_id=1, source_target_pairs={{0,2},{1,3},{2,0},{3,1},{4,6},{5,7},{6,4},{7,5},{8,10},{9,11},{10,... | collective-permute-start | bytes 1572872 | tf_op jit(solution)/shard_map/ppermute | solution.py:985
  154.9 46.1 %collective-permute-start.25 = (bf16[256,1024]{1,0:T(8,128)(2,1)}, bf16[256,1024]{1,0:T(8,128)(2,1)}, u32[]{:S(2)}, u32[]{:S(2)}) collective-permute-start(bf16[256,1024]{1,0:T(8,128)(2,1)} %get-tuple-element.195.p0), channel_id=1, source_target_pairs={{0,3},{1,2},{2,1},{3,0},{4,7},{5,6},{6,5},{7,4},{8,11},{9,10},{10,... | collective-permute-start | bytes 1572872 | tf_op jit(solution)/shard_map/ppermute | solution.py:985
  177.0 48.7 %collective-permute-start.30 = (bf16[4,64,3072]{2,1,0:T(8,128)(2,1)S(1)}, bf16[4,64,3072]{2,1,0:T(8,128)(2,1)}, u32[]{:S(2)}, u32[]{:S(2)}) collective-permute-start(bf16[4,64,3072]{2,1,0:T(8,128)(2,1)S(1)} %pad_maximum_fusion.3), channel_id=1, source_target_pairs={{0,16},{1,17},{2,18},{3,19},{4,20},{5,21},{6,22},{7,23},{8,24},{9,... | collective-permute-start | bytes 4718600 | tf_op jit(solution)/shard_map/ppermute | solution.py:985
  204.6 38.8 %collective-permute-start.29 = (bf16[2,256,1024]{2,1,0:T(8,128)(2,1)S(1)}, bf16[2,256,1024]{2,1,0:T(8,128)(2,1)}, u32[]{:S(2)}, u32[]{:S(2)}) collective-permute-start(bf16[2,256,1024]{2,1,0:T(8,128)(2,1)S(1)} %pad_maximum_fusion.7.refs_0_), channel_id=1, source_target_pairs={{0,1},{1,0},{2,3},{3,2},{4,5},{5,4},{6,7},{7,6},{8,9},{9,8},{10,11... | collective-permute-start | bytes 3145736 | tf_op jit(solution)/shard_map/ppermute | solution.py:985
  244.8 58.3 %all-to-all-start = ((bf16[8,80,1024]{2,1,0:T(8,128)(2,1)}), bf16[8,80,1024]{2,1,0:T(8,128)(2,1)}, u32[]{:S(2)}, u32[]{:S(2)}) async-start(bf16[8,80,1024]{2,1,0:T(8,128)(2,1)} %pad_maximum_fusion.6), calls=%async_computation | async-start | bytes 2621440 | tf_op jit(solution)/shard_map/all_to_all | solution.py:1161
  258.1 43.0 %collective-permute-start.32 = (bf16[4,64,3072]{2,1,0:T(8,128)(2,1)S(1)}, bf16[4,64,3072]{2,1,0:T(8,128)(2,1)S(1)}, u32[]{:S(2)}, u32[]{:S(2)}) collective-permute-start(bf16[4,64,3072]{2,1,0:T(8,128)(2,1)S(1)} %pad_maximum_fusion.4), channel_id=1, source_target_pairs={{0,16},{1,17},{2,18},{3,19},{4,20},{5,21},{6,22},{7,23},{8,24},{9,... | collective-permute-start | bytes 4718600 | tf_op jit(solution)/shard_map/ppermute | solution.py:985
  262.8 38.3 %collective-permute-start.35 = (bf16[384,1024]{1,0:T(8,128)(2,1)S(1)}, bf16[384,1024]{1,0:T(8,128)(2,1)S(1)}, u32[]{:S(2)}, u32[]{:S(2)}) collective-permute-start(bf16[384,1024]{1,0:T(8,128)(2,1)S(1)} %copy-done.35), channel_id=1, source_target_pairs={{0,3},{1,2},{2,1},{3,0},{4,7},{5,6},{6,5},{7,4},{8,11},{9,10},{10,... | collective-permute-start | bytes 2359304 | tf_op jit(solution)/shard_map/ppermute | solution.py:985
  374.1 92.3 %collective-permute-start.44 = (bf16[2,2,2,64,3072]{4,3,2,1,0:T(8,128)(2,1)}, bf16[2,2,2,64,3072]{4,3,2,1,0:T(8,128)(2,1)}, u32[]{:S(2)}, u32[]{:S(2)}) collective-permute-start(bf16[2,2,2,64,3072]{4,3,2,1,0:T(8,128)(2,1)} %get-tuple-element.372), channel_id=1, source_target_pairs={{0,16},{1,17},{2,18},{3,19},{4,20},{5,21},{6,22},{7,23},{8,24},{9,... | collective-permute-start | bytes 9437192 | tf_op jit(solution)/shard_map/ppermute | solution.py:985
  394.6 56.8 %collective-permute-start.41 = (bf16[2,384,1024]{2,1,0:T(8,128)(2,1)}, bf16[2,384,1024]{2,1,0:T(8,128)(2,1)}, u32[]{:S(2)}, u32[]{:S(2)}) collective-permute-start(bf16[2,384,1024]{2,1,0:T(8,128)(2,1)} %dynamic-slice_bitcast_fusion.2), channel_id=1, source_target_pairs={{0,1},{1,0},{2,3},{3,2},{4,5},{5,4},{6,7},{7,6},{8,9},{9,8},{10,11... | collective-permute-start | bytes 4718600 | tf_op jit(solution)/shard_map/ppermute | solution.py:985
  395.2 56.2 %collective-permute-start.42 = (bf16[2,256,1024]{2,1,0:T(8,128)(2,1)S(1)}, bf16[2,256,1024]{2,1,0:T(8,128)(2,1)}, u32[]{:S(2)}, u32[]{:S(2)}) collective-permute-start(bf16[2,256,1024]{2,1,0:T(8,128)(2,1)S(1)} %dynamic-slice_bitcast_fusion.7), channel_id=1, source_target_pairs={{0,2},{1,3},{2,0},{3,1},{4,6},{5,7},{6,4},{7,5},{8,10},{9,11},{10,... | collective-permute-start | bytes 3145736 | tf_op jit(solution)/shard_map/ppermute | solution.py:985
  395.6 55.8 %all-to-all-start.1 = ((bf16[8,80,1024]{2,1,0:T(8,128)(2,1)}), bf16[8,80,1024]{2,1,0:T(8,128)(2,1)}, u32[]{:S(2)}, u32[]{:S(2)}) async-start(bf16[8,80,1024]{2,1,0:T(8,128)(2,1)} %deal_all.2), calls=%async_computation.1 | async-start | bytes 2621440 | tf_op jit(solution)/shard_map/all_to_all | solution.py:1161
  459.7 35.0 %collective-permute-start.43 = (bf16[8,64,1024]{2,1,0:T(8,128)(2,1)}, bf16[8,64,1024]{2,1,0:T(8,128)(2,1)S(1)}, u32[]{:S(2)}, u32[]{:S(2)}) collective-permute-start(bf16[8,64,1024]{2,1,0:T(8,128)(2,1)} %get-tuple-element.378), channel_id=1, source_target_pairs={{0,16},{1,17},{2,18},{3,19},{4,20},{5,21},{6,22},{7,23},{8,24},{9,... | collective-permute-start | bytes 3145736 | tf_op jit(solution)/shard_map/ppermute | solution.py:985
  463.6 31.0 %collective-permute-start.48 = (bf16[256,1024]{1,0:T(8,128)(2,1)}, bf16[256,1024]{1,0:T(8,128)(2,1)}, u32[]{:S(2)}, u32[]{:S(2)}) collective-permute-start(bf16[256,1024]{1,0:T(8,128)(2,1)} %get-tuple-element.258), channel_id=1, source_target_pairs={{0,3},{1,2},{2,1},{3,0},{4,7},{5,6},{6,5},{7,4},{8,11},{9,10},{10,... | collective-permute-start | bytes 1572872 | tf_op jit(solution)/shard_map/ppermute | solution.py:985
  498.3 62.5 %collective-permute-start.51 = (bf16[384,1024]{1,0:T(8,128)(2,1)}, bf16[384,1024]{1,0:T(8,128)(2,1)}, u32[]{:S(2)}, u32[]{:S(2)}) collective-permute-start(bf16[384,1024]{1,0:T(8,128)(2,1)} %dynamic-slice_bitcast_fusion.9), channel_id=1, source_target_pairs={{0,2},{1,3},{2,0},{3,1},{4,6},{5,7},{6,4},{7,5},{8,10},{9,11},{10,... | collective-permute-start | bytes 2359304 | tf_op jit(solution)/shard_map/ppermute | solution.py:985
  504.6 35.2 %collective-permute-start.49 = (bf16[2,2,64,3072]{3,2,1,0:T(8,128)(2,1)}, bf16[2,2,64,3072]{3,2,1,0:T(8,128)(2,1)}, u32[]{:S(2)}, u32[]{:S(2)}) collective-permute-start(bf16[2,2,64,3072]{3,2,1,0:T(8,128)(2,1)} %dynamic-slice_bitcast_fusion.1), channel_id=1, source_target_pairs={{0,1},{1,0},{2,3},{3,2},{4,5},{5,4},{6,7},{7,6},{8,9},{9,8},{10,11... | collective-permute-start | bytes 4718600 | tf_op jit(solution)/shard_map/ppermute | solution.py:985
  569.0 48.0 %all-to-all-start.2 = ((bf16[8,80,1024]{2,1,0:T(8,128)(2,1)}), bf16[8,80,1024]{2,1,0:T(8,128)(2,1)S(1)}, u32[]{:S(2)}, u32[]{:S(2)}) async-start(bf16[8,80,1024]{2,1,0:T(8,128)(2,1)} %deal_all.3), calls=%async_computation.2 | async-start | bytes 2621440 | tf_op jit(solution)/shard_map/all_to_all | solution.py:1161
  575.8 34.9 %collective-permute-start.53 = (bf16[640,1024]{1,0:T(8,128)(2,1)}, bf16[640,1024]{1,0:T(8,128)(2,1)}, u32[]{:S(2)}, u32[]{:S(2)}) collective-permute-start(bf16[640,1024]{1,0:T(8,128)(2,1)} %constant_dynamic-update-slice_fusion.4), channel_id=1, source_target_pairs={{4,0},{5,1},{6,2},{7,3},{8,12},{9,13},{10,14},{11,15},{20,16},{21,... | collective-permute-start | bytes 3932168 | tf_op jit(solution)/shard_map/ppermute | solution.py:985
  581.1 35.9 %collective-permute-start.55 = (bf16[8,64,1024]{2,1,0:T(8,128)(2,1)}, bf16[8,64,1024]{2,1,0:T(8,128)(2,1)}, u32[]{:S(2)}, u32[]{:S(2)}) collective-permute-start(bf16[8,64,1024]{2,1,0:T(8,128)(2,1)} %get-tuple-element.376), channel_id=1, source_target_pairs={{0,16},{1,17},{2,18},{3,19},{4,20},{5,21},{6,22},{7,23},{8,24},{9,... | collective-permute-start | bytes 3145736 | tf_op jit(solution)/shard_map/ppermute | solution.py:985
  617.1 34.6 %collective-permute-start.61 = (bf16[2,64,3072]{2,1,0:T(8,128)(2,1)S(1)}, bf16[2,64,3072]{2,1,0:T(8,128)(2,1)S(1)}, u32[]{:S(2)}, u32[]{:S(2)}) collective-permute-start(bf16[2,64,3072]{2,1,0:T(8,128)(2,1)S(1)} %dynamic-slice_bitcast_fusion.8), channel_id=1, source_target_pairs={{0,2},{1,3},{2,0},{3,1},{4,6},{5,7},{6,4},{7,5},{8,10},{9,11},{10,... | collective-permute-start | bytes 2359304 | tf_op jit(solution)/shard_map/ppermute | solution.py:985
  617.1 37.9 %collective-permute-start.59 = (bf16[640,1024]{1,0:T(8,128)(2,1)S(1)}, bf16[640,1024]{1,0:T(8,128)(2,1)S(1)}, u32[]{:S(2)}, u32[]{:S(2)}) collective-permute-start(bf16[640,1024]{1,0:T(8,128)(2,1)S(1)} %bitcast.173), channel_id=1, source_target_pairs={{4,8},{5,9},{6,10},{7,11},{8,4},{9,5},{10,6},{11,7},{20,24},{21,25... | collective-permute-start | bytes 3932168 | tf_op jit(solution)/shard_map/ppermute | solution.py:985
  620.2 37.9 %collective-permute-start.64 = (bf16[2,64,1024]{2,1,0:T(8,128)(2,1)S(1)}, bf16[2,64,1024]{2,1,0:T(8,128)(2,1)S(1)}, u32[]{:S(2)}, u32[]{:S(2)}) collective-permute-start(bf16[2,64,1024]{2,1,0:T(8,128)(2,1)S(1)} %pad_maximum_fusion.20), channel_id=1, source_target_pairs={{0,3},{1,2},{2,1},{3,0},{4,7},{5,6},{6,5},{7,4},{8,11},{9,10},{10,... | collective-permute-start | bytes 786440 | tf_op jit(solution)/shard_map/ppermute | solution.py:985
  623.2 38.3 %collective-permute-start.63 = (bf16[2,64,1024]{2,1,0:T(8,128)(2,1)S(1)}, bf16[2,64,1024]{2,1,0:T(8,128)(2,1)S(1)}, u32[]{:S(2)}, u32[]{:S(2)}) collective-permute-start(bf16[2,64,1024]{2,1,0:T(8,128)(2,1)S(1)} %pad_maximum_fusion.19), channel_id=1, source_target_pairs={{0,2},{1,3},{2,0},{3,1},{4,6},{5,7},{6,4},{7,5},{8,10},{9,11},{10,... | collective-permute-start | bytes 786440 | tf_op jit(solution)/shard_map/ppermute | solution.py:985
  627.0 34.5 %collective-permute-start.62 = (bf16[2,64,1024]{2,1,0:T(8,128)(2,1)S(1)}, bf16[2,64,1024]{2,1,0:T(8,128)(2,1)S(1)}, u32[]{:S(2)}, u32[]{:S(2)}) collective-permute-start(bf16[2,64,1024]{2,1,0:T(8,128)(2,1)S(1)} %pad_maximum_fusion.18), channel_id=1, source_target_pairs={{0,1},{1,0},{2,3},{3,2},{4,5},{5,4},{6,7},{7,6},{8,9},{9,8},{10,11... | collective-permute-start | bytes 786440 | tf_op jit(solution)/shard_map/ppermute | solution.py:985
  661.5 31.8 %collective-permute-start.66 = (bf16[64,3072]{1,0:T(8,128)(2,1)S(1)}, bf16[64,3072]{1,0:T(8,128)(2,1)S(1)}, u32[]{:S(2)}, u32[]{:S(2)}) collective-permute-start(bf16[64,3072]{1,0:T(8,128)(2,1)S(1)} %dynamic-slice_bitcast_fusion.11), channel_id=1, source_target_pairs={{0,4},{1,5},{2,6},{3,7},{4,0},{5,1},{6,2},{7,3},{8,12},{9,13},{10,... | collective-permute-start | bytes 1179656 | tf_op jit(solution)/shard_map/ppermute | solution.py:985
  661.8 31.5 %collective-permute-start.65 = (bf16[64,2048]{1,0:T(8,128)(2,1)S(1)}, bf16[64,2048]{1,0:T(8,128)(2,1)S(1)}, u32[]{:S(2)}, u32[]{:S(2)}) collective-permute-start(bf16[64,2048]{1,0:T(8,128)(2,1)S(1)} %fusion.21), channel_id=1, source_target_pairs={{0,4},{1,5},{2,6},{3,7},{4,0},{5,1},{6,2},{7,3},{8,12},{9,13},{10,... | collective-permute-start | bytes 786440 | tf_op jit(solution)/shard_map/ppermute | solution.py:985
  (110 other events, 1658.1 us)

commit v3 on v2

--- a/solution.py
+++ b/solution.py
@@ -844,12 +844,11 @@
     sib_ref[...] = nn(o_ref[half:, :], w_ref[...]).astype(bf16)
 
 
-def mlp_kernel(info, h_ref, g_ref, *refs):
+def mlp_kernel(info, h_own, h_sib, g_own, g_sib, *refs):
     w2, w3 = refs[:10], refs[10:14]
     hid_ref, dgu_ref, out_ref, outs_ref, dh_ref, dhs_ref = refs[14:20]
     w_ref, wd_ref, out_acc, dh_acc = refs[20:]
     step = pl.program_id(0)
-    width = h_ref.shape[1]
     ff = hid_ref.shape[1]
     half = out_ref.shape[0]
     for e in range(8):
@@ -867,15 +866,16 @@
         for ref in (out_ref, dh_ref, out_acc, dh_acc):
             ref[...] = jnp.zeros_like(ref)
 
-    for b, out, dh in ((0, out_ref, dh_ref), (1, out_acc, dh_acc)):
+    sides = ((h_own, g_own, out_ref, dh_ref), (h_sib, g_sib, out_acc, dh_acc))
+    for b, (h_ref, g_ref, out, dh) in enumerate(sides):
         rows = slice(b * half, (b + 1) * half)
-        both = nn(h_ref[rows, :], w_ref[...])
+        both = nn(h_ref[...], w_ref[...])
         gate, up = both[:, :ff], both[:, ff:]
         sig = jax.nn.sigmoid(gate)
         silu = gate * sig
         hid = (silu * up).astype(bf16)
         hid_ref[rows, :] = hid
-        dhid = nt(g_ref[rows, :], wd_ref[...])
+        dhid = nt(g_ref[...], wd_ref[...])
         dgu_ref[rows, :ff] = (dhid * up * sig * (1.0 + gate * (1.0 - sig))).astype(bf16)
         dgu_ref[rows, ff:] = (dhid * silu).astype(bf16)
         dh[...] += nt(dgu_ref[rows, :], w_ref[...])
@@ -888,8 +888,8 @@
 
 
 def mlp(info, hidden, grad, w2, w3, ff):
-    rows, width = hidden.shape
-    half = rows // 2
+    half, width = hidden[0].shape
+    rows = 2 * half
     once = pl.Buffered(1)
 
     def still(shape):
@@ -900,7 +900,7 @@
         grid_spec=pltpu.PrefetchScalarGridSpec(
             num_scalar_prefetch=1,
             grid=(4,),
-            in_specs=[still((rows, width))] * 2
+            in_specs=[still((half, width))] * 4
             + [pl.BlockSpec((64, 2 * ff), lambda g, s: (0, s[4] ^ g))] * 8
             + [pl.BlockSpec((4, 64, 2 * ff), lambda g, s: (0, 0, s[4] ^ g))] * 2
             + [still(w3[0].shape)] * 4,
@@ -927,7 +927,34 @@
         compiler_params=params(),
         cost_estimate=pl.CostEstimate(flops=38*10**9, bytes_accessed=10**7, transcendentals=0),
         name="feed_forward",
-    )(info, hidden, grad, *w2, *w3)
+    )(info, *hidden, *grad, *w2, *w3)
+
+
+def gate_up_kernel(info, own_ref, sib_ref, gate_ref, up_ref):
+    ff = own_ref.shape[1] // 8
+    for first, (low, high) in ((0, (own_ref, sib_ref)), (1, (sib_ref, own_ref))):
+
+        @pl.when(info[2] == first)
+        def write(low=low, high=high):
+            for c, ref in enumerate((low, high)):
+                for b in range(4):
+                    cols = slice((c * 4 + b) * ff, (c * 4 + b + 1) * ff)
+                    gate_ref[:, cols] = ref[:, 2 * b * ff : (2 * b + 1) * ff].astype(f32)
+                    up_ref[:, cols] = ref[:, (2 * b + 1) * ff : (2 * b + 2) * ff].astype(f32)
+
+
+def attn_weights_kernel(info, own_ref, sib_ref, query_ref, key_ref, value_ref):
+    for first, (low, high) in ((0, (own_ref, sib_ref)), (1, (sib_ref, own_ref))):
+
+        @pl.when(info[2] == first)
+        def write(low=low, high=high):
+            for c, ref in enumerate((low, high)):
+                query_ref[:, c * 1024 : (c + 1) * 1024] = ref[:, :1024].astype(f32)
+                for h in range(4):
+                    start = 1024 + h * 256
+                    to = head(c * 4 + h)
+                    key_ref[:, to] = ref[:, start : start + 128].astype(f32)
+                    value_ref[:, to] = ref[:, start + 128 : start + 256].astype(f32)
 
 
 def device_of(y, core, z_hi, z_lo, x):
@@ -964,6 +991,10 @@
 ]
 OVER_Y = permutation(lambda y, core, z_hi, z_lo, x: (1 - y, core, z_hi, z_lo, x))
 SIBLING = permutation(lambda y, core, z_hi, z_lo, x: (y, 1 - core, z_hi, z_lo, x))
+OVER_Y_HOME = permutation(
+    lambda y, core, z_hi, z_lo, x: (1 - y, core, z_hi, z_lo, x),
+    lambda y, core, z_hi, z_lo, x: z_hi == core,
+)
 MIDDLE = permutation(lambda y, core, z_hi, z_lo, x: (y, core, 1 - z_hi, z_lo, x))
 MIDDLE_OUT = permutation(
     lambda y, core, z_hi, z_lo, x: (y, core, 1 - z_hi, z_lo, x),
@@ -1124,27 +1155,28 @@
 
     two = around(own_two)
     middle_two = permute(own_two, MIDDLE)
+    outs = jnp.stack([home_out, permute(home_out, CHIP[2])])
     kv, rawk, w_kv, prompt_kv = project(
         key_value_kernel, "key_value", info, hidden_one, one, 4, kg, cos, sin, HEAD_SIZE, 1
     )
-    prompt_kv, home_out, out_grad, hidden_q, middle_two, *two = together(
-        prompt_kv, home_out, out_grad, hidden_one, middle_two, *two
+    prompt_kv, outs, out_grad, hidden_q, middle_two, *two = together(
+        prompt_kv, outs, out_grad, hidden_one, middle_two, *two
     )
 
     prompt = around(prompt_kv)
-    outs = jnp.stack([home_out, permute(home_out, CHIP[2])])
+    outs = [outs, permute(outs, CHIP[1])]
     grad_here = regrouped(out_grad)
     q, rawq, w_q = project(query_kernel, "query", info, hidden_q, one, 0, qg, cos, sin, 256, 0)
-    q, outs, grad_here, middle_two, home_down, *prompt = together(
-        q, outs, grad_here, middle_two, home_down, *prompt
-    )
+    q, grad_here, middle_two, home_down, *rest = together(
+        q, grad_here, middle_two, home_down, *outs, *prompt
+    )
+    outs, prompt = rest[:2], rest[2:]
 
     two += around(middle_two)
     other_two = [permute(jnp.stack(two[:4]), OVER_Y)]
-    outs = [outs, permute(outs, CHIP[1])]
     mixed, lse = attn_fwd(info, q, kv, prompt)
-    mixed, home_down, grad_here, *rest = together(mixed, home_down, grad_here, *two, *outs, *other_two)
-    two, outs, other_two = rest[:8], rest[8:10], rest[10:]
+    mixed, home_down, grad_here, *rest = together(mixed, home_down, grad_here, *two, *other_two)
+    two, other_two = rest[:8], rest[8:]
 
     other_two.append(permute(jnp.stack(two[4:]), OVER_Y))
     downs = around(home_down)
@@ -1182,12 +1214,14 @@
     hidden_two = (normed_two * norm2_gain).astype(bf16)
     hidden_two, other_far, *downs = together(hidden_two, other_two[1], *downs)
     other_two = [other_two[0], other_far]
-    hidden_two = both(hidden_two)
+    hidden_two = [hidden_two, permute(hidden_two, SIBLING)]
     grad_low = place_all(in_turn, grad_here, row_total, bf16)
-    grad_both = both(grad_low)
+    grad_both = [grad_low, permute(grad_low, SIBLING)]
     hid, grad_gu, ff_own, ff_sib, back_own, back_sib = mlp(
         info, hidden_two, grad_both, two + other_two, downs, ff
     )
+    hidden_two = jnp.concatenate(hidden_two, axis=0)
+    grad_both = jnp.concatenate(grad_both, axis=0)
     grad_two = back_own + permute(back_sib, SIBLING).astype(f32)
     gain_two_part = jnp.sum(grad_two * normed_two, axis=0)
     grad_resid = grad_low.astype(f32) + norm_back(grad_two * norm2_gain, normed_two, inverse_two)
@@ -1232,10 +1266,10 @@
     prompt_parts = [prompt_parts[0]] + [permute(prompt_parts[t], CHIP[t]) for t in range(1, 4)]
     grad_wq = tn(hidden_one, grad_q).astype(bf16).reshape(8, 2, 64, -1)
     keep_q, send_q = pick(grad_wq, y, 1), permute(pick(grad_wq, 1 - y, 1), OVER_Y)
+    grad_q, keep_q, send_q, send_down, send_out, send_two, leaving, *prompt_parts = together(
+        grad_q, keep_q, send_q, send_down, send_out, send_two, leaving, *prompt_parts
+    )
     left = regrouped(leaving.reshape(-1, width))
-    grad_q, keep_q, send_q, send_down, send_out, send_two, left, *prompt_parts = together(
-        grad_q, keep_q, send_q, send_down, send_out, send_two, left, *prompt_parts
-    )
     sum_two = added(keep_two, send_two)
     down, out = added(keep_down, send_down), added(keep_out, send_out)
     down = halved(down, 0, z_lo, CHIP[2])
@@ -1271,8 +1305,8 @@
     three = added(three, permute(three, MIDDLE_IN))
     gain_grads = gain_grads + permute(gain_grads, SIBLING)
     outcome = place_all(home_in_turn, left.reshape(8, -1, width), row_total, bf16)
-    going, three, gain_grads, outcome, keep_kv, send_kv, sum_two, *q_sent = together(
-        going, three, gain_grads, outcome, keep_kv, send_kv, sum_two, *q_sent
+    going, gain_grads, outcome, keep_kv, send_kv, sum_two, *q_sent = together(
+        going, gain_grads, outcome, keep_kv, send_kv, sum_two, *q_sent
     )
     going = regrouped(going.reshape(-1, width))
     sum_two = halved(sum_two, 1, z_lo, CHIP[2])
@@ -1280,13 +1314,15 @@
     kv_parts = chip_parts(added(keep_kv, send_kv))
     kv_sent = sent_to_chips(kv_parts)
     part_q = added(q_parts[0], *q_sent)
-    going, gain_grads, sum_two, *kv_sent = together(going, gain_grads, sum_two, *kv_sent)
+    going, gain_grads, sum_two, three, *kv_sent = together(
+        going, gain_grads, sum_two, three, *kv_sent
+    )
     gain_grads = gain_grads + permute(gain_grads, CHIP[2])
     grad_tokens = place_all(home_in_turn, going.reshape(8, -1, width), row_total, f32)
     part_kv = added(kv_parts[0], *kv_sent)
     sum_one = jnp.concatenate([part_q, part_kv], axis=2)
     sum_one = added(sum_one[0], permute(sum_one[1], MIDDLE))
-    three = added(three, permute(three, OVER_Y))
+    three = added(three, permute(three, OVER_Y_HOME))
     sum_two = from_middle(sum_two)
     sum_one, sum_two, three, gain_grads = together(sum_one, sum_two, three, gain_grads)
     sum_two = jnp.concatenate(in_order(y == 0, sum_two, permute(sum_two, OVER_Y)), axis=0)
@@ -1295,27 +1331,33 @@
     total = jnp.where(at_home, three, permute(three, SIBLING)).astype(f32)
     sum_one, sum_two, gain_grads = together(sum_one, sum_two, gain_grads)
     gain_grads = gain_grads + permute(gain_grads, MIDDLE)
-    gate_up = jnp.stack(in_order(core == 0, sum_two, permute(sum_two, SIBLING)), axis=1)
-    gate_up = gate_up.reshape(-1, 2, 4, 2, ff).astype(f32)
-    one_halves = in_order(core == 0, sum_one, permute(sum_one, SIBLING))
-    query_halves = [part[:, :1024] for part in one_halves]
-    kv_halves = [part[:, 1024:] for part in one_halves]
-    kv_grad = jnp.concatenate(kv_halves, axis=1).reshape(-1, 8, 2, HEAD_SIZE).astype(f32)
-
+    shard = sum_two.shape[0]
+    gate_grad, up_grad = whole_call(
+        gate_up_kernel,
+        "gate_up_gradients",
+        (info, sum_two, permute(sum_two, SIBLING)),
+        [((shard, 8 * ff), f32)] * 2,
+    )
+    query_grad, key_grad, value_grad = whole_call(
+        attn_weights_kernel,
+        "attn_weight_gradients",
+        (info, sum_one, permute(sum_one, SIBLING)),
+        [((shard, 2048), f32), ((shard, 1024), f32), ((shard, 1024), f32)],
+    )
     gain_grads = gain_grads.reshape(-1)
     return (
         outcome,
         grad_tokens,
         gain_grads[:width],
-        jnp.concatenate(query_halves, axis=1).astype(f32),
-        kv_grad[:, :, 0].reshape(-1, 1024),
-        kv_grad[:, :, 1].reshape(-1, 1024),
+        query_grad,
+        key_grad,
+        value_grad,
         gain_grads[2 * width : 2 * width + HEAD_SIZE],
         gain_grads[2 * width + HEAD_SIZE :],
         total[3 * RUN :],
         gain_grads[width : 2 * width],
-        gate_up[:, :, :, 0].reshape(-1, 8 * ff),
-        gate_up[:, :, :, 1].reshape(-1, 8 * ff),
+        gate_grad,
+        up_grad,
         total[: 3 * RUN],
     )
 

time: 741 us -> 705 us (0.951)
  waiting for transfers between devices: 302 us -> 266 us
    ppermute x76, waiting for transfers between devices: 302 us -> 266 us  [permute(): return lax.ppermute(a, AXES, pairs)]
    pallas_call x9 -> x11, Pallas kernels: 31 us -> 36.9 us  [whole_call(): pl.pallas_call(kernel, in_specs=[smem if a.dtype == jnp.int32 else vmem f...]
    unnamed x142 -> x156, local copies, waits for them, and re-layouts: 16.7 us -> 14.3 us
  transfers between devices with their start and end apart: 79 -> 79, of which waited for: 30 -> 28; matrix products, arithmetic and copies ran while one was open for 18% -> 19% of each run, Pallas kernels for 15% -> 17%
where the time goes in v3:
time: 705 us; the launch traced here: 698 us
  waiting for transfers between devices  266 us (38%)
  Pallas kernels  163 us (23%)
  starting transfers between devices  112 us (16%)
  other arithmetic  61.8 us (9%)
  local copies, waits for them, and re-layouts  47.3 us (7%)
  matrix products  45.4 us (6%)
    ppermute x76, waiting for transfers between devices, permute(): return lax.ppermute(a, AXES, pairs)  266 us
    ppermute x76, starting transfers between devices, permute(): return lax.ppermute(a, AXES, pairs)  99.3 us
    pallas_call x1, Pallas kernels, attn_bwd(): pl.pallas_call(attn_bwd_kernel, grid_spec=pltpu.PrefetchScalarGridSpec(nu...  45.6 us
    pallas_call x1, Pallas kernels, mlp(): pl.pallas_call(mlp_kernel, grid_spec=pltpu.PrefetchScalarGridSpec(num_sca...  39.1 us
    pallas_call x11, Pallas kernels, whole_call(): pl.pallas_call(kernel, in_specs=[smem if a.dtype == jnp.int32 else vmem f...  36.9 us
    dot_general x5, matrix products, tn(): lax.dot_general(a, b, (((0,), (0,)), ((), ())), preferred_element_type=f32)  34.6 us
    pallas_call x2, Pallas kernels, project(): pl.pallas_call(kernel, grid_spec=pltpu.PrefetchScalarGridSpec(num_scalar_...  21.2 us
    pallas_call x1, Pallas kernels, attn_fwd(): pl.pallas_call(attn_fwd_kernel, grid_spec=pltpu.PrefetchScalarGridSpec(nu...  19.8 us
  transfers between devices with their start and end apart: 79, of which 28 were waited for; matrix products, arithmetic and copies ran while one was open for 19% of the time, Pallas kernels for 17%

profile of v3, /device:TPU:0, one launch (start us, length us, event | category | flops | bytes accessed | tf_op | source)
XLA Modules:
  0.0 697.7 jit_solution(12572369749405471694)
XLA Ops:
  24.5 7.7 %collective-permute-start.7 = (bf16[80,1024]{1,0:T(8,128)(2,1)S(1)}, bf16[80,1024]{1,0:T(8,128)(2,1)S(1)}, u32[]{:S(2)}, u32[]{:S(2)}) collective-permute-start(bf16[80,1024]{1,0:T(8,128)(2,1)S(1)} %copy-done.67), channel_id=1, source_target_pairs={{0,11},{1,10},{2,9},{3,8},{4,3},{5,2},{6,1},{7,0},{8,15},{9,14},{1... | collective-permute-start | bytes 491528 | tf_op jit(solution)/shard_map/ppermute | solution.py:1016
  41.2 5.5 collective-permute-start.13
  64.1 6.7 collective-permute-done.13.refs_4_
  81.9 23.9 %collective-permute-done.12.refs_3_ = bf16[128,2048]{1,0:T(8,128)(2,1)} collective-permute-done((bf16[128,2048]{1,0:T(8,128)(2,1)S(1)}, bf16[128,2048]{1,0:T(8,128)(2,1)}, u32[]{:S(2)}, u32[]{:S(2)}) %collective-permute-start.12) | collective-permute-done | bytes 524320 | tf_op jit(solution)/shard_map/ppermute | solution.py:1016
  105.8 5.6 collective-permute-done.15.refs_6_
  111.5 8.0 %collective-permute-done.16.refs_7_ = bf16[128,2048]{1,0:T(8,128)(2,1)} collective-permute-done((bf16[128,2048]{1,0:T(8,128)(2,1)S(1)}, bf16[128,2048]{1,0:T(8,128)(2,1)}, u32[]{:S(2)}, u32[]{:S(2)}) %collective-permute-start.16) | collective-permute-done | bytes 524320 | tf_op jit(solution)/shard_map/ppermute | solution.py:1016
  130.7 9.8 %key_value.1 = (bf16[1152,1024]{1,0:T(8,128)(2,1)}, f32[1152,512]{1,0:T(8,128)}, bf16[1024,1024]{1,0:T(8,128)(2,1)}, bf16[256,1024]{1,0:T(8,128)(2,1)}) custom-call(s32[5]{0:T(128)} %stack.129.info, bf16[1152,1024]{1,0:T(8,128)(2,1)} %pad_maximum_fusion.h_ref, bf16[128,2048]{1,0:T(8,128)(2,1)} %copy-done.16, bf16[128,2048]{1,0:T(8,128)(2,1)} %copy-done.23, ...), custom_call_target="tpu_custom_call" | custom-call | tf_op jit(solution)/shard_map/key_value/pallas_call | solution.py:625
  146.3 7.1 %collective-permute-done.20.refs_2_ = bf16[64,3072]{1,0:T(8,128)(2,1)S(1)} collective-permute-done((bf16[64,3072]{1,0:T(8,128)(2,1)}, bf16[64,3072]{1,0:T(8,128)(2,1)S(1)}, u32[]{:S(2)}, u32[]{:S(2)}) %collective-permute-start.20) | collective-permute-done | bytes 393248 | tf_op jit(solution)/shard_map/ppermute | solution.py:1016
  153.5 6.6 collective-permute-done.21.refs_3_
  167.6 11.3 %query.1 = (bf16[1152,1024]{1,0:T(8,128)(2,1)}, f32[1152,1024]{1,0:T(8,128)}, bf16[1024,1024]{1,0:T(8,128)(2,1)}) custom-call(s32[5]{0:T(128)} %stack.129.info, bf16[1152,1024]{1,0:T(8,128)(2,1)} %pad_maximum_fusion.h_ref, bf16[128,2048]{1,0:T(8,128)(2,1)} %copy-done.16, bf16[128,2048]{1,0:T(8,128)(2,1)} %copy-done.23, bf16[128,2048]{1,0:T(8,128)(2,1)} %copy-done.24, ...), custom_call_target="tpu_custom_call" | custom-call | tf_op jit(solution)/shard_map/query/pallas_call | solution.py:625
  182.4 26.7 %collective-permute-done.24.p1 = bf16[256,1024]{1,0:T(8,128)(2,1)} collective-permute-done((bf16[256,1024]{1,0:T(8,128)(2,1)}, bf16[256,1024]{1,0:T(8,128)(2,1)}, u32[]{:S(2)}, u32[]{:S(2)}) %collective-permute-start.24) | collective-permute-done | bytes 524320 | tf_op jit(solution)/shard_map/ppermute | solution.py:1016
  212.6 19.8 %attn_fwd.1 = (bf16[1152,1024]{1,0:T(8,128)(2,1)}, f32[4,8,1280]{2,1,0:T(8,128)}) custom-call(s32[5]{0:T(128)} %stack.129.info, bf16[1152,1024]{1,0:T(8,128)(2,1)} %get-tuple-element.197.q_ref, bf16[1152,1024]{1,0:T(8,128)(2,1)} %get-tuple-element.198.kv_ref, bf16[256,1024]{1,0:T(8,128)(2,1)} %get-tuple-element.199.p0, ...), custom_call_target="tpu_custom_call" | custom-call | flops 20000000000 | bytes 10000000 | tf_op jit(solution)/shard_map/attn_fwd/pallas_call | solution.py:717
  239.3 6.8 out_projection.1
  259.4 15.2 %collective-permute-done.33.refs_11_ = bf16[384,1024]{1,0:T(8,128)(2,1)S(1)} collective-permute-done((bf16[384,1024]{1,0:T(8,128)(2,1)}, bf16[384,1024]{1,0:T(8,128)(2,1)S(1)}, u32[]{:S(2)}, u32[]{:S(2)}) %collective-permute-start.33) | collective-permute-done | bytes 786464 | tf_op jit(solution)/shard_map/ppermute | solution.py:1016
  274.7 16.5 %collective-permute-done.35.refs_13_ = bf16[384,1024]{1,0:T(8,128)(2,1)S(1)} collective-permute-done((bf16[384,1024]{1,0:T(8,128)(2,1)}, bf16[384,1024]{1,0:T(8,128)(2,1)S(1)}, u32[]{:S(2)}, u32[]{:S(2)}) %collective-permute-start.35) | collective-permute-done | bytes 786464 | tf_op jit(solution)/shard_map/ppermute | solution.py:1016
  297.9 39.1 %feed_forward.1 = (bf16[1152,1536]{1,0:T(8,128)(2,1)}, bf16[1152,3072]{1,0:T(8,128)(2,1)}, f32[576,1024]{1,0:T(8,128)}, bf16[576,1024]{1,0:T(8,128)(2,1)}, f32[5...) custom-call(s32[5]{0:T(128)} %stack.129.info, bf16[576,1024]{1,0:T(8,128)(2,1)} %copy-done.28, ...), custom_call_target="tpu_custom_call" | custom-call | flops 38000001024 | bytes 10000000 | tf_op jit(solution)/shard_map/feed_forward/pallas_call | solution.py:898
  337.6 12.3 %convolution_convert_fusion = bf16[1024,3072]{1,0:T(8,128)(2,1)S(1)} fusion(bf16[1152,3072]{1,0:T(8,128)(2,1)} %get-tuple-element.239, bf16[576,1024]{1,0:T(8,128)(2,1)} %collective-permute-done.36.h_sib, bf16[576,1024]{1,0:T(8,128)(2,1)} %copy-done.28), kind=kOutput, calls=%fused_computation.1 | convolution fusion | flops 7255621632 | bytes 15728640 | tf_op jit(solution)/shard_map/dot_general | solution.py:466
  360.7 7.0 %convolution_convert_fusion.2 = bf16[1536,1024]{1,0:T(8,128)(2,1)} fusion(bf16[1152,1536]{1,0:T(8,128)(2,1)S(1)} %copy-done.71, bf16[576,1024]{1,0:T(8,128)(2,1)} %collective-permute-done.37.g_sib, bf16[576,1024]{1,0:T(8,128)(2,1)S(1)} %copy-done.13), kind=kOutput, calls=%fused_computation.4 | convolution fusion | flops 3630170112 | bytes 9043968 | tf_op jit(solution)/shard_map/dot_general | solution.py:466
  384.7 5.5 convolution_convert_fusion.1.refs_0_
  390.2 45.6 %attn_bwd.1 = (bf16[1152,1024]{1,0:T(8,128)(2,1)}, bf16[1152,1024]{1,0:T(8,128)(2,1)}, bf16[256,1024]{1,0:T(8,128)(2,1)}, bf16[256,1024]{1,0:T(8,128)(2,1)}, bf1...) custom-call(s32[5]{0:T(128)} %stack.129.info, bf16[1152,1024]{1,0:T(8,128)(2,1)} %get-tuple-element.197.q_ref, ...), custom_call_target="tpu_custom_call" | custom-call | flops 44999999488 | bytes 10000000 | tf_op jit(solution)/shard_map/attn_bwd/pallas_call | solution.py:801
  446.8 10.8 %collective-permute-done.45.d1 = bf16[256,1024]{1,0:T(8,128)(2,1)} collective-permute-done((bf16[256,1024]{1,0:T(8,128)(2,1)}, bf16[256,1024]{1,0:T(8,128)(2,1)}, u32[]{:S(2)}, u32[]{:S(2)}) %collective-permute-start.45) | collective-permute-done | bytes 524320 | tf_op jit(solution)/shard_map/ppermute | solution.py:1016
  460.4 9.6 %collective-permute-done.47.d3 = bf16[256,1024]{1,0:T(8,128)(2,1)} collective-permute-done((bf16[256,1024]{1,0:T(8,128)(2,1)}, bf16[256,1024]{1,0:T(8,128)(2,1)}, u32[]{:S(2)}, u32[]{:S(2)}) %collective-permute-start.47) | collective-permute-done | bytes 524320 | tf_op jit(solution)/shard_map/ppermute | solution.py:1016
  488.8 5.7 prompt_back.1
  494.5 6.1 convolution_convert_fusion.3
  506.0 18.1 %collective-permute-done.48 = bf16[2,2,64,3072]{3,2,0,1:T(8,128)(2,1)} collective-permute-done((bf16[2,2,64,3072]{3,2,0,1:T(8,128)(2,1)}, bf16[2,2,64,3072]{3,2,0,1:T(8,128)(2,1)}, u32[]{:S(2)}, u32[]{:S(2)}) %collective-permute-start.48) | collective-permute-done | bytes 1572896 | tf_op jit(solution)/shard_map/ppermute | solution.py:1016
  563.3 18.4 %collective-permute-done.61 = bf16[640,1024]{1,0:T(8,128)(2,1)} collective-permute-done((bf16[640,1024]{1,0:T(8,128)(2,1)}, bf16[640,1024]{1,0:T(8,128)(2,1)}, u32[]{:S(2)}, u32[]{:S(2)}) %collective-permute-start.61) | collective-permute-done | bytes 1310752 | tf_op jit(solution)/shard_map/ppermute | solution.py:1016
  598.5 24.0 %collective-permute-done.60 = bf16[2,64,3072]{2,1,0:T(8,128)(2,1)S(1)} collective-permute-done((bf16[2,64,3072]{2,1,0:T(8,128)(2,1)S(1)}, bf16[2,64,3072]{2,1,0:T(8,128)(2,1)S(1)}, u32[]{:S(2)}, u32[]{:S(2)}) %collective-permute-start.60) | collective-permute-done | bytes 786464 | tf_op jit(solution)/shard_map/ppermute | solution.py:1016
  624.0 4.9 collective-permute-done.64
  638.4 18.2 %collective-permute-done.65 = bf16[64,2048]{1,0:T(8,128)(2,1)S(1)} collective-permute-done((bf16[64,2048]{1,0:T(8,128)(2,1)S(1)}, bf16[64,2048]{1,0:T(8,128)(2,1)S(1)}, u32[]{:S(2)}, u32[]{:S(2)}) %collective-permute-start.65) | collective-permute-done | bytes 262176 | tf_op jit(solution)/shard_map/ppermute | solution.py:1016
  656.7 8.3 %collective-permute-done.66 = bf16[64,3072]{1,0:T(8,128)(2,1)S(1)} collective-permute-done((bf16[64,3072]{1,0:T(8,128)(2,1)S(1)}, bf16[64,3072]{1,0:T(8,128)(2,1)S(1)}, u32[]{:S(2)}, u32[]{:S(2)}) %collective-permute-start.66) | collective-permute-done | bytes 393248 | tf_op jit(solution)/shard_map/ppermute | solution.py:1016
  668.6 6.5 collective-permute-done.71
  676.2 6.4 collective-permute-done.70
  (423 shorter events, 271.6 us)
Async XLA Ops:
  41.2 33.1 %collective-permute-start.8 = (bf16[576,1024]{1,0:T(8,128)(2,1)}, bf16[576,1024]{1,0:T(8,128)(2,1)}, u32[]{:S(2)}, u32[]{:S(2)}) collective-permute-start(bf16[576,1024]{1,0:T(8,128)(2,1)} %get-tuple-element.174), channel_id=1, source_target_pairs={{0,8},{1,9},{2,10},{3,11},{4,12},{5,13},{6,14},{7,15},{8,0},{9,1},... | collective-permute-start | bytes 3538952 | tf_op jit(solution)/shard_map/ppermute | solution.py:1016
  59.2 60.2 %collective-permute-start.9 = (bf16[640,1024]{1,0:T(8,128)(2,1)}, bf16[640,1024]{1,0:T(8,128)(2,1)}, u32[]{:S(2)}, u32[]{:S(2)}) collective-permute-start(bf16[640,1024]{1,0:T(8,128)(2,1)} %pad_maximum_fusion.4), channel_id=1, source_target_pairs={{0,4},{1,5},{2,6},{3,7},{12,8},{13,9},{14,10},{15,11},{16,20},{17,... | collective-permute-start | bytes 3932168 | tf_op jit(solution)/shard_map/ppermute | solution.py:1016
  70.8 35.1 %collective-permute-start.12 = (bf16[128,2048]{1,0:T(8,128)(2,1)S(1)}, bf16[128,2048]{1,0:T(8,128)(2,1)}, u32[]{:S(2)}, u32[]{:S(2)}) collective-permute-start(bf16[128,2048]{1,0:T(8,128)(2,1)S(1)} %constant_dynamic-update-slice_fusion.refs_0_), channel_id=1, source_target_pairs={{0,3},{1,2},{2,1},{3,0},{4,7},{5,6},{6,5},{7,4},{8,11},{9,10},{10,... | collective-permute-start | bytes 1572872 | tf_op jit(solution)/shard_map/ppermute | solution.py:1016
  70.8 35.0 %collective-permute-start.14 = (bf16[128,2048]{1,0:T(8,128)(2,1)S(1)}, bf16[128,2048]{1,0:T(8,128)(2,1)}, u32[]{:S(2)}, u32[]{:S(2)}) collective-permute-start(bf16[128,2048]{1,0:T(8,128)(2,1)S(1)} %collective-permute-done.13.refs_4_), channel_id=1, source_target_pairs={{0,1},{1,0},{2,3},{3,2},{4,5},{5,4},{6,7},{7,6},{8,9},{9,8},{10,11... | collective-permute-start | bytes 1572872 | tf_op jit(solution)/shard_map/ppermute | solution.py:1016
  71.7 39.7 %collective-permute-start.15 = (bf16[128,2048]{1,0:T(8,128)(2,1)S(1)}, bf16[128,2048]{1,0:T(8,128)(2,1)}, u32[]{:S(2)}, u32[]{:S(2)}) collective-permute-start(bf16[128,2048]{1,0:T(8,128)(2,1)S(1)} %collective-permute-done.13.refs_4_), channel_id=1, source_target_pairs={{0,2},{1,3},{2,0},{3,1},{4,6},{5,7},{6,4},{7,5},{8,10},{9,11},{10,... | collective-permute-start | bytes 1572872 | tf_op jit(solution)/shard_map/ppermute | solution.py:1016
  74.3 45.1 %collective-permute-start.16 = (bf16[128,2048]{1,0:T(8,128)(2,1)S(1)}, bf16[128,2048]{1,0:T(8,128)(2,1)}, u32[]{:S(2)}, u32[]{:S(2)}) collective-permute-start(bf16[128,2048]{1,0:T(8,128)(2,1)S(1)} %collective-permute-done.13.refs_4_), channel_id=1, source_target_pairs={{0,3},{1,2},{2,1},{3,0},{4,7},{5,6},{6,5},{7,4},{8,11},{9,10},{10,... | collective-permute-start | bytes 1572872 | tf_op jit(solution)/shard_map/ppermute | solution.py:1016
  125.2 34.9 %collective-permute-start.21 = (bf16[64,3072]{1,0:T(8,128)(2,1)}, bf16[64,3072]{1,0:T(8,128)(2,1)}, u32[]{:S(2)}, u32[]{:S(2)}) collective-permute-start(bf16[64,3072]{1,0:T(8,128)(2,1)} %dynamic-slice_bitcast_fusion.11.refs_0_), channel_id=1, source_target_pairs={{0,3},{1,2},{2,1},{3,0},{4,7},{5,6},{6,5},{7,4},{8,11},{9,10},{10,... | collective-permute-start | bytes 1179656 | tf_op jit(solution)/shard_map/ppermute | solution.py:1016
  162.0 47.0 %collective-permute-start.23 = (bf16[2,256,1024]{2,1,0:T(8,128)(2,1)S(1)}, bf16[2,256,1024]{2,1,0:T(8,128)(2,1)}, u32[]{:S(2)}, u32[]{:S(2)}) collective-permute-start(bf16[2,256,1024]{2,1,0:T(8,128)(2,1)S(1)} %pad_maximum_fusion.6.refs_0_), channel_id=1, source_target_pairs={{0,1},{1,0},{2,3},{3,2},{4,5},{5,4},{6,7},{7,6},{8,9},{9,8},{10,11... | collective-permute-start | bytes 3145736 | tf_op jit(solution)/shard_map/ppermute | solution.py:1016
  164.1 45.0 %collective-permute-start.24 = (bf16[256,1024]{1,0:T(8,128)(2,1)}, bf16[256,1024]{1,0:T(8,128)(2,1)}, u32[]{:S(2)}, u32[]{:S(2)}) collective-permute-start(bf16[256,1024]{1,0:T(8,128)(2,1)} %get-tuple-element.199.p0), channel_id=1, source_target_pairs={{0,1},{1,0},{2,3},{3,2},{4,5},{5,4},{6,7},{7,6},{8,9},{9,8},{10,11... | collective-permute-start | bytes 1572872 | tf_op jit(solution)/shard_map/ppermute | solution.py:1016
  165.1 44.0 %collective-permute-start.25 = (bf16[256,1024]{1,0:T(8,128)(2,1)}, bf16[256,1024]{1,0:T(8,128)(2,1)}, u32[]{:S(2)}, u32[]{:S(2)}) collective-permute-start(bf16[256,1024]{1,0:T(8,128)(2,1)} %get-tuple-element.199.p0), channel_id=1, source_target_pairs={{0,2},{1,3},{2,0},{3,1},{4,6},{5,7},{6,4},{7,5},{8,10},{9,11},{10,... | collective-permute-start | bytes 1572872 | tf_op jit(solution)/shard_map/ppermute | solution.py:1016
  165.3 43.7 %collective-permute-start.26 = (bf16[256,1024]{1,0:T(8,128)(2,1)}, bf16[256,1024]{1,0:T(8,128)(2,1)}, u32[]{:S(2)}, u32[]{:S(2)}) collective-permute-start(bf16[256,1024]{1,0:T(8,128)(2,1)} %get-tuple-element.199.p0), channel_id=1, source_target_pairs={{0,3},{1,2},{2,1},{3,0},{4,7},{5,6},{6,5},{7,4},{8,11},{9,10},{10,... | collective-permute-start | bytes 1572872 | tf_op jit(solution)/shard_map/ppermute | solution.py:1016
  180.6 51.9 %collective-permute-start.30 = (bf16[4,64,3072]{2,1,0:T(8,128)(2,1)S(1)}, bf16[4,64,3072]{2,1,0:T(8,128)(2,1)}, u32[]{:S(2)}, u32[]{:S(2)}) collective-permute-start(bf16[4,64,3072]{2,1,0:T(8,128)(2,1)S(1)} %pad_maximum_fusion.2), channel_id=1, source_target_pairs={{0,16},{1,17},{2,18},{3,19},{4,20},{5,21},{6,22},{7,23},{8,24},{9,... | collective-permute-start | bytes 4718600 | tf_op jit(solution)/shard_map/ppermute | solution.py:1016
  234.6 57.5 %all-to-all-start = ((bf16[8,80,1024]{2,1,0:T(8,128)(2,1)}), bf16[8,80,1024]{2,1,0:T(8,128)(2,1)}, u32[]{:S(2)}, u32[]{:S(2)}) async-start(bf16[8,80,1024]{2,1,0:T(8,128)(2,1)} %pad_maximum_fusion.5), calls=%async_computation | async-start | bytes 2621440 | tf_op jit(solution)/shard_map/all_to_all | solution.py:1193
  249.1 42.0 %collective-permute-start.32 = (bf16[4,64,3072]{2,1,0:T(8,128)(2,1)}, bf16[4,64,3072]{2,1,0:T(8,128)(2,1)}, u32[]{:S(2)}, u32[]{:S(2)}) collective-permute-start(bf16[4,64,3072]{2,1,0:T(8,128)(2,1)} %pad_maximum_fusion.3), channel_id=1, source_target_pairs={{0,16},{1,17},{2,18},{3,19},{4,20},{5,21},{6,22},{7,23},{8,24},{9,... | collective-permute-start | bytes 4718600 | tf_op jit(solution)/shard_map/ppermute | solution.py:1016
  254.4 36.7 %collective-permute-start.35 = (bf16[384,1024]{1,0:T(8,128)(2,1)}, bf16[384,1024]{1,0:T(8,128)(2,1)S(1)}, u32[]{:S(2)}, u32[]{:S(2)}) collective-permute-start(bf16[384,1024]{1,0:T(8,128)(2,1)} %slice.128.refs_10_), channel_id=1, source_target_pairs={{0,3},{1,2},{2,1},{3,0},{4,7},{5,6},{6,5},{7,4},{8,11},{9,10},{10,... | collective-permute-start | bytes 2359304 | tf_op jit(solution)/shard_map/ppermute | solution.py:1016
  359.1 87.6 %collective-permute-start.44 = (bf16[2,2,2,64,3072]{4,3,0,1,2:T(8,128)(2,1)}, bf16[2,2,2,64,3072]{4,3,0,1,2:T(8,128)(2,1)}, u32[]{:S(2)}, u32[]{:S(2)}) collective-permute-start(bf16[2,2,2,64,3072]{4,3,0,1,2:T(8,128)(2,1)} %bitcast.155), channel_id=1, source_target_pairs={{0,16},{1,17},{2,18},{3,19},{4,20},{5,21},{6,22},{7,23},{8,24},{9,... | collective-permute-start | bytes 9437192 | tf_op jit(solution)/shard_map/ppermute | solution.py:1016
  378.9 56.9 %collective-permute-start.41 = (bf16[2,384,1024]{2,1,0:T(8,128)(2,1)}, bf16[2,384,1024]{2,1,0:T(8,128)(2,1)}, u32[]{:S(2)}, u32[]{:S(2)}) collective-permute-start(bf16[2,384,1024]{2,1,0:T(8,128)(2,1)} %dynamic-slice_bitcast_fusion.1), channel_id=1, source_target_pairs={{0,1},{1,0},{2,3},{3,2},{4,5},{5,4},{6,7},{7,6},{8,9},{9,8},{10,11... | collective-permute-start | bytes 4718600 | tf_op jit(solution)/shard_map/ppermute | solution.py:1016
  379.5 56.2 %collective-permute-start.42 = (bf16[2,256,1024]{2,1,0:T(8,128)(2,1)S(1)}, bf16[2,256,1024]{2,1,0:T(8,128)(2,1)}, u32[]{:S(2)}, u32[]{:S(2)}) collective-permute-start(bf16[2,256,1024]{2,1,0:T(8,128)(2,1)S(1)} %dynamic-slice_bitcast_fusion.6), channel_id=1, source_target_pairs={{0,2},{1,3},{2,0},{3,1},{4,6},{5,7},{6,4},{7,5},{8,10},{9,11},{10,... | collective-permute-start | bytes 3145736 | tf_op jit(solution)/shard_map/ppermute | solution.py:1016
  380.1 55.7 %all-to-all-start.1 = ((bf16[8,80,1024]{2,1,0:T(8,128)(2,1)}), bf16[8,80,1024]{2,1,0:T(8,128)(2,1)}, u32[]{:S(2)}, u32[]{:S(2)}) async-start(bf16[8,80,1024]{2,1,0:T(8,128)(2,1)} %deal_all.2), calls=%async_computation.1 | async-start | bytes 2621440 | tf_op jit(solution)/shard_map/all_to_all | solution.py:1193
  471.0 60.7 %collective-permute-start.52 = (bf16[640,1024]{1,0:T(8,128)(2,1)}, bf16[640,1024]{1,0:T(8,128)(2,1)}, u32[]{:S(2)}, u32[]{:S(2)}) collective-permute-start(bf16[640,1024]{1,0:T(8,128)(2,1)} %bitcast.56), channel_id=1, source_target_pairs={{4,8},{5,9},{6,10},{7,11},{8,4},{9,5},{10,6},{11,7},{20,24},{21,25... | collective-permute-start | bytes 3932168 | tf_op jit(solution)/shard_map/ppermute | solution.py:1016
  475.6 52.8 %collective-permute-start.51 = (bf16[256,1024]{1,0:T(8,128)(2,1)}, bf16[256,1024]{1,0:T(8,128)(2,1)S(1)}, u32[]{:S(2)}, u32[]{:S(2)}) collective-permute-start(bf16[256,1024]{1,0:T(8,128)(2,1)} %dynamic-slice_bitcast_fusion.9), channel_id=1, source_target_pairs={{0,1},{1,0},{2,3},{3,2},{4,5},{5,4},{6,7},{7,6},{8,9},{9,8},{10,11... | collective-permute-start | bytes 1572872 | tf_op jit(solution)/shard_map/ppermute | solution.py:1016
  480.4 48.9 %collective-permute-start.50 = (bf16[384,1024]{1,0:T(8,128)(2,1)}, bf16[384,1024]{1,0:T(8,128)(2,1)}, u32[]{:S(2)}, u32[]{:S(2)}) collective-permute-start(bf16[384,1024]{1,0:T(8,128)(2,1)} %dynamic-slice_bitcast_fusion.8), channel_id=1, source_target_pairs={{0,2},{1,3},{2,0},{3,1},{4,6},{5,7},{6,4},{7,5},{8,10},{9,11},{10,... | collective-permute-start | bytes 2359304 | tf_op jit(solution)/shard_map/ppermute | solution.py:1016
  487.9 36.2 %collective-permute-start.48 = (bf16[2,2,64,3072]{3,2,0,1:T(8,128)(2,1)}, bf16[2,2,64,3072]{3,2,0,1:T(8,128)(2,1)}, u32[]{:S(2)}, u32[]{:S(2)}) collective-permute-start(bf16[2,2,64,3072]{3,2,0,1:T(8,128)(2,1)} %dynamic-slice_bitcast_fusion), channel_id=1, source_target_pairs={{0,1},{1,0},{2,3},{3,2},{4,5},{5,4},{6,7},{7,6},{8,9},{9,8},{10,11... | collective-permute-start | bytes 4718600 | tf_op jit(solution)/shard_map/ppermute | solution.py:1016
  540.2 47.6 %all-to-all-start.2 = ((bf16[8,80,1024]{2,1,0:T(8,128)(2,1)}), bf16[8,80,1024]{2,1,0:T(8,128)(2,1)S(1)}, u32[]{:S(2)}, u32[]{:S(2)}) async-start(bf16[8,80,1024]{2,1,0:T(8,128)(2,1)} %deal_all.3), calls=%async_computation.2 | async-start | bytes 2621440 | tf_op jit(solution)/shard_map/all_to_all | solution.py:1193
  546.8 34.9 %collective-permute-start.61 = (bf16[640,1024]{1,0:T(8,128)(2,1)}, bf16[640,1024]{1,0:T(8,128)(2,1)}, u32[]{:S(2)}, u32[]{:S(2)}) collective-permute-start(bf16[640,1024]{1,0:T(8,128)(2,1)} %constant_dynamic-update-slice_fusion.2), channel_id=1, source_target_pairs={{4,0},{5,1},{6,2},{7,3},{8,12},{9,13},{10,14},{11,15},{20,16},{21,... | collective-permute-start | bytes 3932168 | tf_op jit(solution)/shard_map/ppermute | solution.py:1016
  552.1 35.8 %collective-permute-start.54 = (bf16[8,64,1024]{2,1,0:T(8,128)(2,1)}, bf16[8,64,1024]{2,1,0:T(8,128)(2,1)}, u32[]{:S(2)}, u32[]{:S(2)}) collective-permute-start(bf16[8,64,1024]{2,1,0:T(8,128)(2,1)} %get-tuple-element.330), channel_id=1, source_target_pairs={{0,16},{1,17},{2,18},{3,19},{4,20},{5,21},{6,22},{7,23},{8,24},{9,... | collective-permute-start | bytes 3145736 | tf_op jit(solution)/shard_map/ppermute | solution.py:1016
  587.9 34.6 %collective-permute-start.60 = (bf16[2,64,3072]{2,1,0:T(8,128)(2,1)S(1)}, bf16[2,64,3072]{2,1,0:T(8,128)(2,1)S(1)}, u32[]{:S(2)}, u32[]{:S(2)}) collective-permute-start(bf16[2,64,3072]{2,1,0:T(8,128)(2,1)S(1)} %dynamic-slice_bitcast_fusion.7), channel_id=1, source_target_pairs={{0,2},{1,3},{2,0},{3,1},{4,6},{5,7},{6,4},{7,5},{8,10},{9,11},{10,... | collective-permute-start | bytes 2359304 | tf_op jit(solution)/shard_map/ppermute | solution.py:1016
  588.0 34.7 %collective-permute-start.58 = (bf16[640,1024]{1,0:T(8,128)(2,1)S(1)}, bf16[640,1024]{1,0:T(8,128)(2,1)S(1)}, u32[]{:S(2)}, u32[]{:S(2)}) collective-permute-start(bf16[640,1024]{1,0:T(8,128)(2,1)S(1)} %bitcast.157), channel_id=1, source_target_pairs={{4,8},{5,9},{6,10},{7,11},{8,4},{9,5},{10,6},{11,7},{20,24},{21,25... | collective-permute-start | bytes 3932168 | tf_op jit(solution)/shard_map/ppermute | solution.py:1016
  591.1 37.9 %collective-permute-start.64 = (bf16[2,64,1024]{2,1,0:T(8,128)(2,1)S(1)}, bf16[2,64,1024]{2,1,0:T(8,128)(2,1)S(1)}, u32[]{:S(2)}, u32[]{:S(2)}) collective-permute-start(bf16[2,64,1024]{2,1,0:T(8,128)(2,1)S(1)} %pad_maximum_fusion.19), channel_id=1, source_target_pairs={{0,3},{1,2},{2,1},{3,0},{4,7},{5,6},{6,5},{7,4},{8,11},{9,10},{10,... | collective-permute-start | bytes 786440 | tf_op jit(solution)/shard_map/ppermute | solution.py:1016
  594.0 38.3 %collective-permute-start.63 = (bf16[2,64,1024]{2,1,0:T(8,128)(2,1)S(1)}, bf16[2,64,1024]{2,1,0:T(8,128)(2,1)S(1)}, u32[]{:S(2)}, u32[]{:S(2)}) collective-permute-start(bf16[2,64,1024]{2,1,0:T(8,128)(2,1)S(1)} %pad_maximum_fusion.18), channel_id=1, source_target_pairs={{0,2},{1,3},{2,0},{3,1},{4,6},{5,7},{6,4},{7,5},{8,10},{9,11},{10,... | collective-permute-start | bytes 786440 | tf_op jit(solution)/shard_map/ppermute | solution.py:1016
  597.9 34.5 %collective-permute-start.62 = (bf16[2,64,1024]{2,1,0:T(8,128)(2,1)S(1)}, bf16[2,64,1024]{2,1,0:T(8,128)(2,1)S(1)}, u32[]{:S(2)}, u32[]{:S(2)}) collective-permute-start(bf16[2,64,1024]{2,1,0:T(8,128)(2,1)S(1)} %pad_maximum_fusion.17), channel_id=1, source_target_pairs={{0,1},{1,0},{2,3},{3,2},{4,5},{5,4},{6,7},{7,6},{8,9},{9,8},{10,11... | collective-permute-start | bytes 786440 | tf_op jit(solution)/shard_map/ppermute | solution.py:1016
  632.3 32.7 %collective-permute-start.67 = (bf16[640,1024]{1,0:T(8,128)(2,1)S(1)}, bf16[640,1024]{1,0:T(8,128)(2,1)S(1)}, u32[]{:S(2)}, u32[]{:S(2)}) collective-permute-start(bf16[640,1024]{1,0:T(8,128)(2,1)S(1)} %copy-done.12), channel_id=1, source_target_pairs={{0,16},{1,17},{2,18},{3,19},{12,28},{13,29},{14,30},{15,31},{16,0}... | collective-permute-start | bytes 3932168 | tf_op jit(solution)/shard_map/ppermute | solution.py:1016
  (119 other events, 1550.4 us)

commit v4 on v3

--- a/solution.py
+++ b/solution.py
@@ -1143,15 +1143,12 @@
 
     inputs_low, first_low = place_norm(arrive, arrived, norm1_gain.reshape(1, width), row_total)
     hidden_one = both(first_low)
-    own_two, own_three, out_grad = together(
-        own_two, jnp.concatenate([w_down, w_out], axis=0), out_grad, first_low
-    )[:3]
-    middle_three = permute(own_three, MIDDLE_OUT)
-    hidden_one, middle_three, own_two, out_grad, *one = together(
-        hidden_one, middle_three, own_two, out_grad, *one
-    )
-    home_three = jnp.where(at_home, own_three, middle_three)
-    home_down, home_out = home_three[: 3 * RUN], home_three[3 * RUN :]
+    own_two, w_out, w_down, out_grad = together(own_two, w_out, w_down, out_grad, first_low)[:4]
+    middle_out = permute(after(w_out, one[:4]), MIDDLE_OUT)
+    hidden_one, middle_out, own_two, w_down, out_grad, *one = together(
+        hidden_one, middle_out, own_two, w_down, out_grad, *one
+    )
+    home_out = jnp.where(at_home, w_out, middle_out)
 
     two = around(own_two)
     middle_two = permute(own_two, MIDDLE)
@@ -1167,14 +1164,16 @@
     outs = [outs, permute(outs, CHIP[1])]
     grad_here = regrouped(out_grad)
     q, rawq, w_q = project(query_kernel, "query", info, hidden_q, one, 0, qg, cos, sin, 256, 0)
-    q, grad_here, middle_two, home_down, *rest = together(
-        q, grad_here, middle_two, home_down, *outs, *prompt
+    q, grad_here, middle_two, w_down, *rest = together(
+        q, grad_here, middle_two, w_down, *outs, *prompt
     )
     outs, prompt = rest[:2], rest[2:]
 
     two += around(middle_two)
     other_two = [permute(jnp.stack(two[:4]), OVER_Y)]
+    middle_down = permute(w_down, MIDDLE_OUT)
     mixed, lse = attn_fwd(info, q, kv, prompt)
+    home_down = jnp.where(at_home, w_down, middle_down)
     mixed, home_down, grad_here, *rest = together(mixed, home_down, grad_here, *two, *other_two)
     two, other_two = rest[:8], rest[8:]
 

time: 705 us -> 693 us (0.983)
  local copies, waits for them, and re-layouts: 47.3 us -> 39.4 us
    ppermute x76 -> x77, starting transfers between devices: 99.3 us -> 97.5 us  [permute(): return lax.ppermute(a, AXES, pairs)]
    unnamed x156 -> x136, local copies, waits for them, and re-layouts: 14.3 us -> 13.9 us
    ppermute x76 -> x77, waiting for transfers between devices: 266 us -> 266 us  [permute(): return lax.ppermute(a, AXES, pairs)]
  transfers between devices with their start and end apart: 79 -> 80, of which waited for: 28 -> 31; matrix products, arithmetic and copies ran while one was open for 19% -> 18% of each run, Pallas kernels for 17% -> 17%
where the time goes in v4:
time: 693 us; the launch traced here: 686 us
  waiting for transfers between devices  266 us (38%)
  Pallas kernels  163 us (24%)
  starting transfers between devices  111 us (16%)
  other arithmetic  60.1 us (9%)
  matrix products  45.3 us (7%)
  local copies, waits for them, and re-layouts  39.4 us (6%)
    ppermute x77, waiting for transfers between devices, permute(): return lax.ppermute(a, AXES, pairs)  266 us
    ppermute x77, starting transfers between devices, permute(): return lax.ppermute(a, AXES, pairs)  97.5 us
    pallas_call x1, Pallas kernels, attn_bwd(): pl.pallas_call(attn_bwd_kernel, grid_spec=pltpu.PrefetchScalarGridSpec(nu...  45.6 us
    pallas_call x1, Pallas kernels, mlp(): pl.pallas_call(mlp_kernel, grid_spec=pltpu.PrefetchScalarGridSpec(num_sca...  39.1 us
    pallas_call x11, Pallas kernels, whole_call(): pl.pallas_call(kernel, in_specs=[smem if a.dtype == jnp.int32 else vmem f...  36.9 us
    dot_general x5, matrix products, tn(): lax.dot_general(a, b, (((0,), (0,)), ((), ())), preferred_element_type=f32)  34.5 us
    pallas_call x2, Pallas kernels, project(): pl.pallas_call(kernel, grid_spec=pltpu.PrefetchScalarGridSpec(num_scalar_...  21.1 us
    pallas_call x1, Pallas kernels, attn_fwd(): pl.pallas_call(attn_fwd_kernel, grid_spec=pltpu.PrefetchScalarGridSpec(nu...  19.8 us
  transfers between devices with their start and end apart: 80, of which 31 were waited for; matrix products, arithmetic and copies ran while one was open for 18% of the time, Pallas kernels for 17%

profile of v4, /device:TPU:0, one launch (start us, length us, event | category | flops | bytes accessed | tf_op | source)
XLA Modules:
  0.0 686.1 jit_solution(9619161437959844333)
XLA Ops:
  44.7 17.5 %collective-permute-done.10.refs_2_ = bf16[128,2048]{1,0:T(8,128)(2,1)S(1)} collective-permute-done((bf16[128,2048]{1,0:T(8,128)(2,1)S(1)}, bf16[128,2048]{1,0:T(8,128)(2,1)S(1)}, u32[]{:S(2)}, u32[]{:S(2)}) %collective-permute-start.10) | collective-permute-done | bytes 524320 | tf_op jit(solution)/shard_map/ppermute | solution.py:1016
  62.2 10.2 %collective-permute-done.11.refs_3_ = bf16[128,2048]{1,0:T(8,128)(2,1)S(1)} collective-permute-done((bf16[128,2048]{1,0:T(8,128)(2,1)S(1)}, bf16[128,2048]{1,0:T(8,128)(2,1)S(1)}, u32[]{:S(2)}, u32[]{:S(2)}) %collective-permute-start.11) | collective-permute-done | bytes 524320 | tf_op jit(solution)/shard_map/ppermute | solution.py:1016
  86.6 9.6 %collective-permute-done.15.refs_6_ = bf16[128,2048]{1,0:T(8,128)(2,1)} collective-permute-done((bf16[128,2048]{1,0:T(8,128)(2,1)}, bf16[128,2048]{1,0:T(8,128)(2,1)}, u32[]{:S(2)}, u32[]{:S(2)}) %collective-permute-start.15) | collective-permute-done | bytes 524320 | tf_op jit(solution)/shard_map/ppermute | solution.py:1016
  96.2 8.5 %collective-permute-done.16.refs_7_ = bf16[128,2048]{1,0:T(8,128)(2,1)} collective-permute-done((bf16[128,2048]{1,0:T(8,128)(2,1)}, bf16[128,2048]{1,0:T(8,128)(2,1)}, u32[]{:S(2)}, u32[]{:S(2)}) %collective-permute-start.16) | collective-permute-done | bytes 524320 | tf_op jit(solution)/shard_map/ppermute | solution.py:1016
  105.3 5.4 collective-permute-start.18
  116.5 9.7 %key_value.1 = (bf16[1152,1024]{1,0:T(8,128)(2,1)}, f32[1152,512]{1,0:T(8,128)}, bf16[1024,1024]{1,0:T(8,128)(2,1)}, bf16[256,1024]{1,0:T(8,128)(2,1)}) custom-call(s32[5]{0:T(128)} %stack.129.info, bf16[1152,1024]{1,0:T(8,128)(2,1)} %pad_maximum_fusion.h_ref, bf16[128,2048]{1,0:T(8,128)(2,1)} %copy-done.14, bf16[128,2048]{1,0:T(8,128)(2,1)} %copy-done.22, ...), custom_call_target="tpu_custom_call" | custom-call | tf_op jit(solution)/shard_map/key_value/pallas_call | solution.py:625
  129.4 7.1 %collective-permute-done.20.refs_2_ = bf16[64,3072]{1,0:T(8,128)(2,1)S(1)} collective-permute-done((bf16[64,3072]{1,0:T(8,128)(2,1)S(1)}, bf16[64,3072]{1,0:T(8,128)(2,1)S(1)}, u32[]{:S(2)}, u32[]{:S(2)}) %collective-permute-start.20) | collective-permute-done | bytes 393248 | tf_op jit(solution)/shard_map/ppermute | solution.py:1016
  136.5 5.6 collective-permute-done.21.refs_3_
  148.4 11.5 %query.1 = (bf16[1152,1024]{1,0:T(8,128)(2,1)}, f32[1152,1024]{1,0:T(8,128)}, bf16[1024,1024]{1,0:T(8,128)(2,1)}) custom-call(s32[5]{0:T(128)} %stack.129.info, bf16[1152,1024]{1,0:T(8,128)(2,1)} %pad_maximum_fusion.h_ref, bf16[128,2048]{1,0:T(8,128)(2,1)} %copy-done.14, bf16[128,2048]{1,0:T(8,128)(2,1)} %copy-done.22, bf16[128,2048]{1,0:T(8,128)(2,1)} %copy-done.20, ...), custom_call_target="tpu_custom_call" | custom-call | tf_op jit(solution)/shard_map/query/pallas_call | solution.py:625
  163.2 25.2 %collective-permute-done.24.p1 = bf16[256,1024]{1,0:T(8,128)(2,1)} collective-permute-done((bf16[256,1024]{1,0:T(8,128)(2,1)}, bf16[256,1024]{1,0:T(8,128)(2,1)}, u32[]{:S(2)}, u32[]{:S(2)}) %collective-permute-start.24) | collective-permute-done | bytes 524320 | tf_op jit(solution)/shard_map/ppermute | solution.py:1016
  192.0 8.1 %collective-permute-start.27 = (bf16[384,1024]{1,0:T(8,128)(2,1)}, bf16[384,1024]{1,0:T(8,128)(2,1)S(1)}, u32[]{:S(2)}, u32[]{:S(2)}) collective-permute-start(bf16[384,1024]{1,0:T(8,128)(2,1)} %param.26), channel_id=1, source_target_pairs={{0,4},{1,5},{2,6},{3,7},{12,8},{13,9},{14,10},{15,11},{16,20},{17,... | collective-permute-start | bytes 2359304 | tf_op jit(solution)/shard_map/ppermute | solution.py:1016
  200.2 19.8 %attn_fwd.1 = (bf16[1152,1024]{1,0:T(8,128)(2,1)}, f32[4,8,1280]{2,1,0:T(8,128)}) custom-call(s32[5]{0:T(128)} %stack.129.info, bf16[1152,1024]{1,0:T(8,128)(2,1)} %get-tuple-element.203.q_ref, bf16[1152,1024]{1,0:T(8,128)(2,1)} %get-tuple-element.204.kv_ref, bf16[256,1024]{1,0:T(8,128)(2,1)} %get-tuple-element.205.p0, ...), custom_call_target="tpu_custom_call" | custom-call | flops 20000000000 | bytes 10000000 | tf_op jit(solution)/shard_map/attn_fwd/pallas_call | solution.py:717
  228.2 6.7 out_projection.1
  248.3 15.2 %collective-permute-done.34.refs_11_ = bf16[384,1024]{1,0:T(8,128)(2,1)S(1)} collective-permute-done((bf16[384,1024]{1,0:T(8,128)(2,1)}, bf16[384,1024]{1,0:T(8,128)(2,1)S(1)}, u32[]{:S(2)}, u32[]{:S(2)}) %collective-permute-start.34) | collective-permute-done | bytes 786464 | tf_op jit(solution)/shard_map/ppermute | solution.py:1016
  263.6 16.5 %collective-permute-done.36.refs_13_ = bf16[384,1024]{1,0:T(8,128)(2,1)S(1)} collective-permute-done((bf16[384,1024]{1,0:T(8,128)(2,1)}, bf16[384,1024]{1,0:T(8,128)(2,1)S(1)}, u32[]{:S(2)}, u32[]{:S(2)}) %collective-permute-start.36) | collective-permute-done | bytes 786464 | tf_op jit(solution)/shard_map/ppermute | solution.py:1016
  286.7 39.1 %feed_forward.1 = (bf16[1152,1536]{1,0:T(8,128)(2,1)}, bf16[1152,3072]{1,0:T(8,128)(2,1)}, f32[576,1024]{1,0:T(8,128)}, bf16[576,1024]{1,0:T(8,128)(2,1)}, f32[5...) custom-call(s32[5]{0:T(128)} %stack.129.info, bf16[576,1024]{1,0:T(8,128)(2,1)} %copy-done.28, ...), custom_call_target="tpu_custom_call" | custom-call | flops 38000001024 | bytes 10000000 | tf_op jit(solution)/shard_map/feed_forward/pallas_call | solution.py:898
  326.4 12.3 %convolution_convert_fusion = bf16[1024,3072]{1,0:T(8,128)(2,1)S(1)} fusion(bf16[1152,3072]{1,0:T(8,128)(2,1)} %get-tuple-element.245, bf16[576,1024]{1,0:T(8,128)(2,1)} %collective-permute-done.37.h_sib, bf16[576,1024]{1,0:T(8,128)(2,1)} %copy-done.28), kind=kOutput, calls=%fused_computation.1 | convolution fusion | flops 7255621632 | bytes 15728640 | tf_op jit(solution)/shard_map/dot_general | solution.py:466
  349.4 7.0 %convolution_convert_fusion.2 = bf16[1536,1024]{1,0:T(8,128)(2,1)} fusion(bf16[1152,1536]{1,0:T(8,128)(2,1)S(1)} %copy-done.61, bf16[576,1024]{1,0:T(8,128)(2,1)} %collective-permute-done.38.g_sib, bf16[576,1024]{1,0:T(8,128)(2,1)S(1)} %copy-done.11), kind=kOutput, calls=%fused_computation.4 | convolution fusion | flops 3630170112 | bytes 9043968 | tf_op jit(solution)/shard_map/dot_general | solution.py:466
  373.3 5.5 convolution_convert_fusion.1.refs_0_
  378.8 45.6 %attn_bwd.1 = (bf16[1152,1024]{1,0:T(8,128)(2,1)}, bf16[1152,1024]{1,0:T(8,128)(2,1)}, bf16[256,1024]{1,0:T(8,128)(2,1)}, bf16[256,1024]{1,0:T(8,128)(2,1)}, bf1...) custom-call(s32[5]{0:T(128)} %stack.129.info, bf16[1152,1024]{1,0:T(8,128)(2,1)} %get-tuple-element.203.q_ref, ...), custom_call_target="tpu_custom_call" | custom-call | flops 44999999488 | bytes 10000000 | tf_op jit(solution)/shard_map/attn_bwd/pallas_call | solution.py:801
  435.5 10.8 %collective-permute-done.46.d1 = bf16[256,1024]{1,0:T(8,128)(2,1)} collective-permute-done((bf16[256,1024]{1,0:T(8,128)(2,1)}, bf16[256,1024]{1,0:T(8,128)(2,1)}, u32[]{:S(2)}, u32[]{:S(2)}) %collective-permute-start.46) | collective-permute-done | bytes 524320 | tf_op jit(solution)/shard_map/ppermute | solution.py:1016
  449.1 9.6 %collective-permute-done.48.d3 = bf16[256,1024]{1,0:T(8,128)(2,1)} collective-permute-done((bf16[256,1024]{1,0:T(8,128)(2,1)}, bf16[256,1024]{1,0:T(8,128)(2,1)}, u32[]{:S(2)}, u32[]{:S(2)}) %collective-permute-start.48) | collective-permute-done | bytes 524320 | tf_op jit(solution)/shard_map/ppermute | solution.py:1016
  477.4 5.7 prompt_back.1
  483.2 6.1 convolution_convert_fusion.3
  494.7 18.7 %collective-permute-done.49 = bf16[2,2,64,3072]{3,2,0,1:T(8,128)(2,1)} collective-permute-done((bf16[2,2,64,3072]{3,2,0,1:T(8,128)(2,1)}, bf16[2,2,64,3072]{3,2,0,1:T(8,128)(2,1)}, u32[]{:S(2)}, u32[]{:S(2)}) %collective-permute-start.49) | collective-permute-done | bytes 1572896 | tf_op jit(solution)/shard_map/ppermute | solution.py:1016
  550.8 19.4 %collective-permute-done.62 = bf16[640,1024]{1,0:T(8,128)(2,1)} collective-permute-done((bf16[640,1024]{1,0:T(8,128)(2,1)}, bf16[640,1024]{1,0:T(8,128)(2,1)}, u32[]{:S(2)}, u32[]{:S(2)}) %collective-permute-start.62) | collective-permute-done | bytes 1310752 | tf_op jit(solution)/shard_map/ppermute | solution.py:1016
  587.0 24.0 %collective-permute-done.61 = bf16[2,64,3072]{2,1,0:T(8,128)(2,1)S(1)} collective-permute-done((bf16[2,64,3072]{2,1,0:T(8,128)(2,1)S(1)}, bf16[2,64,3072]{2,1,0:T(8,128)(2,1)S(1)}, u32[]{:S(2)}, u32[]{:S(2)}) %collective-permute-start.61) | collective-permute-done | bytes 786464 | tf_op jit(solution)/shard_map/ppermute | solution.py:1016
  612.5 4.9 collective-permute-done.65
  626.9 18.1 %collective-permute-done.66 = bf16[64,2048]{1,0:T(8,128)(2,1)S(1)} collective-permute-done((bf16[64,2048]{1,0:T(8,128)(2,1)S(1)}, bf16[64,2048]{1,0:T(8,128)(2,1)S(1)}, u32[]{:S(2)}, u32[]{:S(2)}) %collective-permute-start.66) | collective-permute-done | bytes 262176 | tf_op jit(solution)/shard_map/ppermute | solution.py:1016
  645.1 8.3 %collective-permute-done.67 = bf16[64,3072]{1,0:T(8,128)(2,1)S(1)} collective-permute-done((bf16[64,3072]{1,0:T(8,128)(2,1)S(1)}, bf16[64,3072]{1,0:T(8,128)(2,1)S(1)}, u32[]{:S(2)}, u32[]{:S(2)}) %collective-permute-start.67) | collective-permute-done | bytes 393248 | tf_op jit(solution)/shard_map/ppermute | solution.py:1016
  657.0 6.5 collective-permute-done.72
  664.6 6.4 collective-permute-done.71
  (403 shorter events, 259.2 us)
Async XLA Ops:
  29.3 32.8 %collective-permute-start.10 = (bf16[128,2048]{1,0:T(8,128)(2,1)S(1)}, bf16[128,2048]{1,0:T(8,128)(2,1)S(1)}, u32[]{:S(2)}, u32[]{:S(2)}) collective-permute-start(bf16[128,2048]{1,0:T(8,128)(2,1)S(1)} %constant_dynamic-update-slice_fusion.refs_0_), channel_id=1, source_target_pairs={{0,2},{1,3},{2,0},{3,1},{4,6},{5,7},{6,4},{7,5},{8,10},{9,11},{10,... | collective-permute-start | bytes 1572872 | tf_op jit(solution)/shard_map/ppermute | solution.py:1016
  33.9 38.5 %collective-permute-start.11 = (bf16[128,2048]{1,0:T(8,128)(2,1)S(1)}, bf16[128,2048]{1,0:T(8,128)(2,1)S(1)}, u32[]{:S(2)}, u32[]{:S(2)}) collective-permute-start(bf16[128,2048]{1,0:T(8,128)(2,1)S(1)} %constant_dynamic-update-slice_fusion.refs_0_), channel_id=1, source_target_pairs={{0,3},{1,2},{2,1},{3,0},{4,7},{5,6},{6,5},{7,4},{8,11},{9,10},{10,... | collective-permute-start | bytes 1572872 | tf_op jit(solution)/shard_map/ppermute | solution.py:1016
  35.6 36.8 %collective-permute-start.9 = (bf16[128,2048]{1,0:T(8,128)(2,1)S(1)}, bf16[128,2048]{1,0:T(8,128)(2,1)S(1)}, u32[]{:S(2)}, u32[]{:S(2)}) collective-permute-start(bf16[128,2048]{1,0:T(8,128)(2,1)S(1)} %constant_dynamic-update-slice_fusion.refs_0_), channel_id=1, source_target_pairs={{0,1},{1,0},{2,3},{3,2},{4,5},{5,4},{6,7},{7,6},{8,9},{9,8},{10,11... | collective-permute-start | bytes 1572872 | tf_op jit(solution)/shard_map/ppermute | solution.py:1016
  37.9 36.8 %collective-permute-start.13 = (bf16[128,2048]{1,0:T(8,128)(2,1)S(1)}, bf16[128,2048]{1,0:T(8,128)(2,1)}, u32[]{:S(2)}, u32[]{:S(2)}) collective-permute-start(bf16[128,2048]{1,0:T(8,128)(2,1)S(1)} %constant_dynamic-update-slice_fusion.refs_0_), channel_id=1, source_target_pairs={{0,4},{1,5},{2,6},{3,7},{4,0},{5,1},{6,2},{7,3},{8,12},{9,13},{10,... | collective-permute-start | bytes 1572872 | tf_op jit(solution)/shard_map/ppermute | solution.py:1016
  42.3 39.8 %collective-permute-start.8 = (bf16[576,1024]{1,0:T(8,128)(2,1)}, bf16[576,1024]{1,0:T(8,128)(2,1)}, u32[]{:S(2)}, u32[]{:S(2)}) collective-permute-start(bf16[576,1024]{1,0:T(8,128)(2,1)} %get-tuple-element.177), channel_id=1, source_target_pairs={{0,8},{1,9},{2,10},{3,11},{4,12},{5,13},{6,14},{7,15},{8,0},{9,1},... | collective-permute-start | bytes 3538952 | tf_op jit(solution)/shard_map/ppermute | solution.py:1016
  143.8 44.6 %collective-permute-start.23 = (bf16[2,256,1024]{2,1,0:T(8,128)(2,1)S(1)}, bf16[2,256,1024]{2,1,0:T(8,128)(2,1)}, u32[]{:S(2)}, u32[]{:S(2)}) collective-permute-start(bf16[2,256,1024]{2,1,0:T(8,128)(2,1)S(1)} %pad_maximum_fusion.5.refs_0_), channel_id=1, source_target_pairs={{0,1},{1,0},{2,3},{3,2},{4,5},{5,4},{6,7},{7,6},{8,9},{9,8},{10,11... | collective-permute-start | bytes 3145736 | tf_op jit(solution)/shard_map/ppermute | solution.py:1016
  144.9 43.5 %collective-permute-start.24 = (bf16[256,1024]{1,0:T(8,128)(2,1)}, bf16[256,1024]{1,0:T(8,128)(2,1)}, u32[]{:S(2)}, u32[]{:S(2)}) collective-permute-start(bf16[256,1024]{1,0:T(8,128)(2,1)} %get-tuple-element.205.p0), channel_id=1, source_target_pairs={{0,1},{1,0},{2,3},{3,2},{4,5},{5,4},{6,7},{7,6},{8,9},{9,8},{10,11... | collective-permute-start | bytes 1572872 | tf_op jit(solution)/shard_map/ppermute | solution.py:1016
  145.9 42.6 %collective-permute-start.25 = (bf16[256,1024]{1,0:T(8,128)(2,1)}, bf16[256,1024]{1,0:T(8,128)(2,1)}, u32[]{:S(2)}, u32[]{:S(2)}) collective-permute-start(bf16[256,1024]{1,0:T(8,128)(2,1)} %get-tuple-element.205.p0), channel_id=1, source_target_pairs={{0,2},{1,3},{2,0},{3,1},{4,6},{5,7},{6,4},{7,5},{8,10},{9,11},{10,... | collective-permute-start | bytes 1572872 | tf_op jit(solution)/shard_map/ppermute | solution.py:1016
  146.2 42.3 %collective-permute-start.26 = (bf16[256,1024]{1,0:T(8,128)(2,1)}, bf16[256,1024]{1,0:T(8,128)(2,1)}, u32[]{:S(2)}, u32[]{:S(2)}) collective-permute-start(bf16[256,1024]{1,0:T(8,128)(2,1)} %get-tuple-element.205.p0), channel_id=1, source_target_pairs={{0,3},{1,2},{2,1},{3,0},{4,7},{5,6},{6,5},{7,4},{8,11},{9,10},{10,... | collective-permute-start | bytes 1572872 | tf_op jit(solution)/shard_map/ppermute | solution.py:1016
  161.5 60.6 %collective-permute-start.31 = (bf16[4,64,3072]{2,1,0:T(8,128)(2,1)S(1)}, bf16[4,64,3072]{2,1,0:T(8,128)(2,1)}, u32[]{:S(2)}, u32[]{:S(2)}) collective-permute-start(bf16[4,64,3072]{2,1,0:T(8,128)(2,1)S(1)} %pad_maximum_fusion.2), channel_id=1, source_target_pairs={{0,16},{1,17},{2,18},{3,19},{4,20},{5,21},{6,22},{7,23},{8,24},{9,... | collective-permute-start | bytes 4718600 | tf_op jit(solution)/shard_map/ppermute | solution.py:1016
  188.4 33.6 %collective-permute-start.28 = (bf16[64,3072]{1,0:T(8,128)(2,1)}, bf16[64,3072]{1,0:T(8,128)(2,1)}, u32[]{:S(2)}, u32[]{:S(2)}) collective-permute-start(bf16[64,3072]{1,0:T(8,128)(2,1)} %collective-permute-done.18.refs_4_), channel_id=1, source_target_pairs={{0,1},{1,0},{2,3},{3,2},{4,5},{5,4},{6,7},{7,6},{8,9},{9,8},{10,11... | collective-permute-start | bytes 1179656 | tf_op jit(solution)/shard_map/ppermute | solution.py:1016
  189.1 33.0 %collective-permute-start.29 = (bf16[64,3072]{1,0:T(8,128)(2,1)}, bf16[64,3072]{1,0:T(8,128)(2,1)}, u32[]{:S(2)}, u32[]{:S(2)}) collective-permute-start(bf16[64,3072]{1,0:T(8,128)(2,1)} %collective-permute-done.18.refs_4_), channel_id=1, source_target_pairs={{0,2},{1,3},{2,0},{3,1},{4,6},{5,7},{6,4},{7,5},{8,10},{9,11},{10,... | collective-permute-start | bytes 1179656 | tf_op jit(solution)/shard_map/ppermute | solution.py:1016
  189.1 33.0 %collective-permute-start.30 = (bf16[64,3072]{1,0:T(8,128)(2,1)}, bf16[64,3072]{1,0:T(8,128)(2,1)}, u32[]{:S(2)}, u32[]{:S(2)}) collective-permute-start(bf16[64,3072]{1,0:T(8,128)(2,1)} %collective-permute-done.18.refs_4_), channel_id=1, source_target_pairs={{0,3},{1,2},{2,1},{3,0},{4,7},{5,6},{6,5},{7,4},{8,11},{9,10},{10,... | collective-permute-start | bytes 1179656 | tf_op jit(solution)/shard_map/ppermute | solution.py:1016
  223.5 57.4 %all-to-all-start = ((bf16[8,80,1024]{2,1,0:T(8,128)(2,1)}), bf16[8,80,1024]{2,1,0:T(8,128)(2,1)}, u32[]{:S(2)}, u32[]{:S(2)}) async-start(bf16[8,80,1024]{2,1,0:T(8,128)(2,1)} %pad_maximum_fusion.4), calls=%async_computation | async-start | bytes 2621440 | tf_op jit(solution)/shard_map/all_to_all | solution.py:1192
  238.1 42.0 %collective-permute-start.33 = (bf16[4,64,3072]{2,1,0:T(8,128)(2,1)}, bf16[4,64,3072]{2,1,0:T(8,128)(2,1)}, u32[]{:S(2)}, u32[]{:S(2)}) collective-permute-start(bf16[4,64,3072]{2,1,0:T(8,128)(2,1)} %pad_maximum_fusion.3), channel_id=1, source_target_pairs={{0,16},{1,17},{2,18},{3,19},{4,20},{5,21},{6,22},{7,23},{8,24},{9,... | collective-permute-start | bytes 4718600 | tf_op jit(solution)/shard_map/ppermute | solution.py:1016
  243.4 36.6 %collective-permute-start.36 = (bf16[384,1024]{1,0:T(8,128)(2,1)}, bf16[384,1024]{1,0:T(8,128)(2,1)S(1)}, u32[]{:S(2)}, u32[]{:S(2)}) collective-permute-start(bf16[384,1024]{1,0:T(8,128)(2,1)} %broadcast_select_fusion.3.refs_10_), channel_id=1, source_target_pairs={{0,3},{1,2},{2,1},{3,0},{4,7},{5,6},{6,5},{7,4},{8,11},{9,10},{10,... | collective-permute-start | bytes 2359304 | tf_op jit(solution)/shard_map/ppermute | solution.py:1016
  347.8 87.7 %collective-permute-start.45 = (bf16[2,2,2,64,3072]{4,3,0,1,2:T(8,128)(2,1)}, bf16[2,2,2,64,3072]{4,3,0,1,2:T(8,128)(2,1)}, u32[]{:S(2)}, u32[]{:S(2)}) collective-permute-start(bf16[2,2,2,64,3072]{4,3,0,1,2:T(8,128)(2,1)} %bitcast.154), channel_id=1, source_target_pairs={{0,16},{1,17},{2,18},{3,19},{4,20},{5,21},{6,22},{7,23},{8,24},{9,... | collective-permute-start | bytes 9437192 | tf_op jit(solution)/shard_map/ppermute | solution.py:1016
  367.6 56.8 %collective-permute-start.42 = (bf16[2,384,1024]{2,1,0:T(8,128)(2,1)}, bf16[2,384,1024]{2,1,0:T(8,128)(2,1)}, u32[]{:S(2)}, u32[]{:S(2)}) collective-permute-start(bf16[2,384,1024]{2,1,0:T(8,128)(2,1)} %dynamic-slice_bitcast_fusion.1), channel_id=1, source_target_pairs={{0,1},{1,0},{2,3},{3,2},{4,5},{5,4},{6,7},{7,6},{8,9},{9,8},{10,11... | collective-permute-start | bytes 4718600 | tf_op jit(solution)/shard_map/ppermute | solution.py:1016
  368.2 56.1 %collective-permute-start.43 = (bf16[2,256,1024]{2,1,0:T(8,128)(2,1)S(1)}, bf16[2,256,1024]{2,1,0:T(8,128)(2,1)}, u32[]{:S(2)}, u32[]{:S(2)}) collective-permute-start(bf16[2,256,1024]{2,1,0:T(8,128)(2,1)S(1)} %dynamic-slice_bitcast_fusion.6), channel_id=1, source_target_pairs={{0,2},{1,3},{2,0},{3,1},{4,6},{5,7},{6,4},{7,5},{8,10},{9,11},{10,... | collective-permute-start | bytes 3145736 | tf_op jit(solution)/shard_map/ppermute | solution.py:1016
  368.6 55.7 %all-to-all-start.1 = ((bf16[8,80,1024]{2,1,0:T(8,128)(2,1)}), bf16[8,80,1024]{2,1,0:T(8,128)(2,1)}, u32[]{:S(2)}, u32[]{:S(2)}) async-start(bf16[8,80,1024]{2,1,0:T(8,128)(2,1)} %deal_all.2), calls=%async_computation.1 | async-start | bytes 2621440 | tf_op jit(solution)/shard_map/all_to_all | solution.py:1192
  459.7 60.5 %collective-permute-start.53 = (bf16[640,1024]{1,0:T(8,128)(2,1)}, bf16[640,1024]{1,0:T(8,128)(2,1)}, u32[]{:S(2)}, u32[]{:S(2)}) collective-permute-start(bf16[640,1024]{1,0:T(8,128)(2,1)} %bitcast.56), channel_id=1, source_target_pairs={{4,8},{5,9},{6,10},{7,11},{8,4},{9,5},{10,6},{11,7},{20,24},{21,25... | collective-permute-start | bytes 3932168 | tf_op jit(solution)/shard_map/ppermute | solution.py:1016
  464.3 52.6 %collective-permute-start.52 = (bf16[256,1024]{1,0:T(8,128)(2,1)}, bf16[256,1024]{1,0:T(8,128)(2,1)S(1)}, u32[]{:S(2)}, u32[]{:S(2)}) collective-permute-start(bf16[256,1024]{1,0:T(8,128)(2,1)} %dynamic-slice_bitcast_fusion.9), channel_id=1, source_target_pairs={{0,1},{1,0},{2,3},{3,2},{4,5},{5,4},{6,7},{7,6},{8,9},{9,8},{10,11... | collective-permute-start | bytes 1572872 | tf_op jit(solution)/shard_map/ppermute | solution.py:1016
  469.1 48.8 %collective-permute-start.51 = (bf16[384,1024]{1,0:T(8,128)(2,1)}, bf16[384,1024]{1,0:T(8,128)(2,1)}, u32[]{:S(2)}, u32[]{:S(2)}) collective-permute-start(bf16[384,1024]{1,0:T(8,128)(2,1)} %dynamic-slice_bitcast_fusion.8), channel_id=1, source_target_pairs={{0,2},{1,3},{2,0},{3,1},{4,6},{5,7},{6,4},{7,5},{8,10},{9,11},{10,... | collective-permute-start | bytes 2359304 | tf_op jit(solution)/shard_map/ppermute | solution.py:1016
  476.6 36.8 %collective-permute-start.49 = (bf16[2,2,64,3072]{3,2,0,1:T(8,128)(2,1)}, bf16[2,2,64,3072]{3,2,0,1:T(8,128)(2,1)}, u32[]{:S(2)}, u32[]{:S(2)}) collective-permute-start(bf16[2,2,64,3072]{3,2,0,1:T(8,128)(2,1)} %dynamic-slice_bitcast_fusion), channel_id=1, source_target_pairs={{0,1},{1,0},{2,3},{3,2},{4,5},{5,4},{6,7},{7,6},{8,9},{9,8},{10,11... | collective-permute-start | bytes 4718600 | tf_op jit(solution)/shard_map/ppermute | solution.py:1016
  528.7 47.6 %all-to-all-start.2 = ((bf16[8,80,1024]{2,1,0:T(8,128)(2,1)}), bf16[8,80,1024]{2,1,0:T(8,128)(2,1)S(1)}, u32[]{:S(2)}, u32[]{:S(2)}) async-start(bf16[8,80,1024]{2,1,0:T(8,128)(2,1)} %deal_all.3), calls=%async_computation.2 | async-start | bytes 2621440 | tf_op jit(solution)/shard_map/all_to_all | solution.py:1192
  535.3 34.9 %collective-permute-start.62 = (bf16[640,1024]{1,0:T(8,128)(2,1)}, bf16[640,1024]{1,0:T(8,128)(2,1)}, u32[]{:S(2)}, u32[]{:S(2)}) collective-permute-start(bf16[640,1024]{1,0:T(8,128)(2,1)} %constant_dynamic-update-slice_fusion.2), channel_id=1, source_target_pairs={{4,0},{5,1},{6,2},{7,3},{8,12},{9,13},{10,14},{11,15},{20,16},{21,... | collective-permute-start | bytes 3932168 | tf_op jit(solution)/shard_map/ppermute | solution.py:1016
  540.6 35.8 %collective-permute-start.55 = (bf16[8,64,1024]{2,1,0:T(8,128)(2,1)}, bf16[8,64,1024]{2,1,0:T(8,128)(2,1)}, u32[]{:S(2)}, u32[]{:S(2)}) collective-permute-start(bf16[8,64,1024]{2,1,0:T(8,128)(2,1)} %get-tuple-element.336), channel_id=1, source_target_pairs={{0,16},{1,17},{2,18},{3,19},{4,20},{5,21},{6,22},{7,23},{8,24},{9,... | collective-permute-start | bytes 3145736 | tf_op jit(solution)/shard_map/ppermute | solution.py:1016
  576.4 34.6 %collective-permute-start.61 = (bf16[2,64,3072]{2,1,0:T(8,128)(2,1)S(1)}, bf16[2,64,3072]{2,1,0:T(8,128)(2,1)S(1)}, u32[]{:S(2)}, u32[]{:S(2)}) collective-permute-start(bf16[2,64,3072]{2,1,0:T(8,128)(2,1)S(1)} %dynamic-slice_bitcast_fusion.7), channel_id=1, source_target_pairs={{0,2},{1,3},{2,0},{3,1},{4,6},{5,7},{6,4},{7,5},{8,10},{9,11},{10,... | collective-permute-start | bytes 2359304 | tf_op jit(solution)/shard_map/ppermute | solution.py:1016
  576.5 34.7 %collective-permute-start.59 = (bf16[640,1024]{1,0:T(8,128)(2,1)S(1)}, bf16[640,1024]{1,0:T(8,128)(2,1)S(1)}, u32[]{:S(2)}, u32[]{:S(2)}) collective-permute-start(bf16[640,1024]{1,0:T(8,128)(2,1)S(1)} %bitcast.156), channel_id=1, source_target_pairs={{4,8},{5,9},{6,10},{7,11},{8,4},{9,5},{10,6},{11,7},{20,24},{21,25... | collective-permute-start | bytes 3932168 | tf_op jit(solution)/shard_map/ppermute | solution.py:1016
  579.6 37.9 %collective-permute-start.65 = (bf16[2,64,1024]{2,1,0:T(8,128)(2,1)S(1)}, bf16[2,64,1024]{2,1,0:T(8,128)(2,1)S(1)}, u32[]{:S(2)}, u32[]{:S(2)}) collective-permute-start(bf16[2,64,1024]{2,1,0:T(8,128)(2,1)S(1)} %pad_maximum_fusion.18), channel_id=1, source_target_pairs={{0,3},{1,2},{2,1},{3,0},{4,7},{5,6},{6,5},{7,4},{8,11},{9,10},{10,... | collective-permute-start | bytes 786440 | tf_op jit(solution)/shard_map/ppermute | solution.py:1016
  582.5 38.3 %collective-permute-start.64 = (bf16[2,64,1024]{2,1,0:T(8,128)(2,1)S(1)}, bf16[2,64,1024]{2,1,0:T(8,128)(2,1)S(1)}, u32[]{:S(2)}, u32[]{:S(2)}) collective-permute-start(bf16[2,64,1024]{2,1,0:T(8,128)(2,1)S(1)} %pad_maximum_fusion.17), channel_id=1, source_target_pairs={{0,2},{1,3},{2,0},{3,1},{4,6},{5,7},{6,4},{7,5},{8,10},{9,11},{10,... | collective-permute-start | bytes 786440 | tf_op jit(solution)/shard_map/ppermute | solution.py:1016
  586.4 34.5 %collective-permute-start.63 = (bf16[2,64,1024]{2,1,0:T(8,128)(2,1)S(1)}, bf16[2,64,1024]{2,1,0:T(8,128)(2,1)S(1)}, u32[]{:S(2)}, u32[]{:S(2)}) collective-permute-start(bf16[2,64,1024]{2,1,0:T(8,128)(2,1)S(1)} %pad_maximum_fusion.16), channel_id=1, source_target_pairs={{0,1},{1,0},{2,3},{3,2},{4,5},{5,4},{6,7},{7,6},{8,9},{9,8},{10,11... | collective-permute-start | bytes 786440 | tf_op jit(solution)/shard_map/ppermute | solution.py:1016
  (110 other events, 1489.1 us)

commit v5 on v4

--- a/solution.py
+++ b/solution.py
@@ -1263,10 +1263,10 @@
     )
 
     prompt_parts = [prompt_parts[0]] + [permute(prompt_parts[t], CHIP[t]) for t in range(1, 4)]
-    grad_wq = tn(hidden_one, grad_q).astype(bf16).reshape(8, 2, 64, -1)
+    grad_wq = tn(hidden_one, after(grad_q, prompt_parts[1])).astype(bf16).reshape(8, 2, 64, -1)
     keep_q, send_q = pick(grad_wq, y, 1), permute(pick(grad_wq, 1 - y, 1), OVER_Y)
-    grad_q, keep_q, send_q, send_down, send_out, send_two, leaving, *prompt_parts = together(
-        grad_q, keep_q, send_q, send_down, send_out, send_two, leaving, *prompt_parts
+    grad_q, send_down, send_out, send_two, leaving, *prompt_parts = together(
+        grad_q, send_down, send_out, send_two, leaving, *prompt_parts
     )
     left = regrouped(leaving.reshape(-1, width))
     sum_two = added(keep_two, send_two)

time: 693 us -> 700 us (1.010)
  transfers between devices with their start and end apart: 80 -> 80, of which waited for: 31 -> 32; matrix products, arithmetic and copies ran while one was open for 18% -> 18% of each run, Pallas kernels for 17% -> 17%
where the time goes in v5:
time: 700 us; the launch traced here: 694 us
  waiting for transfers between devices  272 us (39%)
  Pallas kernels  163 us (23%)
  starting transfers between devices  112 us (16%)
  other arithmetic  62.6 us (9%)
  matrix products  45.4 us (6%)
  local copies, waits for them, and re-layouts  36.7 us (5%)
    ppermute x77, waiting for transfers between devices, permute(): return lax.ppermute(a, AXES, pairs)  272 us
    ppermute x77, starting transfers between devices, permute(): return lax.ppermute(a, AXES, pairs)  99 us
    pallas_call x1, Pallas kernels, attn_bwd(): pl.pallas_call(attn_bwd_kernel, grid_spec=pltpu.PrefetchScalarGridSpec(nu...  45.6 us
    pallas_call x1, Pallas kernels, mlp(): pl.pallas_call(mlp_kernel, grid_spec=pltpu.PrefetchScalarGridSpec(num_sca...  39.1 us
    pallas_call x11, Pallas kernels, whole_call(): pl.pallas_call(kernel, in_specs=[smem if a.dtype == jnp.int32 else vmem f...  36.9 us
    dot_general x5, matrix products, tn(): lax.dot_general(a, b, (((0,), (0,)), ((), ())), preferred_element_type=f32)  33.7 us
    pallas_call x2, Pallas kernels, project(): pl.pallas_call(kernel, grid_spec=pltpu.PrefetchScalarGridSpec(num_scalar_...  21.1 us
    pallas_call x1, Pallas kernels, attn_fwd(): pl.pallas_call(attn_fwd_kernel, grid_spec=pltpu.PrefetchScalarGridSpec(nu...  19.9 us
  transfers between devices with their start and end apart: 80, of which 32 were waited for; matrix products, arithmetic and copies ran while one was open for 18% of the time, Pallas kernels for 17%

profile of v5, /device:TPU:0, one launch (start us, length us, event | category | flops | bytes accessed | tf_op | source)
XLA Modules:
  0.0 693.7 jit_solution(12770101586301533182)
XLA Ops:
  44.2 18.1 %collective-permute-done.10.refs_2_ = bf16[128,2048]{1,0:T(8,128)(2,1)S(1)} collective-permute-done((bf16[128,2048]{1,0:T(8,128)(2,1)S(1)}, bf16[128,2048]{1,0:T(8,128)(2,1)S(1)}, u32[]{:S(2)}, u32[]{:S(2)}) %collective-permute-start.10) | collective-permute-done | bytes 524320 | tf_op jit(solution)/shard_map/ppermute | solution.py:1016
  62.3 10.2 %collective-permute-done.11.refs_3_ = bf16[128,2048]{1,0:T(8,128)(2,1)S(1)} collective-permute-done((bf16[128,2048]{1,0:T(8,128)(2,1)S(1)}, bf16[128,2048]{1,0:T(8,128)(2,1)S(1)}, u32[]{:S(2)}, u32[]{:S(2)}) %collective-permute-start.11) | collective-permute-done | bytes 524320 | tf_op jit(solution)/shard_map/ppermute | solution.py:1016
  86.7 9.5 %collective-permute-done.15.refs_6_ = bf16[128,2048]{1,0:T(8,128)(2,1)} collective-permute-done((bf16[128,2048]{1,0:T(8,128)(2,1)}, bf16[128,2048]{1,0:T(8,128)(2,1)}, u32[]{:S(2)}, u32[]{:S(2)}) %collective-permute-start.15) | collective-permute-done | bytes 524320 | tf_op jit(solution)/shard_map/ppermute | solution.py:1016
  96.2 8.5 %collective-permute-done.16.refs_7_ = bf16[128,2048]{1,0:T(8,128)(2,1)} collective-permute-done((bf16[128,2048]{1,0:T(8,128)(2,1)}, bf16[128,2048]{1,0:T(8,128)(2,1)}, u32[]{:S(2)}, u32[]{:S(2)}) %collective-permute-start.16) | collective-permute-done | bytes 524320 | tf_op jit(solution)/shard_map/ppermute | solution.py:1016
  105.3 5.7 collective-permute-start.18
  116.9 9.7 %key_value.1 = (bf16[1152,1024]{1,0:T(8,128)(2,1)}, f32[1152,512]{1,0:T(8,128)}, bf16[1024,1024]{1,0:T(8,128)(2,1)}, bf16[256,1024]{1,0:T(8,128)(2,1)}) custom-call(s32[5]{0:T(128)} %stack.129.info, bf16[1152,1024]{1,0:T(8,128)(2,1)} %pad_maximum_fusion.h_ref, bf16[128,2048]{1,0:T(8,128)(2,1)} %copy-done.15, bf16[128,2048]{1,0:T(8,128)(2,1)} %copy-done.22, ...), custom_call_target="tpu_custom_call" | custom-call | tf_op jit(solution)/shard_map/key_value/pallas_call | solution.py:625
  129.4 7.1 %collective-permute-done.20.refs_2_ = bf16[64,3072]{1,0:T(8,128)(2,1)S(1)} collective-permute-done((bf16[64,3072]{1,0:T(8,128)(2,1)S(1)}, bf16[64,3072]{1,0:T(8,128)(2,1)S(1)}, u32[]{:S(2)}, u32[]{:S(2)}) %collective-permute-start.20) | collective-permute-done | bytes 393248 | tf_op jit(solution)/shard_map/ppermute | solution.py:1016
  136.6 5.7 collective-permute-done.21.refs_3_
  148.5 11.4 %query.1 = (bf16[1152,1024]{1,0:T(8,128)(2,1)}, f32[1152,1024]{1,0:T(8,128)}, bf16[1024,1024]{1,0:T(8,128)(2,1)}) custom-call(s32[5]{0:T(128)} %stack.129.info, bf16[1152,1024]{1,0:T(8,128)(2,1)} %pad_maximum_fusion.h_ref, bf16[128,2048]{1,0:T(8,128)(2,1)} %copy-done.15, bf16[128,2048]{1,0:T(8,128)(2,1)} %copy-done.22, bf16[128,2048]{1,0:T(8,128)(2,1)} %copy-done.20, ...), custom_call_target="tpu_custom_call" | custom-call | tf_op jit(solution)/shard_map/query/pallas_call | solution.py:625
  164.3 23.8 %collective-permute-done.24.p1 = bf16[256,1024]{1,0:T(8,128)(2,1)} collective-permute-done((bf16[256,1024]{1,0:T(8,128)(2,1)}, bf16[256,1024]{1,0:T(8,128)(2,1)}, u32[]{:S(2)}, u32[]{:S(2)}) %collective-permute-start.24) | collective-permute-done | bytes 524320 | tf_op jit(solution)/shard_map/ppermute | solution.py:1016
  191.7 9.0 %collective-permute-start.27 = (bf16[384,1024]{1,0:T(8,128)(2,1)}, bf16[384,1024]{1,0:T(8,128)(2,1)S(1)}, u32[]{:S(2)}, u32[]{:S(2)}) collective-permute-start(bf16[384,1024]{1,0:T(8,128)(2,1)} %param.26), channel_id=1, source_target_pairs={{0,4},{1,5},{2,6},{3,7},{12,8},{13,9},{14,10},{15,11},{16,20},{17,... | collective-permute-start | bytes 2359304 | tf_op jit(solution)/shard_map/ppermute | solution.py:1016
  200.7 19.9 %attn_fwd.1 = (bf16[1152,1024]{1,0:T(8,128)(2,1)}, f32[4,8,1280]{2,1,0:T(8,128)}) custom-call(s32[5]{0:T(128)} %stack.129.info, bf16[1152,1024]{1,0:T(8,128)(2,1)} %get-tuple-element.202.q_ref, bf16[1152,1024]{1,0:T(8,128)(2,1)} %get-tuple-element.203.kv_ref, bf16[256,1024]{1,0:T(8,128)(2,1)} %get-tuple-element.204.p0, ...), custom_call_target="tpu_custom_call" | custom-call | flops 20000000000 | bytes 10000000 | tf_op jit(solution)/shard_map/attn_fwd/pallas_call | solution.py:717
  228.8 6.7 out_projection.1
  248.4 15.8 %collective-permute-done.34.refs_11_ = bf16[384,1024]{1,0:T(8,128)(2,1)S(1)} collective-permute-done((bf16[384,1024]{1,0:T(8,128)(2,1)}, bf16[384,1024]{1,0:T(8,128)(2,1)S(1)}, u32[]{:S(2)}, u32[]{:S(2)}) %collective-permute-start.34) | collective-permute-done | bytes 786464 | tf_op jit(solution)/shard_map/ppermute | solution.py:1016
  264.1 16.5 %collective-permute-done.36.refs_13_ = bf16[384,1024]{1,0:T(8,128)(2,1)S(1)} collective-permute-done((bf16[384,1024]{1,0:T(8,128)(2,1)}, bf16[384,1024]{1,0:T(8,128)(2,1)S(1)}, u32[]{:S(2)}, u32[]{:S(2)}) %collective-permute-start.36) | collective-permute-done | bytes 786464 | tf_op jit(solution)/shard_map/ppermute | solution.py:1016
  287.3 39.1 %feed_forward.1 = (bf16[1152,1536]{1,0:T(8,128)(2,1)}, bf16[1152,3072]{1,0:T(8,128)(2,1)}, f32[576,1024]{1,0:T(8,128)}, bf16[576,1024]{1,0:T(8,128)(2,1)}, f32[5...) custom-call(s32[5]{0:T(128)} %stack.129.info, bf16[576,1024]{1,0:T(8,128)(2,1)} %copy-done.27, ...), custom_call_target="tpu_custom_call" | custom-call | flops 38000001024 | bytes 10000000 | tf_op jit(solution)/shard_map/feed_forward/pallas_call | solution.py:898
  327.0 12.3 %convolution_convert_fusion = bf16[1024,3072]{1,0:T(8,128)(2,1)S(1)} fusion(bf16[1152,3072]{1,0:T(8,128)(2,1)} %get-tuple-element.244, bf16[576,1024]{1,0:T(8,128)(2,1)} %collective-permute-done.37.h_sib, bf16[576,1024]{1,0:T(8,128)(2,1)} %copy-done.27), kind=kOutput, calls=%fused_computation.1 | convolution fusion | flops 7255621632 | bytes 15728640 | tf_op jit(solution)/shard_map/dot_general | solution.py:466
  348.6 7.0 %convolution_convert_fusion.2 = bf16[1536,1024]{1,0:T(8,128)(2,1)} fusion(bf16[1152,1536]{1,0:T(8,128)(2,1)S(1)} %copy-done.56, bf16[576,1024]{1,0:T(8,128)(2,1)} %collective-permute-done.38.g_sib, bf16[576,1024]{1,0:T(8,128)(2,1)S(1)} %copy-done.10), kind=kOutput, calls=%fused_computation.4 | convolution fusion | flops 3630170112 | bytes 9043968 | tf_op jit(solution)/shard_map/dot_general | solution.py:466
  375.3 6.4 convolution_convert_fusion.1.refs_0_
  381.7 45.6 %attn_bwd.1 = (bf16[1152,1024]{1,0:T(8,128)(2,1)}, bf16[1152,1024]{1,0:T(8,128)(2,1)}, bf16[256,1024]{1,0:T(8,128)(2,1)}, bf16[256,1024]{1,0:T(8,128)(2,1)}, bf1...) custom-call(s32[5]{0:T(128)} %stack.129.info, bf16[1152,1024]{1,0:T(8,128)(2,1)} %get-tuple-element.202.q_ref, ...), custom_call_target="tpu_custom_call" | custom-call | flops 44999999488 | bytes 10000000 | tf_op jit(solution)/shard_map/attn_bwd/pallas_call | solution.py:801
  430.9 11.1 %collective-permute-done.45.d1 = bf16[256,1024]{1,0:T(8,128)(2,1)} collective-permute-done((bf16[256,1024]{1,0:T(8,128)(2,1)}, bf16[256,1024]{1,0:T(8,128)(2,1)}, u32[]{:S(2)}, u32[]{:S(2)}) %collective-permute-start.45) | collective-permute-done | bytes 524320 | tf_op jit(solution)/shard_map/ppermute | solution.py:1016
  444.4 9.9 %collective-permute-done.47.d3 = bf16[256,1024]{1,0:T(8,128)(2,1)} collective-permute-done((bf16[256,1024]{1,0:T(8,128)(2,1)}, bf16[256,1024]{1,0:T(8,128)(2,1)}, u32[]{:S(2)}, u32[]{:S(2)}) %collective-permute-start.47) | collective-permute-done | bytes 524320 | tf_op jit(solution)/shard_map/ppermute | solution.py:1016
  472.0 5.9 prompt_back.1
  477.9 5.9 convolution_convert_fusion.4
  492.4 15.5 %collective-permute-done.48 = bf16[2,2,64,3072]{3,2,0,1:T(8,128)(2,1)S(1)} collective-permute-done((bf16[2,2,64,3072]{3,2,0,1:T(8,128)(2,1)}, bf16[2,2,64,3072]{3,2,0,1:T(8,128)(2,1)S(1)}, u32[]{:S(2)}, u32[]{:S(2)}) %collective-permute-start.48) | collective-permute-done | bytes 1572896 | tf_op jit(solution)/shard_map/ppermute | solution.py:1016
  524.4 11.8 %collective-permute-done.52 = bf16[8,64,1024]{2,1,0:T(8,128)(2,1)} collective-permute-done((bf16[8,64,1024]{2,1,0:T(8,128)(2,1)}, bf16[8,64,1024]{2,1,0:T(8,128)(2,1)}, u32[]{:S(2)}, u32[]{:S(2)}) %collective-permute-start.52) | collective-permute-done | bytes 1048608 | tf_op jit(solution)/shard_map/ppermute | solution.py:1016
  560.0 17.8 %collective-permute-done.62 = bf16[640,1024]{1,0:T(8,128)(2,1)} collective-permute-done((bf16[640,1024]{1,0:T(8,128)(2,1)}, bf16[640,1024]{1,0:T(8,128)(2,1)}, u32[]{:S(2)}, u32[]{:S(2)}) %collective-permute-start.62) | collective-permute-done | bytes 1310752 | tf_op jit(solution)/shard_map/ppermute | solution.py:1016
  594.3 24.2 %collective-permute-done.61 = bf16[2,64,3072]{2,1,0:T(8,128)(2,1)S(1)} collective-permute-done((bf16[2,64,3072]{2,1,0:T(8,128)(2,1)S(1)}, bf16[2,64,3072]{2,1,0:T(8,128)(2,1)S(1)}, u32[]{:S(2)}, u32[]{:S(2)}) %collective-permute-start.61) | collective-permute-done | bytes 786464 | tf_op jit(solution)/shard_map/ppermute | solution.py:1016
  634.8 17.8 %collective-permute-done.66 = bf16[64,2048]{1,0:T(8,128)(2,1)S(1)} collective-permute-done((bf16[64,2048]{1,0:T(8,128)(2,1)S(1)}, bf16[64,2048]{1,0:T(8,128)(2,1)S(1)}, u32[]{:S(2)}, u32[]{:S(2)}) %collective-permute-start.66) | collective-permute-done | bytes 262176 | tf_op jit(solution)/shard_map/ppermute | solution.py:1016
  652.7 8.3 %collective-permute-done.67 = bf16[64,3072]{1,0:T(8,128)(2,1)S(1)} collective-permute-done((bf16[64,3072]{1,0:T(8,128)(2,1)S(1)}, bf16[64,3072]{1,0:T(8,128)(2,1)S(1)}, u32[]{:S(2)}, u32[]{:S(2)}) %collective-permute-start.67) | collective-permute-done | bytes 393248 | tf_op jit(solution)/shard_map/ppermute | solution.py:1016
  664.8 6.2 collective-permute-done.72
  672.1 6.4 collective-permute-done.71
  (393 shorter events, 262.6 us)
Async XLA Ops:
  29.4 32.9 %collective-permute-start.10 = (bf16[128,2048]{1,0:T(8,128)(2,1)S(1)}, bf16[128,2048]{1,0:T(8,128)(2,1)S(1)}, u32[]{:S(2)}, u32[]{:S(2)}) collective-permute-start(bf16[128,2048]{1,0:T(8,128)(2,1)S(1)} %constant_dynamic-update-slice_fusion.refs_0_), channel_id=1, source_target_pairs={{0,2},{1,3},{2,0},{3,1},{4,6},{5,7},{6,4},{7,5},{8,10},{9,11},{10,... | collective-permute-start | bytes 1572872 | tf_op jit(solution)/shard_map/ppermute | solution.py:1016
  32.1 40.4 %collective-permute-start.11 = (bf16[128,2048]{1,0:T(8,128)(2,1)S(1)}, bf16[128,2048]{1,0:T(8,128)(2,1)S(1)}, u32[]{:S(2)}, u32[]{:S(2)}) collective-permute-start(bf16[128,2048]{1,0:T(8,128)(2,1)S(1)} %constant_dynamic-update-slice_fusion.refs_0_), channel_id=1, source_target_pairs={{0,3},{1,2},{2,1},{3,0},{4,7},{5,6},{6,5},{7,4},{8,11},{9,10},{10,... | collective-permute-start | bytes 1572872 | tf_op jit(solution)/shard_map/ppermute | solution.py:1016
  35.1 37.4 %collective-permute-start.9 = (bf16[128,2048]{1,0:T(8,128)(2,1)S(1)}, bf16[128,2048]{1,0:T(8,128)(2,1)S(1)}, u32[]{:S(2)}, u32[]{:S(2)}) collective-permute-start(bf16[128,2048]{1,0:T(8,128)(2,1)S(1)} %constant_dynamic-update-slice_fusion.refs_0_), channel_id=1, source_target_pairs={{0,1},{1,0},{2,3},{3,2},{4,5},{5,4},{6,7},{7,6},{8,9},{9,8},{10,11... | collective-permute-start | bytes 1572872 | tf_op jit(solution)/shard_map/ppermute | solution.py:1016
  37.6 37.1 %collective-permute-start.13 = (bf16[128,2048]{1,0:T(8,128)(2,1)S(1)}, bf16[128,2048]{1,0:T(8,128)(2,1)}, u32[]{:S(2)}, u32[]{:S(2)}) collective-permute-start(bf16[128,2048]{1,0:T(8,128)(2,1)S(1)} %constant_dynamic-update-slice_fusion.refs_0_), channel_id=1, source_target_pairs={{0,4},{1,5},{2,6},{3,7},{4,0},{5,1},{6,2},{7,3},{8,12},{9,13},{10,... | collective-permute-start | bytes 1572872 | tf_op jit(solution)/shard_map/ppermute | solution.py:1016
  42.4 39.8 %collective-permute-start.8 = (bf16[576,1024]{1,0:T(8,128)(2,1)}, bf16[576,1024]{1,0:T(8,128)(2,1)}, u32[]{:S(2)}, u32[]{:S(2)}) collective-permute-start(bf16[576,1024]{1,0:T(8,128)(2,1)} %get-tuple-element.176), channel_id=1, source_target_pairs={{0,8},{1,9},{2,10},{3,11},{4,12},{5,13},{6,14},{7,15},{8,0},{9,1},... | collective-permute-start | bytes 3538952 | tf_op jit(solution)/shard_map/ppermute | solution.py:1016
  143.9 44.2 %collective-permute-start.23 = (bf16[2,256,1024]{2,1,0:T(8,128)(2,1)S(1)}, bf16[2,256,1024]{2,1,0:T(8,128)(2,1)}, u32[]{:S(2)}, u32[]{:S(2)}) collective-permute-start(bf16[2,256,1024]{2,1,0:T(8,128)(2,1)S(1)} %pad_maximum_fusion.5.refs_0_), channel_id=1, source_target_pairs={{0,1},{1,0},{2,3},{3,2},{4,5},{5,4},{6,7},{7,6},{8,9},{9,8},{10,11... | collective-permute-start | bytes 3145736 | tf_op jit(solution)/shard_map/ppermute | solution.py:1016
  145.1 43.1 %collective-permute-start.24 = (bf16[256,1024]{1,0:T(8,128)(2,1)}, bf16[256,1024]{1,0:T(8,128)(2,1)}, u32[]{:S(2)}, u32[]{:S(2)}) collective-permute-start(bf16[256,1024]{1,0:T(8,128)(2,1)} %get-tuple-element.204.p0), channel_id=1, source_target_pairs={{0,1},{1,0},{2,3},{3,2},{4,5},{5,4},{6,7},{7,6},{8,9},{9,8},{10,11... | collective-permute-start | bytes 1572872 | tf_op jit(solution)/shard_map/ppermute | solution.py:1016
  145.9 42.2 %collective-permute-start.25 = (bf16[256,1024]{1,0:T(8,128)(2,1)}, bf16[256,1024]{1,0:T(8,128)(2,1)}, u32[]{:S(2)}, u32[]{:S(2)}) collective-permute-start(bf16[256,1024]{1,0:T(8,128)(2,1)} %get-tuple-element.204.p0), channel_id=1, source_target_pairs={{0,2},{1,3},{2,0},{3,1},{4,6},{5,7},{6,4},{7,5},{8,10},{9,11},{10,... | collective-permute-start | bytes 1572872 | tf_op jit(solution)/shard_map/ppermute | solution.py:1016
  146.3 41.8 %collective-permute-start.26 = (bf16[256,1024]{1,0:T(8,128)(2,1)}, bf16[256,1024]{1,0:T(8,128)(2,1)}, u32[]{:S(2)}, u32[]{:S(2)}) collective-permute-start(bf16[256,1024]{1,0:T(8,128)(2,1)} %get-tuple-element.204.p0), channel_id=1, source_target_pairs={{0,3},{1,2},{2,1},{3,0},{4,7},{5,6},{6,5},{7,4},{8,11},{9,10},{10,... | collective-permute-start | bytes 1572872 | tf_op jit(solution)/shard_map/ppermute | solution.py:1016
  161.3 61.3 %collective-permute-start.31 = (bf16[4,64,3072]{2,1,0:T(8,128)(2,1)S(1)}, bf16[4,64,3072]{2,1,0:T(8,128)(2,1)}, u32[]{:S(2)}, u32[]{:S(2)}) collective-permute-start(bf16[4,64,3072]{2,1,0:T(8,128)(2,1)S(1)} %pad_maximum_fusion.2), channel_id=1, source_target_pairs={{0,16},{1,17},{2,18},{3,19},{4,20},{5,21},{6,22},{7,23},{8,24},{9,... | collective-permute-start | bytes 4718600 | tf_op jit(solution)/shard_map/ppermute | solution.py:1016
  188.1 34.5 %collective-permute-start.28 = (bf16[64,3072]{1,0:T(8,128)(2,1)}, bf16[64,3072]{1,0:T(8,128)(2,1)}, u32[]{:S(2)}, u32[]{:S(2)}) collective-permute-start(bf16[64,3072]{1,0:T(8,128)(2,1)} %collective-permute-done.18.refs_4_), channel_id=1, source_target_pairs={{0,1},{1,0},{2,3},{3,2},{4,5},{5,4},{6,7},{7,6},{8,9},{9,8},{10,11... | collective-permute-start | bytes 1179656 | tf_op jit(solution)/shard_map/ppermute | solution.py:1016
  188.8 33.9 %collective-permute-start.29 = (bf16[64,3072]{1,0:T(8,128)(2,1)}, bf16[64,3072]{1,0:T(8,128)(2,1)}, u32[]{:S(2)}, u32[]{:S(2)}) collective-permute-start(bf16[64,3072]{1,0:T(8,128)(2,1)} %collective-permute-done.18.refs_4_), channel_id=1, source_target_pairs={{0,2},{1,3},{2,0},{3,1},{4,6},{5,7},{6,4},{7,5},{8,10},{9,11},{10,... | collective-permute-start | bytes 1179656 | tf_op jit(solution)/shard_map/ppermute | solution.py:1016
  188.8 33.9 %collective-permute-start.30 = (bf16[64,3072]{1,0:T(8,128)(2,1)}, bf16[64,3072]{1,0:T(8,128)(2,1)}, u32[]{:S(2)}, u32[]{:S(2)}) collective-permute-start(bf16[64,3072]{1,0:T(8,128)(2,1)} %collective-permute-done.18.refs_4_), channel_id=1, source_target_pairs={{0,3},{1,2},{2,1},{3,0},{4,7},{5,6},{6,5},{7,4},{8,11},{9,10},{10,... | collective-permute-start | bytes 1179656 | tf_op jit(solution)/shard_map/ppermute | solution.py:1016
  224.1 57.4 %all-to-all-start = ((bf16[8,80,1024]{2,1,0:T(8,128)(2,1)}), bf16[8,80,1024]{2,1,0:T(8,128)(2,1)}, u32[]{:S(2)}, u32[]{:S(2)}) async-start(bf16[8,80,1024]{2,1,0:T(8,128)(2,1)} %pad_maximum_fusion.4), calls=%async_computation | async-start | bytes 2621440 | tf_op jit(solution)/shard_map/all_to_all | solution.py:1192
  238.7 41.9 %collective-permute-start.33 = (bf16[4,64,3072]{2,1,0:T(8,128)(2,1)}, bf16[4,64,3072]{2,1,0:T(8,128)(2,1)}, u32[]{:S(2)}, u32[]{:S(2)}) collective-permute-start(bf16[4,64,3072]{2,1,0:T(8,128)(2,1)} %pad_maximum_fusion.3), channel_id=1, source_target_pairs={{0,16},{1,17},{2,18},{3,19},{4,20},{5,21},{6,22},{7,23},{8,24},{9,... | collective-permute-start | bytes 4718600 | tf_op jit(solution)/shard_map/ppermute | solution.py:1016
  244.1 36.6 %collective-permute-start.36 = (bf16[384,1024]{1,0:T(8,128)(2,1)}, bf16[384,1024]{1,0:T(8,128)(2,1)S(1)}, u32[]{:S(2)}, u32[]{:S(2)}) collective-permute-start(bf16[384,1024]{1,0:T(8,128)(2,1)} %broadcast_select_fusion.3.refs_10_), channel_id=1, source_target_pairs={{0,3},{1,2},{2,1},{3,0},{4,7},{5,6},{6,5},{7,4},{8,11},{9,10},{10,... | collective-permute-start | bytes 2359304 | tf_op jit(solution)/shard_map/ppermute | solution.py:1016
  347.1 83.8 %collective-permute-start.44 = (bf16[2,2,2,64,3072]{4,3,0,1,2:T(8,128)(2,1)}, bf16[2,2,2,64,3072]{4,3,0,1,2:T(8,128)(2,1)}, u32[]{:S(2)}, u32[]{:S(2)}) collective-permute-start(bf16[2,2,2,64,3072]{4,3,0,1,2:T(8,128)(2,1)} %bitcast.154), channel_id=1, source_target_pairs={{0,16},{1,17},{2,18},{3,19},{4,20},{5,21},{6,22},{7,23},{8,24},{9,... | collective-permute-start | bytes 9437192 | tf_op jit(solution)/shard_map/ppermute | solution.py:1016
  368.7 58.6 %collective-permute-start.42 = (bf16[2,384,1024]{2,1,0:T(8,128)(2,1)}, bf16[2,384,1024]{2,1,0:T(8,128)(2,1)}, u32[]{:S(2)}, u32[]{:S(2)}) collective-permute-start(bf16[2,384,1024]{2,1,0:T(8,128)(2,1)} %dynamic-slice_bitcast_fusion.1), channel_id=1, source_target_pairs={{0,1},{1,0},{2,3},{3,2},{4,5},{5,4},{6,7},{7,6},{8,9},{9,8},{10,11... | collective-permute-start | bytes 4718600 | tf_op jit(solution)/shard_map/ppermute | solution.py:1016
  370.3 56.9 %collective-permute-start.43 = (bf16[2,256,1024]{2,1,0:T(8,128)(2,1)}, bf16[2,256,1024]{2,1,0:T(8,128)(2,1)}, u32[]{:S(2)}, u32[]{:S(2)}) collective-permute-start(bf16[2,256,1024]{2,1,0:T(8,128)(2,1)} %dynamic-slice_bitcast_fusion.6), channel_id=1, source_target_pairs={{0,2},{1,3},{2,0},{3,1},{4,6},{5,7},{6,4},{7,5},{8,10},{9,11},{10,... | collective-permute-start | bytes 3145736 | tf_op jit(solution)/shard_map/ppermute | solution.py:1016
  370.6 56.7 %all-to-all-start.1 = ((bf16[8,80,1024]{2,1,0:T(8,128)(2,1)}), bf16[8,80,1024]{2,1,0:T(8,128)(2,1)}, u32[]{:S(2)}, u32[]{:S(2)}) async-start(bf16[8,80,1024]{2,1,0:T(8,128)(2,1)} %deal_all.2), calls=%async_computation.1 | async-start | bytes 2621440 | tf_op jit(solution)/shard_map/all_to_all | solution.py:1192
  454.4 61.6 %collective-permute-start.53 = (bf16[640,1024]{1,0:T(8,128)(2,1)}, bf16[640,1024]{1,0:T(8,128)(2,1)}, u32[]{:S(2)}, u32[]{:S(2)}) collective-permute-start(bf16[640,1024]{1,0:T(8,128)(2,1)} %bitcast.56), channel_id=1, source_target_pairs={{4,8},{5,9},{6,10},{7,11},{8,4},{9,5},{10,6},{11,7},{20,24},{21,25... | collective-permute-start | bytes 3932168 | tf_op jit(solution)/shard_map/ppermute | solution.py:1016
  459.2 53.1 %collective-permute-start.51 = (bf16[256,1024]{1,0:T(8,128)(2,1)}, bf16[256,1024]{1,0:T(8,128)(2,1)}, u32[]{:S(2)}, u32[]{:S(2)}) collective-permute-start(bf16[256,1024]{1,0:T(8,128)(2,1)} %dynamic-slice_bitcast_fusion.9), channel_id=1, source_target_pairs={{0,1},{1,0},{2,3},{3,2},{4,5},{5,4},{6,7},{7,6},{8,9},{9,8},{10,11... | collective-permute-start | bytes 1572872 | tf_op jit(solution)/shard_map/ppermute | solution.py:1016
  464.0 49.6 %collective-permute-start.50 = (bf16[384,1024]{1,0:T(8,128)(2,1)}, bf16[384,1024]{1,0:T(8,128)(2,1)}, u32[]{:S(2)}, u32[]{:S(2)}) collective-permute-start(bf16[384,1024]{1,0:T(8,128)(2,1)} %dynamic-slice_bitcast_fusion.8), channel_id=1, source_target_pairs={{0,2},{1,3},{2,0},{3,1},{4,6},{5,7},{6,4},{7,5},{8,10},{9,11},{10,... | collective-permute-start | bytes 2359304 | tf_op jit(solution)/shard_map/ppermute | solution.py:1016
  471.5 36.4 %collective-permute-start.48 = (bf16[2,2,64,3072]{3,2,0,1:T(8,128)(2,1)}, bf16[2,2,64,3072]{3,2,0,1:T(8,128)(2,1)S(1)}, u32[]{:S(2)}, u32[]{:S(2)}) collective-permute-start(bf16[2,2,64,3072]{3,2,0,1:T(8,128)(2,1)} %dynamic-slice_bitcast_fusion), channel_id=1, source_target_pairs={{0,1},{1,0},{2,3},{3,2},{4,5},{5,4},{6,7},{7,6},{8,9},{9,8},{10,11... | collective-permute-start | bytes 4718600 | tf_op jit(solution)/shard_map/ppermute | solution.py:1016
  536.3 47.6 %all-to-all-start.2 = ((bf16[8,80,1024]{2,1,0:T(8,128)(2,1)}), bf16[8,80,1024]{2,1,0:T(8,128)(2,1)S(1)}, u32[]{:S(2)}, u32[]{:S(2)}) async-start(bf16[8,80,1024]{2,1,0:T(8,128)(2,1)} %deal_all.3), calls=%async_computation.2 | async-start | bytes 2621440 | tf_op jit(solution)/shard_map/all_to_all | solution.py:1192
  542.9 34.9 %collective-permute-start.62 = (bf16[640,1024]{1,0:T(8,128)(2,1)}, bf16[640,1024]{1,0:T(8,128)(2,1)}, u32[]{:S(2)}, u32[]{:S(2)}) collective-permute-start(bf16[640,1024]{1,0:T(8,128)(2,1)} %constant_dynamic-update-slice_fusion.2), channel_id=1, source_target_pairs={{4,0},{5,1},{6,2},{7,3},{8,12},{9,13},{10,14},{11,15},{20,16},{21,... | collective-permute-start | bytes 3932168 | tf_op jit(solution)/shard_map/ppermute | solution.py:1016
  548.3 35.6 %collective-permute-start.55 = (bf16[8,64,1024]{2,1,0:T(8,128)(2,1)}, bf16[8,64,1024]{2,1,0:T(8,128)(2,1)}, u32[]{:S(2)}, u32[]{:S(2)}) collective-permute-start(bf16[8,64,1024]{2,1,0:T(8,128)(2,1)} %get-tuple-element.334), channel_id=1, source_target_pairs={{0,16},{1,17},{2,18},{3,19},{4,20},{5,21},{6,22},{7,23},{8,24},{9,... | collective-permute-start | bytes 3145736 | tf_op jit(solution)/shard_map/ppermute | solution.py:1016
  584.0 34.6 %collective-permute-start.61 = (bf16[2,64,3072]{2,1,0:T(8,128)(2,1)S(1)}, bf16[2,64,3072]{2,1,0:T(8,128)(2,1)S(1)}, u32[]{:S(2)}, u32[]{:S(2)}) collective-permute-start(bf16[2,64,3072]{2,1,0:T(8,128)(2,1)S(1)} %dynamic-slice_bitcast_fusion.7), channel_id=1, source_target_pairs={{0,2},{1,3},{2,0},{3,1},{4,6},{5,7},{6,4},{7,5},{8,10},{9,11},{10,... | collective-permute-start | bytes 2359304 | tf_op jit(solution)/shard_map/ppermute | solution.py:1016
  584.0 34.7 %collective-permute-start.59 = (bf16[640,1024]{1,0:T(8,128)(2,1)S(1)}, bf16[640,1024]{1,0:T(8,128)(2,1)S(1)}, u32[]{:S(2)}, u32[]{:S(2)}) collective-permute-start(bf16[640,1024]{1,0:T(8,128)(2,1)S(1)} %bitcast.156), channel_id=1, source_target_pairs={{4,8},{5,9},{6,10},{7,11},{8,4},{9,5},{10,6},{11,7},{20,24},{21,25... | collective-permute-start | bytes 3932168 | tf_op jit(solution)/shard_map/ppermute | solution.py:1016
  586.9 38.1 %collective-permute-start.65 = (bf16[2,64,1024]{2,1,0:T(8,128)(2,1)S(1)}, bf16[2,64,1024]{2,1,0:T(8,128)(2,1)S(1)}, u32[]{:S(2)}, u32[]{:S(2)}) collective-permute-start(bf16[2,64,1024]{2,1,0:T(8,128)(2,1)S(1)} %pad_maximum_fusion.18), channel_id=1, source_target_pairs={{0,3},{1,2},{2,1},{3,0},{4,7},{5,6},{6,5},{7,4},{8,11},{9,10},{10,... | collective-permute-start | bytes 786440 | tf_op jit(solution)/shard_map/ppermute | solution.py:1016
  589.9 38.5 %collective-permute-start.64 = (bf16[2,64,1024]{2,1,0:T(8,128)(2,1)S(1)}, bf16[2,64,1024]{2,1,0:T(8,128)(2,1)S(1)}, u32[]{:S(2)}, u32[]{:S(2)}) collective-permute-start(bf16[2,64,1024]{2,1,0:T(8,128)(2,1)S(1)} %pad_maximum_fusion.17), channel_id=1, source_target_pairs={{0,2},{1,3},{2,0},{3,1},{4,6},{5,7},{6,4},{7,5},{8,10},{9,11},{10,... | collective-permute-start | bytes 786440 | tf_op jit(solution)/shard_map/ppermute | solution.py:1016
  593.7 34.7 %collective-permute-start.63 = (bf16[2,64,1024]{2,1,0:T(8,128)(2,1)S(1)}, bf16[2,64,1024]{2,1,0:T(8,128)(2,1)S(1)}, u32[]{:S(2)}, u32[]{:S(2)}) collective-permute-start(bf16[2,64,1024]{2,1,0:T(8,128)(2,1)S(1)} %pad_maximum_fusion.16), channel_id=1, source_target_pairs={{0,1},{1,0},{2,3},{3,2},{4,5},{5,4},{6,7},{7,6},{8,9},{9,8},{10,11... | collective-permute-start | bytes 786440 | tf_op jit(solution)/shard_map/ppermute | solution.py:1016
  (105 other events, 1426.9 us)
